TPU v7x, 32 devices: a whole 2x2x4 slice. The times are simulated.
32 devices in a mesh: gz: 4 (over x, core), subj: 8 (over z, y).
Axes of the slice: x: 2, y: 2, z: 4, core: 2. Of those that a mesh axis runs over, the one named last changes fastest.
Arguments:
- template: bfloat16 [256, 8, 128], P(('gz', 'subj')), may hold values from -6 to 6
- subjects: bfloat16 [8, 256, 8, 128], P('subj', 'gz'), may hold values from -6 to 6
- shifts: int32 [8, 3, 256, 8, 128], P('subj', None, 'gz'), may hold values from -2 to 2
- fractions: bfloat16 [8, 3, 256, 8, 128], P('subj', None, 'gz'), may hold values from 0 to 1
Outputs:
- velocity_step: float32 [8, 3, 256, 8, 128], P('subj', None, 'gz')
- template_force: float32 [256, 8, 128], P(('gz', 'subj'))
All inputs are finite; a program needn't handle non-finite values.
Results may differ from a plain program's by a relative error of at most 0.0029.
Values may be sent and summed in bfloat16 or wider, within the bound.
No kernel may reach another device: no remote copies, remote signals or barrier semaphores. Data moves between devices by JAX's collectives and lax.ppermute only.
A program may use at most 64 MiB of HBM per device.

v0:
```python
import math

import jax
import jax.numpy as jnp
from jax import lax
from jax.sharding import PartitionSpec as P

SHIFT = 2
WIN = 4
SMOOTH = 4


sigma = 1.5
epsilon = 1e-05
highest = lax.Precision.HIGHEST


def with_halo(block, sides, width):
    for axis, dim in sides:
        count = lax.axis_size(axis)
        forward = [(i, i + 1) for i in range(count - 1)]
        backward = [(target, source) for source, target in forward]
        low = lax.ppermute(
            lax.slice_in_dim(block, block.shape[dim] - width, None, axis=dim), axis, forward
        )
        high = lax.ppermute(lax.slice_in_dim(block, 0, width, axis=dim), axis, backward)
        block = jnp.concatenate([low, block, high], axis=dim)
    return block


def gauss_norm():
    offsets = jnp.arange(-SMOOTH, SMOOTH + 1, dtype=jnp.int32).astype(jnp.float32)
    return jnp.sum(jnp.exp(-0.5 * offsets * offsets / (sigma * sigma)))


def gauss_taps():
    offsets = jnp.arange(-SMOOTH, SMOOTH + 1, dtype=jnp.int32).astype(jnp.float32)
    return jnp.exp(-0.5 * offsets * offsets / (sigma * sigma)) / gauss_norm()


def band_matrix(length, radius):
    places = jnp.arange(length, dtype=jnp.int32)
    apart = places[:, None] - places[None, :]
    return (jnp.abs(apart) <= radius).astype(jnp.float32)


def gauss_matrix(length):
    places = jnp.arange(length, dtype=jnp.int32)
    apart = places[:, None] - places[None, :]
    offsets = apart.astype(jnp.float32)
    values = jnp.exp(-0.5 * offsets * offsets / (sigma * sigma)) / gauss_norm()
    return jnp.where(jnp.abs(apart) <= SMOOTH, values, jnp.zeros_like(values))


def inplane(fields, row_matrix, col_matrix):
    mixed = jnp.einsum("...xy,yv->...xv", fields, col_matrix, precision=highest)
    return jnp.einsum("...xy,xu->...uy", mixed, row_matrix, precision=highest)


def zwindow(fields, length, taps):
    summed = taps[0] * fields[..., 0:length, :, :]
    for offset in range(1, taps.shape[0]):
        summed = summed + taps[offset] * fields[..., offset : offset + length, :, :]
    return summed


def offset_weights(shift_axis, frac_axis):
    result = []
    for offset in range(-SHIFT, SHIFT + 2):
        lower = jnp.where(shift_axis == offset, 1.0 - frac_axis, 0.0)
        upper = jnp.where(shift_axis == offset - 1, frac_axis, 0.0)
        result.append(lower + upper)
    return result


def warp(padded_template, front, shift_one, frac_one):
    depth_len, row_len, col_len = frac_one.shape[1:]
    weights = frac_one.astype(jnp.float32)
    depth_w = offset_weights(shift_one[0], weights[0])
    row_w = offset_weights(shift_one[1], weights[1])
    col_w = offset_weights(shift_one[2], weights[2])
    summed = jnp.zeros(frac_one.shape[1:], jnp.float32)
    for kz in range(2 * SHIFT + 2):
        depth_start = front + kz - SHIFT
        plane_sum = jnp.zeros(frac_one.shape[1:], jnp.float32)
        for kr in range(2 * SHIFT + 2):
            line_sum = jnp.zeros(frac_one.shape[1:], jnp.float32)
            for kc in range(2 * SHIFT + 2):
                piece = padded_template[
                    depth_start : depth_start + depth_len, kr : kr + row_len, kc : kc + col_len
                ]
                line_sum = line_sum + col_w[kc] * piece
            plane_sum = plane_sum + row_w[kr] * line_sum
        summed = summed + depth_w[kz] * plane_sum
    return lax.optimization_barrier(summed.astype(jnp.bfloat16))


def correlation_force(warped_ext, subject_ext, length):
    row_count = warped_ext.shape[-2]
    col_count = warped_ext.shape[-1]
    stacked = jnp.stack(
        [
            warped_ext,
            subject_ext,
            warped_ext * warped_ext,
            subject_ext * subject_ext,
            warped_ext * subject_ext,
        ]
    )
    box_sums = inplane(stacked, band_matrix(row_count, WIN), band_matrix(col_count, WIN))
    window = float((2 * WIN + 1) ** 3)
    local_means = zwindow(box_sums, length, jnp.ones((2 * WIN + 1,), jnp.float32)) / window
    centre_warped = warped_ext[..., WIN : WIN + length, :, :]
    centre_subject = subject_ext[..., WIN : WIN + length, :, :]
    var_warped = local_means[2] - local_means[0] * local_means[0]
    var_subject = local_means[3] - local_means[1] * local_means[1]
    covariance = local_means[4] - local_means[0] * local_means[1]
    factor = (
        centre_subject
        - local_means[1]
        - covariance / (var_warped + epsilon) * (centre_warped - local_means[0])
    ) / jnp.sqrt(var_warped * var_subject + epsilon)
    grad_depth = 0.5 * (
        warped_ext[..., WIN + 1 : WIN + 1 + length, :, :]
        - warped_ext[..., WIN - 1 : WIN - 1 + length, :, :]
    )
    padded = jnp.pad(centre_warped, [(0, 0)] * (centre_warped.ndim - 2) + [(1, 1), (1, 1)])
    grad_rows = 0.5 * (padded[..., 2:, 1:-1] - padded[..., :-2, 1:-1])
    grad_cols = 0.5 * (padded[..., 1:-1, 2:] - padded[..., 1:-1, :-2])
    return jnp.stack([factor * grad_depth, factor * grad_rows, factor * grad_cols], axis=-4)


def smooth(force_ext, length):
    along = zwindow(force_ext, length, gauss_taps())
    return inplane(along, gauss_matrix(force_ext.shape[-2]), gauss_matrix(force_ext.shape[-1]))


def per_device(template, subjects, shifts, fractions):
    slab_whole = lax.all_gather(template, "subj", axis=0, tiled=True)
    slab_depth = slab_whole.shape[0]
    groups = lax.axis_size("gz")
    members = lax.axis_size("subj")
    extended = with_halo(slab_whole, (("gz", 0),), SHIFT + 1)
    padded_template = jnp.pad(
        extended.astype(jnp.float32), ((0, 0), (SHIFT, SHIFT + 1), (SHIFT, SHIFT + 1))
    )
    subject_count = subjects.shape[0]
    warped = jnp.stack([warp(padded_template, SHIFT + 1, shifts[0], fractions[0])])
    residual = jnp.sum(subjects.astype(jnp.float32) - warped.astype(jnp.float32), axis=0)
    paired = jnp.stack([warped, subjects])
    rimmed = with_halo(paired, (("gz", 2),), WIN + SMOOTH).astype(jnp.float32)
    force = correlation_force(rimmed[0], rimmed[1], slab_depth + 2 * SMOOTH)
    positions = (
        lax.axis_index("gz") * slab_depth
        - SMOOTH
        + jnp.arange(slab_depth + 2 * SMOOTH, dtype=jnp.int32)
    )
    inside = ((positions >= 0) & (positions < slab_depth * groups)).astype(jnp.float32)
    force_ext = force * inside[:, None, None]
    velocity_step = smooth(force_ext, slab_depth)
    summed = lax.psum(residual, "subj")
    share_rows = slab_depth // members
    own_rows = lax.dynamic_slice_in_dim(summed, lax.axis_index("subj") * share_rows, share_rows, 0)
    template_force = own_rows * (1.0 / math.sqrt(subject_count * members))
    return (velocity_step, template_force)


def solution(mesh):
    placed = (
        P(("gz", "subj"), None, None),
        P("subj", "gz", None, None),
        P("subj", None, "gz", None, None),
        P("subj", None, "gz", None, None),
    )
    return jax.shard_map(
        per_device,
        mesh=mesh,
        in_specs=placed,
        out_specs=(P("subj", None, "gz", None, None), P(("gz", "subj"), None, None)),
        check_vma=False,
    )
```

profile of v0, /device:TPU:0, one launch (start us, length us, event | category | flops | bytes accessed | tf_op | source)
XLA Modules:
  0.0 149.7 jit_solution(2798989663458457799)
XLA Ops:
  7.2 32.7 %all_gather.3 = bf16[64,8,128]{2,1,0:T(8,128)(2,1)S(1)} all-gather(bf16[8,8,128]{2,1,0:T(8,128)(2,1)} %param.4), channel_id=1, replica_groups=mesh['gz'=4,'subj'=8] {'subj'}, dimensions={0}, use_global_device_ids=true | all-gather | bytes 147456 | tf_op jit(solution)/shard_map/all_gather | solution.py:139
  39.9 1.3 collective-permute-start
  41.2 1.3 collective-permute-start.1
  42.5 0.6 fusion.556
  43.1 1.1 slice_compare_fusion.4
  44.1 0.7 broadcast_divide_fusion
  44.8 0.7 fusion.570
  45.5 1.0 convert_element_type.59
  46.9 0.5 fusion.470
  47.4 0.4 slice_multiply_fusion.14
  48.3 0.5 fusion.505
  48.8 0.5 fusion.517
  49.6 11.0 %fusion.73 = bf16[64,8,128]{2,1,0:T(8,128)(2,1)S(1)} fusion(f32[64,8,128]{2,1,0:T(8,128)S(1)} %get-tuple-element.41, f32[64,8,128]{2,1,0:T(8,128)S(1)} %get-tuple-element.16, f32[70,8,128]{2,1,0:T(8,128)S(1)} %maximum_convert_fusion.1, f32[64,8,128]{2,1,0:T(8,128)S(1)} %get-tuple-element.15, f32[64,8,128]{2,1,0:T(8,128)S(1)} %get-tuple-element.14, ...), kind=kLoop, calls=%fused_computation.313 | loop fusion | flops 27000832 | bytes 8609792 | tf_op jit(solution)/shard_map/add | solution.py:94
  60.6 4.8 %collective-permute-start.2 = (bf16[2,1,8,8,128]{4,3,2,1,0:T(8,128)(2,1)S(1)}, bf16[2,1,8,8,128]{4,3,2,1,0:T(8,128)(2,1)S(1)}, u32[]{:S(2)}, u32[]{:S(2)}) collective-permute-start(bf16[2,1,8,8,128]{4,3,2,1,0:T(8,128)(2,1)S(1)} %get-tuple-element.63), channel_id=1, source_target_pairs={{0,8},{8,16},{16,24},{1,9},{9,17},{17,25},{2,10},{10,18},{18,26},{... | collective-permute-start | bytes 98312 | tf_op jit(solution)/shard_map/ppermute | solution.py:23
  65.4 1.3 collective-permute-start.3
  66.7 0.7 fusion.523
  67.4 2.3 %collective-permute-done.3 = bf16[2,1,8,8,128]{4,3,2,1,0:T(8,128)(2,1)S(1)} collective-permute-done((bf16[2,1,8,8,128]{4,3,2,1,0:T(8,128)(2,1)S(1)}, bf16[2,1,8,8,128]{4,3,2,1,0:T(8,128)(2,1)S(1)}, u32[]{:S(2)}, u32[]{:S(2)}) %collective-permute-start.3) | collective-permute-done | bytes 32800 | tf_op jit(solution)/shard_map/ppermute | solution.py:26
  69.9 0.9 fusion
  70.8 0.9 convolution_bitcast_fusion
  71.6 0.4 fusion.573
  73.1 7.5 %fusion.10 = f32[3,64,8,128]{3,2,1,0:T(8,128)S(1)} fusion(f32[1,3,72,8,128]{4,3,2,1,0:T(8,128)S(1)} %maximum_multiply_fusion, f32[]{:T(128)} %bitcast.58, f32[]{:T(128)} %bitcast.57, f32[]{:T(128)} %bitcast.56, f32[]{:T(128)} %bitcast.55, f32[]{:T(128)} %bitcast.54, f32[]{:T(128)} %bitcast.53, f32[]{:T(128)} %bitcast.52, f32[]{:T(128)} %bitcast.51, ...), kind=kOutput, calls=%fused_computation.237 | convolution fusion | flops 305479680 | bytes 7864360 | tf_op jit(solution)/shard_map/...xy,yv->...xv/dot_general | solution.py:56
  80.6 2.3 %convolution_bitcast_fusion.1 = f32[1,3,64,8,128]{4,3,2,1,0:T(8,128)} fusion(f32[3,64,8,128]{3,2,1,0:T(8,128)S(1)} %fusion.10, f32[]{:T(128)} %fusion.556), kind=kOutput, calls=%fused_computation.232 | convolution fusion | flops 18874944 | bytes 1572868 | tf_op jit(solution)/shard_map/...xy,xu->...uy/dot_general | solution.py:57
  82.9 58.6 %all-reduce.4.cloned.1.call-done = f32[64,8,128]{2,1,0:T(8,128)} async-done(((f32[64,8,128]{2,1,0:T(8,128)}), f32[64,8,128]{2,1,0:T(8,128)}) %all-reduce.4.cloned.1.call-update) | async-done | bytes 262160 | tf_op jit(solution)/shard_map/psum | solution.py:161
  141.5 1.4 dynamic-slice_multiply_fusion
  (25 shorter events, 2.3 us)
Async XLA Ops:
  7.2 39.4 %copy-start = (s32[1,3,64,8,128]{4,3,2,1,0:T(8,128)S(1)}, s32[1,3,64,8,128]{4,3,2,1,0:T(8,128)}, u32[]{:S(2)}) copy-start(s32[1,3,64,8,128]{4,3,2,1,0:T(8,128)} %param.6) | copy-start | bytes 2359300
  7.2 134.4 %all-reduce.4.cloned.1.call-start = ((), (), s32[]{:S(2)}) async-start(), calls=%async_computation | async-start | bytes 524288 | tf_op jit(solution)/shard_map/psum | solution.py:161
  39.9 6.7 %collective-permute-start = (bf16[3,8,128]{2,1,0:T(8,128)(2,1)S(1)}, bf16[3,8,128]{2,1,0:T(8,128)(2,1)S(1)}, u32[]{:S(2)}, u32[]{:S(2)}) collective-permute-start(bf16[3,8,128]{2,1,0:T(8,128)(2,1)S(1)} %get-tuple-element.65), channel_id=1, source_target_pairs={{0,8},{8,16},{16,24},{1,9},{9,17},{17,25},{2,10},{10,18},{18,26},{... | collective-permute-start | bytes 18440 | tf_op jit(solution)/shard_map/ppermute | solution.py:23
  41.2 5.4 %collective-permute-start.1 = (bf16[3,8,128]{2,1,0:T(8,128)(2,1)S(1)}, bf16[3,8,128]{2,1,0:T(8,128)(2,1)S(1)}, u32[]{:S(2)}, u32[]{:S(2)}) collective-permute-start(bf16[3,8,128]{2,1,0:T(8,128)(2,1)S(1)} %get-tuple-element.66), channel_id=1, source_target_pairs={{8,0},{16,8},{24,16},{9,1},{17,9},{25,17},{10,2},{18,10},{26,18},{... | collective-permute-start | bytes 18440 | tf_op jit(solution)/shard_map/ppermute | solution.py:26
  49.5 11.0 %copy-start.1 = (bf16[1,64,8,128]{3,2,1,0:T(8,128)(2,1)S(1)}, bf16[1,64,8,128]{3,2,1,0:T(8,128)(2,1)}, u32[]{:S(2)}) copy-start(bf16[1,64,8,128]{3,2,1,0:T(8,128)(2,1)} %param.5) | copy-start | bytes 393220
  60.6 6.8 %collective-permute-start.2 = (bf16[2,1,8,8,128]{4,3,2,1,0:T(8,128)(2,1)S(1)}, bf16[2,1,8,8,128]{4,3,2,1,0:T(8,128)(2,1)S(1)}, u32[]{:S(2)}, u32[]{:S(2)}) collective-permute-start(bf16[2,1,8,8,128]{4,3,2,1,0:T(8,128)(2,1)S(1)} %get-tuple-element.63), channel_id=1, source_target_pairs={{0,8},{8,16},{16,24},{1,9},{9,17},{17,25},{2,10},{10,18},{18,26},{... | collective-permute-start | bytes 98312 | tf_op jit(solution)/shard_map/ppermute | solution.py:23
  65.4 4.3 %collective-permute-start.3 = (bf16[2,1,8,8,128]{4,3,2,1,0:T(8,128)(2,1)S(1)}, bf16[2,1,8,8,128]{4,3,2,1,0:T(8,128)(2,1)S(1)}, u32[]{:S(2)}, u32[]{:S(2)}) collective-permute-start(bf16[2,1,8,8,128]{4,3,2,1,0:T(8,128)(2,1)S(1)} %get-tuple-element.64), channel_id=1, source_target_pairs={{8,0},{16,8},{24,16},{9,1},{17,9},{25,17},{10,2},{18,10},{26,18},{... | collective-permute-start | bytes 98312 | tf_op jit(solution)/shard_map/ppermute | solution.py:26
Sparse Core Ops, SparseCore 0:
  67.5 73.9 all-reduce.3
where the time goes:
time: 150 us
  waiting for transfers between devices  60.9 us (41%)
  blocking collectives  32.7 us (22%)
  other arithmetic  21 us (14%)
  between operations  14.3 us (10%)
  matrix products  11.6 us (8%)
  starting transfers between devices  8.66 us (6%)
    psum x1, waiting for transfers between devices, per_device(): summed = lax.psum(residual, 'subj')  58.6 us
    all_gather x1, blocking collectives, per_device(): slab_whole = lax.all_gather(template, 'subj', axis=0, tiled=True)  32.7 us
    add x1, other arithmetic, warp(): summed = summed + depth_w[kz] * plane_sum  11 us
    dot_general x2, matrix products, inplane(): mixed = jnp.einsum('...xy,yv->...xv', fields, col_matrix, precision=highest)  8.38 us
    ppermute x2, starting transfers between devices, with_halo(): lax.ppermute(lax.slice_in_dim(block, block.shape[dim] - width, None, axis...  6.04 us
    dot_general x2, matrix products, inplane(): return jnp.einsum('...xy,xu->...uy', mixed, row_matrix, precision=highest)  3.18 us
  transfers between devices with their start and end apart: 5, of which 2 were waited for; matrix products, arithmetic and copies ran while one was open for 12% of the time, Pallas kernels for 0%

commit v1 on v0

--- a/solution.py
+++ b/solution.py
@@ -135,8 +135,38 @@
     return inplane(along, gauss_matrix(force_ext.shape[-2]), gauss_matrix(force_ext.shape[-1]))
 
 
+def swap(block, axis, bit):
+    count = lax.axis_size(axis)
+    return lax.ppermute(block, axis, [(i, i ^ bit) for i in range(count)])
+
+
+def bits_of(count):
+    return [1 << place for place in range(count.bit_length() - 1)]
+
+
+def gather_slab(block, axis):
+    me = lax.axis_index(axis)
+    for bit in bits_of(lax.axis_size(axis)):
+        other = swap(block, axis, bit)
+        upper = (me & bit) != 0
+        block = jnp.concatenate(
+            [jnp.where(upper, other, block), jnp.where(upper, block, other)], axis=0
+        )
+    return block
+
+
+def scatter_sum(block, axis):
+    me = lax.axis_index(axis)
+    for bit in reversed(bits_of(lax.axis_size(axis))):
+        half = block.shape[0] // 2
+        upper = (me & bit) != 0
+        low, high = block[:half], block[half:]
+        block = jnp.where(upper, high, low) + swap(jnp.where(upper, low, high), axis, bit)
+    return block
+
+
 def per_device(template, subjects, shifts, fractions):
-    slab_whole = lax.all_gather(template, "subj", axis=0, tiled=True)
+    slab_whole = gather_slab(template, "subj")
     slab_depth = slab_whole.shape[0]
     groups = lax.axis_size("gz")
     members = lax.axis_size("subj")
@@ -158,9 +188,7 @@
     inside = ((positions >= 0) & (positions < slab_depth * groups)).astype(jnp.float32)
     force_ext = force * inside[:, None, None]
     velocity_step = smooth(force_ext, slab_depth)
-    summed = lax.psum(residual, "subj")
-    share_rows = slab_depth // members
-    own_rows = lax.dynamic_slice_in_dim(summed, lax.axis_index("subj") * share_rows, share_rows, 0)
+    own_rows = scatter_sum(residual, "subj")
     template_force = own_rows * (1.0 / math.sqrt(subject_count * members))
     return (velocity_step, template_force)
 

time: 150 us -> 65.3 us (0.44)
  waiting for transfers between devices: 60.9 us -> 9.69 us
  blocking collectives: 32.7 us -> 0 us
  between operations: 14.3 us -> 0.97 us
  starting transfers between devices: 8.66 us -> 21.7 us
    psum x1 -> x0, waiting for transfers between devices: 58.6 us -> none  [per_device(): summed = lax.psum(residual, 'subj')]
    all_gather x1 -> x0, blocking collectives: 32.7 us -> none  [per_device(): slab_whole = lax.all_gather(template, 'subj', axis=0, tiled=True)]
    ppermute x0 -> x6, starting transfers between devices: none -> 13.5 us  [swap(): return lax.ppermute(block, axis, [(i, i ^ bit) for i in range(count)])]
    ppermute x0 -> x6, waiting for transfers between devices: none -> 6.94 us  [swap(): return lax.ppermute(block, axis, [(i, i ^ bit) for i in range(count)])]
  transfers between devices with their start and end apart: 5 -> 10, of which waited for: 2 -> 6; matrix products, arithmetic and copies ran while one was open for 12% -> 26% of each run, Pallas kernels for 0% -> 0%
where the time goes in v1:
time: 65.3 us; the launch traced here: 64.9 us
  starting transfers between devices  21.7 us (33%)
  other arithmetic  20.4 us (31%)
  matrix products  11.5 us (18%)
  waiting for transfers between devices  9.69 us (15%)
  between operations  0.97 us (1%)
  local copies, waits for them, and re-layouts  0.7 us (1%)
    ppermute x6, starting transfers between devices, swap(): return lax.ppermute(block, axis, [(i, i ^ bit) for i in range(count)])  13.5 us
    add x1, other arithmetic, warp(): summed = summed + depth_w[kz] * plane_sum  11 us
    dot_general x2, matrix products, inplane(): mixed = jnp.einsum('...xy,yv->...xv', fields, col_matrix, precision=highest)  8.31 us
    ppermute x6, waiting for transfers between devices, swap(): return lax.ppermute(block, axis, [(i, i ^ bit) for i in range(count)])  6.94 us
    ppermute x2, starting transfers between devices, with_halo(): lax.ppermute(lax.slice_in_dim(block, block.shape[dim] - width, None, axis...  5.58 us
    dot_general x2, matrix products, inplane(): return jnp.einsum('...xy,xu->...uy', mixed, row_matrix, precision=highest)  3.17 us
    ppermute x2, waiting for transfers between devices, with_halo(): lax.ppermute(lax.slice_in_dim(block, 0, width, axis=dim), axis, backward)  2.75 us
    ppermute x2, starting transfers between devices, with_halo(): lax.ppermute(lax.slice_in_dim(block, 0, width, axis=dim), axis, backward)  2.58 us
  transfers between devices with their start and end apart: 10, of which 6 were waited for; matrix products, arithmetic and copies ran while one was open for 26% of the time, Pallas kernels for 0%

profile of v1, /device:TPU:0, one launch (start us, length us, event | category | flops | bytes accessed | tf_op | source)
XLA Modules:
  0.0 64.9 jit_solution(8782469679185402029)
XLA Ops:
  0.6 3.0 %collective-permute-start = (bf16[8,8,128]{2,1,0:T(8,128)(2,1)}, bf16[8,8,128]{2,1,0:T(8,128)(2,1)S(1)}, u32[]{:S(2)}, u32[]{:S(2)}) collective-permute-start(bf16[8,8,128]{2,1,0:T(8,128)(2,1)} %param.4), channel_id=1, source_target_pairs={{0,1},{1,0},{2,3},{3,2},{4,5},{5,4},{6,7},{7,6},{8,9},{9,8},{10,11... | collective-permute-start | bytes 49160 | tf_op jit(solution)/shard_map/ppermute | solution.py:140
  3.7 1.1 %slice_compare_fusion.4 = (pred[1,1,64,8,128]{4,3,2,1,0:T(8,128)(4,1)S(1)}, pred[1,1,64,8,128]{4,3,2,1,0:T(8,128)(4,1)S(1)}, pred[1,1,64,8,128]{4,3,2,1,0:T(8,128)(4,1)S(1)}) fusion(s32[1,3,64,8,128]{4,3,2,1,0:T(8,128)} %param.6), kind=kLoop, calls=%fused_computation.795 | loop fusion | flops 196608 | bytes 458752 | tf_op jit(solution)/shard_map/eq | solution.py:70
  5.6 0.7 %broadcast_select_fusion.5 = (bf16[8,8,128]{2,1,0:T(8,128)(2,1)S(1)}, bf16[8,8,128]{2,1,0:T(8,128)(2,1)S(1)}) fusion(bf16[8,8,128]{2,1,0:T(8,128)(2,1)S(1)} %collective-permute-done, bf16[8,8,128]{2,1,0:T(8,128)(2,1)} %param.4, pred[]{:T(512)S(6)} %ne.14), kind=kLoop, calls=%fused_computation.838 | loop fusion | flops 16384 | bytes 65537 | tf_op jit(solution)/shard_map/jit(_where)/select_n | solution.py:153
  6.3 2.1 %collective-permute-start.1 = (bf16[16,8,128]{2,1,0:T(8,128)(2,1)S(1)}, bf16[16,8,128]{2,1,0:T(8,128)(2,1)S(1)}, u32[]{:S(2)}, u32[]{:S(2)}) collective-permute-start(bf16[16,8,128]{2,1,0:T(8,128)(2,1)S(1)} %pad_maximum_fusion.3), channel_id=1, source_target_pairs={{0,2},{1,3},{2,0},{3,1},{4,6},{5,7},{6,4},{7,5},{8,10},{9,11},{10,... | collective-permute-start | bytes 98312 | tf_op jit(solution)/shard_map/ppermute | solution.py:140
  8.5 0.7 %broadcast_divide_fusion = f32[9]{0:T(128)S(1)} fusion(f32[]{:T(128)} %fusion.555), kind=kLoop, calls=%fused_computation.859 | loop fusion | flops 54 | bytes 40 | tf_op jit(solution)/shard_map/div | solution.py:38
  9.1 1.2 %collective-permute-done.1 = bf16[16,8,128]{2,1,0:T(8,128)(2,1)S(1)} collective-permute-done((bf16[16,8,128]{2,1,0:T(8,128)(2,1)S(1)}, bf16[16,8,128]{2,1,0:T(8,128)(2,1)S(1)}, u32[]{:S(2)}, u32[]{:S(2)}) %collective-permute-start.1) | collective-permute-done | bytes 32800 | tf_op jit(solution)/shard_map/ppermute | solution.py:140
  10.4 3.1 %collective-permute-start.2 = (bf16[32,8,128]{2,1,0:T(8,128)(2,1)S(1)}, bf16[32,8,128]{2,1,0:T(8,128)(2,1)S(1)}, u32[]{:S(2)}, u32[]{:S(2)}) collective-permute-start(bf16[32,8,128]{2,1,0:T(8,128)(2,1)S(1)} %pad_maximum_fusion), channel_id=1, source_target_pairs={{0,4},{1,5},{2,6},{3,7},{4,0},{5,1},{6,2},{7,3},{8,12},{9,13},{10,... | collective-permute-start | bytes 196616 | tf_op jit(solution)/shard_map/ppermute | solution.py:140
  13.5 0.7 %fusion.568 = (f32[1]{0:T(128)}, f32[1]{0:T(128)}, f32[1]{0:T(128)}, f32[1]{0:T(128)}, f32[1]{0:T(128)}, /*index=5*/f32[1]{0:T(128)}, f32[1]{0:T(128)}, f32[1]{0:T(128)}, f32[1]{0:T(128)}) fusion(f32[9]{0:T(128)S(1)} %broadcast_divide_fusion), kind=kLoop, calls=%fused_computation.872 | loop fusion | bytes 72 | tf_op jit(solution)/shard_map/slice | solution.py:61
  14.2 1.6 %collective-permute-done.2 = bf16[32,8,128]{2,1,0:T(8,128)(2,1)S(1)} collective-permute-done((bf16[32,8,128]{2,1,0:T(8,128)(2,1)S(1)}, bf16[32,8,128]{2,1,0:T(8,128)(2,1)S(1)}, u32[]{:S(2)}, u32[]{:S(2)}) %collective-permute-start.2) | collective-permute-done | bytes 65568 | tf_op jit(solution)/shard_map/ppermute | solution.py:140
  15.8 1.3 %collective-permute-start.3 = (bf16[3,8,128]{2,1,0:T(8,128)(2,1)S(1)}, bf16[3,8,128]{2,1,0:T(8,128)(2,1)S(1)}, u32[]{:S(2)}, u32[]{:S(2)}) collective-permute-start(bf16[3,8,128]{2,1,0:T(8,128)(2,1)S(1)} %slice.1120), channel_id=1, source_target_pairs={{0,8},{8,16},{16,24},{1,9},{9,17},{17,25},{2,10},{10,18},{18,26},{... | collective-permute-start | bytes 18440 | tf_op jit(solution)/shard_map/ppermute | solution.py:23
  17.1 1.3 %collective-permute-start.4 = (bf16[3,8,128]{2,1,0:T(8,128)(2,1)S(1)}, bf16[3,8,128]{2,1,0:T(8,128)(2,1)S(1)}, u32[]{:S(2)}, u32[]{:S(2)}) collective-permute-start(bf16[3,8,128]{2,1,0:T(8,128)(2,1)S(1)} %slice.1121), channel_id=1, source_target_pairs={{8,0},{16,8},{24,16},{9,1},{17,9},{25,17},{10,2},{18,10},{26,18},{... | collective-permute-start | bytes 18440 | tf_op jit(solution)/shard_map/ppermute | solution.py:26
  18.4 1.1 %convert_element_type.59 = f32[1,3,64,8,128]{4,3,2,1,0:T(8,128)S(1)} convert(bf16[1,3,64,8,128]{4,3,2,1,0:T(8,128)(2,1)} %param.7) | non-fusion elementwise | flops 196608 | bytes 1179648 | tf_op jit(solution)/shard_map/convert_element_type | solution.py:78
  19.5 2.7 %collective-permute-done.4 = bf16[3,8,128]{2,1,0:T(8,128)(2,1)S(1)} collective-permute-done((bf16[3,8,128]{2,1,0:T(8,128)(2,1)S(1)}, bf16[3,8,128]{2,1,0:T(8,128)(2,1)S(1)}, u32[]{:S(2)}, u32[]{:S(2)}) %collective-permute-start.4) | collective-permute-done | bytes 6176 | tf_op jit(solution)/shard_map/ppermute | solution.py:26
  25.2 11.0 %fusion.73 = bf16[64,8,128]{2,1,0:T(8,128)(2,1)S(1)} fusion(f32[64,8,128]{2,1,0:T(8,128)S(1)} %get-tuple-element.41, f32[64,8,128]{2,1,0:T(8,128)S(1)} %get-tuple-element.16, f32[70,8,128]{2,1,0:T(8,128)S(1)} %maximum_convert_fusion.1, f32[64,8,128]{2,1,0:T(8,128)S(1)} %get-tuple-element.15, f32[64,8,128]{2,1,0:T(8,128)S(1)} %get-tuple-element.14, ...), kind=kLoop, calls=%fused_computation.313 | loop fusion | flops 27000832 | bytes 8609792 | tf_op jit(solution)/shard_map/add | solution.py:94
  36.2 4.3 %collective-permute-start.5 = (bf16[2,1,8,8,128]{4,3,2,1,0:T(8,128)(2,1)S(1)}, bf16[2,1,8,8,128]{4,3,2,1,0:T(8,128)(2,1)S(1)}, u32[]{:S(2)}, u32[]{:S(2)}) collective-permute-start(bf16[2,1,8,8,128]{4,3,2,1,0:T(8,128)(2,1)S(1)} %get-tuple-element.63), channel_id=1, source_target_pairs={{0,8},{8,16},{16,24},{1,9},{9,17},{17,25},{2,10},{10,18},{18,26},{... | collective-permute-start | bytes 98312 | tf_op jit(solution)/shard_map/ppermute | solution.py:23
  40.5 1.3 %collective-permute-start.6 = (bf16[2,1,8,8,128]{4,3,2,1,0:T(8,128)(2,1)S(1)}, bf16[2,1,8,8,128]{4,3,2,1,0:T(8,128)(2,1)S(1)}, u32[]{:S(2)}, u32[]{:S(2)}) collective-permute-start(bf16[2,1,8,8,128]{4,3,2,1,0:T(8,128)(2,1)S(1)} %get-tuple-element.64), channel_id=1, source_target_pairs={{8,0},{16,8},{24,16},{9,1},{17,9},{25,17},{10,2},{18,10},{26,18},{... | collective-permute-start | bytes 98312 | tf_op jit(solution)/shard_map/ppermute | solution.py:26
  41.9 2.7 %collective-permute-start.7 = (f32[32,8,128]{2,1,0:T(8,128)S(1)}, f32[32,8,128]{2,1,0:T(8,128)S(1)}, u32[]{:S(2)}, u32[]{:S(2)}) collective-permute-start(f32[32,8,128]{2,1,0:T(8,128)S(1)} %select_bitcast_fusion), channel_id=1, source_target_pairs={{0,4},{1,5},{2,6},{3,7},{4,0},{5,1},{6,2},{7,3},{8,12},{9,13},{10,... | collective-permute-start | bytes 393224 | tf_op jit(solution)/shard_map/ppermute | solution.py:140
  44.8 0.9 %fusion = f32[5,80,8,128]{3,2,1,0:T(8,128)S(1)} fusion(f32[1,1,80,8,128]{4,3,2,1,0:T(8,128)S(1)} %get-tuple-element.49, f32[1,1,80,8,128]{4,3,2,1,0:T(8,128)S(1)} %get-tuple-element.48, f32[1,1,80,8,128]{4,3,2,1,0:T(8,128)S(1)} %get-tuple-element.51, f32[2,1,80,8,128]{4,3,2,1,0:T(8,128)S(1)} %maximum_convert_fusion), kind=kOutput, calls=%fused_computation.215 | convolution fusion | flops 630423552 | bytes 3276800 | tf_op jit(solution)/shard_map/...xy,yv->...xv/dot_general | solution.py:56
  45.7 0.9 %convolution_bitcast_fusion = f32[5,1,80,8,128]{4,3,2,0,1:T(8,128)S(1)} fusion(f32[5,80,8,128]{3,2,1,0:T(8,128)S(1)} %fusion), kind=kOutput, calls=%fused_computation.222 | convolution fusion | flops 39321792 | bytes 3276800 | tf_op jit(solution)/shard_map/...xy,xu->...uy/dot_general | solution.py:57
  48.0 3.8 %collective-permute-done.7 = f32[32,8,128]{2,1,0:T(8,128)S(1)} collective-permute-done((f32[32,8,128]{2,1,0:T(8,128)S(1)}, f32[32,8,128]{2,1,0:T(8,128)S(1)}, u32[]{:S(2)}, u32[]{:S(2)}) %collective-permute-start.7) | collective-permute-done | bytes 131104 | tf_op jit(solution)/shard_map/ppermute | solution.py:140
  51.9 1.0 %collective-permute-start.8 = (f32[16,8,128]{2,1,0:T(8,128)S(1)}, f32[16,8,128]{2,1,0:T(8,128)S(1)}, u32[]{:S(2)}, u32[]{:S(2)}) collective-permute-start(f32[16,8,128]{2,1,0:T(8,128)S(1)} %slice_select_fusion), channel_id=1, source_target_pairs={{0,2},{1,3},{2,0},{3,1},{4,6},{5,7},{6,4},{7,5},{8,10},{9,11},{10,... | collective-permute-start | bytes 196616 | tf_op jit(solution)/shard_map/ppermute | solution.py:140
  52.8 7.4 %fusion.10 = f32[3,64,8,128]{3,2,1,0:T(8,128)S(1)} fusion(f32[1,3,72,8,128]{4,3,2,1,0:T(8,128)S(1)} %maximum_multiply_fusion, f32[]{:T(128)} %bitcast.58, f32[]{:T(128)} %bitcast.57, f32[]{:T(128)} %bitcast.56, f32[]{:T(128)} %bitcast.55, f32[]{:T(128)} %bitcast.54, f32[]{:T(128)} %bitcast.53, f32[]{:T(128)} %bitcast.52, f32[]{:T(128)} %bitcast.51, ...), kind=kOutput, calls=%fused_computation.237 | convolution fusion | flops 305479680 | bytes 7864360 | tf_op jit(solution)/shard_map/...xy,yv->...xv/dot_general | solution.py:56
  60.3 1.6 %collective-permute-start.9 = (f32[8,8,128]{2,1,0:T(8,128)S(1)}, f32[8,8,128]{2,1,0:T(8,128)S(1)}, u32[]{:S(2)}, u32[]{:S(2)}) collective-permute-start(f32[8,8,128]{2,1,0:T(8,128)S(1)} %slice_select_fusion.1), channel_id=1, source_target_pairs={{0,1},{1,0},{2,3},{3,2},{4,5},{5,4},{6,7},{7,6},{8,9},{9,8},{10,11... | collective-permute-start | bytes 98312 | tf_op jit(solution)/shard_map/ppermute | solution.py:140
  61.9 2.3 %convolution_bitcast_fusion.1 = f32[1,3,64,8,128]{4,3,2,1,0:T(8,128)} fusion(f32[3,64,8,128]{3,2,1,0:T(8,128)S(1)} %fusion.10, f32[]{:T(128)} %fusion.555), kind=kOutput, calls=%fused_computation.232 | convolution fusion | flops 18874944 | bytes 1572868 | tf_op jit(solution)/shard_map/...xy,xu->...uy/dot_general | solution.py:57
  (44 shorter events, 6.3 us)
Async XLA Ops:
  0.6 21.6 %copy-start = (s32[1,3,64,8,128]{4,3,2,1,0:T(8,128)S(1)}, s32[1,3,64,8,128]{4,3,2,1,0:T(8,128)}, u32[]{:S(2)}) copy-start(s32[1,3,64,8,128]{4,3,2,1,0:T(8,128)} %param.6) | copy-start | bytes 2359300
  0.6 5.0 %collective-permute-start = (bf16[8,8,128]{2,1,0:T(8,128)(2,1)}, bf16[8,8,128]{2,1,0:T(8,128)(2,1)S(1)}, u32[]{:S(2)}, u32[]{:S(2)}) collective-permute-start(bf16[8,8,128]{2,1,0:T(8,128)(2,1)} %param.4), channel_id=1, source_target_pairs={{0,1},{1,0},{2,3},{3,2},{4,5},{5,4},{6,7},{7,6},{8,9},{9,8},{10,11... | collective-permute-start | bytes 49160 | tf_op jit(solution)/shard_map/ppermute | solution.py:140
  6.3 4.0 %collective-permute-start.1 = (bf16[16,8,128]{2,1,0:T(8,128)(2,1)S(1)}, bf16[16,8,128]{2,1,0:T(8,128)(2,1)S(1)}, u32[]{:S(2)}, u32[]{:S(2)}) collective-permute-start(bf16[16,8,128]{2,1,0:T(8,128)(2,1)S(1)} %pad_maximum_fusion.3), channel_id=1, source_target_pairs={{0,2},{1,3},{2,0},{3,1},{4,6},{5,7},{6,4},{7,5},{8,10},{9,11},{10,... | collective-permute-start | bytes 98312 | tf_op jit(solution)/shard_map/ppermute | solution.py:140
  10.4 5.3 %collective-permute-start.2 = (bf16[32,8,128]{2,1,0:T(8,128)(2,1)S(1)}, bf16[32,8,128]{2,1,0:T(8,128)(2,1)S(1)}, u32[]{:S(2)}, u32[]{:S(2)}) collective-permute-start(bf16[32,8,128]{2,1,0:T(8,128)(2,1)S(1)} %pad_maximum_fusion), channel_id=1, source_target_pairs={{0,4},{1,5},{2,6},{3,7},{4,0},{5,1},{6,2},{7,3},{8,12},{9,13},{10,... | collective-permute-start | bytes 196616 | tf_op jit(solution)/shard_map/ppermute | solution.py:140
  15.8 3.7 %collective-permute-start.3 = (bf16[3,8,128]{2,1,0:T(8,128)(2,1)S(1)}, bf16[3,8,128]{2,1,0:T(8,128)(2,1)S(1)}, u32[]{:S(2)}, u32[]{:S(2)}) collective-permute-start(bf16[3,8,128]{2,1,0:T(8,128)(2,1)S(1)} %slice.1120), channel_id=1, source_target_pairs={{0,8},{8,16},{16,24},{1,9},{9,17},{17,25},{2,10},{10,18},{18,26},{... | collective-permute-start | bytes 18440 | tf_op jit(solution)/shard_map/ppermute | solution.py:23
  17.1 5.1 %collective-permute-start.4 = (bf16[3,8,128]{2,1,0:T(8,128)(2,1)S(1)}, bf16[3,8,128]{2,1,0:T(8,128)(2,1)S(1)}, u32[]{:S(2)}, u32[]{:S(2)}) collective-permute-start(bf16[3,8,128]{2,1,0:T(8,128)(2,1)S(1)} %slice.1121), channel_id=1, source_target_pairs={{8,0},{16,8},{24,16},{9,1},{17,9},{25,17},{10,2},{18,10},{26,18},{... | collective-permute-start | bytes 18440 | tf_op jit(solution)/shard_map/ppermute | solution.py:26
  25.2 11.0 %copy-start.1 = (bf16[1,64,8,128]{3,2,1,0:T(8,128)(2,1)S(1)}, bf16[1,64,8,128]{3,2,1,0:T(8,128)(2,1)}, u32[]{:S(2)}) copy-start(bf16[1,64,8,128]{3,2,1,0:T(8,128)(2,1)} %param.5) | copy-start | bytes 393220
  36.2 8.3 %collective-permute-start.5 = (bf16[2,1,8,8,128]{4,3,2,1,0:T(8,128)(2,1)S(1)}, bf16[2,1,8,8,128]{4,3,2,1,0:T(8,128)(2,1)S(1)}, u32[]{:S(2)}, u32[]{:S(2)}) collective-permute-start(bf16[2,1,8,8,128]{4,3,2,1,0:T(8,128)(2,1)S(1)} %get-tuple-element.63), channel_id=1, source_target_pairs={{0,8},{8,16},{16,24},{1,9},{9,17},{17,25},{2,10},{10,18},{18,26},{... | collective-permute-start | bytes 98312 | tf_op jit(solution)/shard_map/ppermute | solution.py:23
  40.5 4.0 %collective-permute-start.6 = (bf16[2,1,8,8,128]{4,3,2,1,0:T(8,128)(2,1)S(1)}, bf16[2,1,8,8,128]{4,3,2,1,0:T(8,128)(2,1)S(1)}, u32[]{:S(2)}, u32[]{:S(2)}) collective-permute-start(bf16[2,1,8,8,128]{4,3,2,1,0:T(8,128)(2,1)S(1)} %get-tuple-element.64), channel_id=1, source_target_pairs={{8,0},{16,8},{24,16},{9,1},{17,9},{25,17},{10,2},{18,10},{26,18},{... | collective-permute-start | bytes 98312 | tf_op jit(solution)/shard_map/ppermute | solution.py:26
  41.9 10.0 %collective-permute-start.7 = (f32[32,8,128]{2,1,0:T(8,128)S(1)}, f32[32,8,128]{2,1,0:T(8,128)S(1)}, u32[]{:S(2)}, u32[]{:S(2)}) collective-permute-start(f32[32,8,128]{2,1,0:T(8,128)S(1)} %select_bitcast_fusion), channel_id=1, source_target_pairs={{0,4},{1,5},{2,6},{3,7},{4,0},{5,1},{6,2},{7,3},{8,12},{9,13},{10,... | collective-permute-start | bytes 393224 | tf_op jit(solution)/shard_map/ppermute | solution.py:140
  51.9 8.4 %collective-permute-start.8 = (f32[16,8,128]{2,1,0:T(8,128)S(1)}, f32[16,8,128]{2,1,0:T(8,128)S(1)}, u32[]{:S(2)}, u32[]{:S(2)}) collective-permute-start(f32[16,8,128]{2,1,0:T(8,128)S(1)} %slice_select_fusion), channel_id=1, source_target_pairs={{0,2},{1,3},{2,0},{3,1},{4,6},{5,7},{6,4},{7,5},{8,10},{9,11},{10,... | collective-permute-start | bytes 196616 | tf_op jit(solution)/shard_map/ppermute | solution.py:140
  60.3 4.0 %collective-permute-start.9 = (f32[8,8,128]{2,1,0:T(8,128)S(1)}, f32[8,8,128]{2,1,0:T(8,128)S(1)}, u32[]{:S(2)}, u32[]{:S(2)}) collective-permute-start(f32[8,8,128]{2,1,0:T(8,128)S(1)} %slice_select_fusion.1), channel_id=1, source_target_pairs={{0,1},{1,0},{2,3},{3,2},{4,5},{5,4},{6,7},{7,6},{8,9},{9,8},{10,11... | collective-permute-start | bytes 98312 | tf_op jit(solution)/shard_map/ppermute | solution.py:140

commit v2 on v0

v2 whole, which is shorter than its diff:
```python
import math

import jax
import jax.numpy as jnp
from jax import lax
from jax.experimental import pallas as pl
from jax.experimental.pallas import tpu as pltpu
from jax.sharding import PartitionSpec as P

SHIFT = 2
WIN = 4
SMOOTH = 4
EDGE = WIN + SMOOTH
HALO = EDGE + SHIFT + 1
TAPS = 2 * SHIFT + 2
sigma = 1.5
epsilon = 1e-05
f32 = jnp.float32
bf16 = jnp.bfloat16
VMEM_LIMIT = 48 * 1024 * 1024

raw = [math.exp(-k * k / (2 * sigma * sigma)) for k in range(SMOOTH + 1)]
norm = raw[0] + 2 * sum(raw[1:])
GAUSS = [value / norm for value in raw]


def swap(block, axis, bit):
    count = lax.axis_size(axis)
    return lax.ppermute(block, axis, [(i, i ^ bit) for i in range(count)])


def swap_near(block, axis):
    count = lax.axis_size(axis)
    pairs = [(i, i ^ 1) for i in range(count) if (i ^ 1) < count]
    return lax.ppermute(block, axis, pairs)


def swap_far(block, axis):
    count = lax.axis_size(axis)
    ups = [(i, i + 1) for i in range(1, count - 1, 2)]
    return lax.ppermute(block, axis, ups + [(target, source) for source, target in ups])


def bits_of(count):
    return [1 << place for place in range(count.bit_length() - 1)]


def mirrored(number, count):
    places = count.bit_length() - 1
    return sum(((number >> place) & 1) << (places - 1 - place) for place in range(places))


def scatter_sum(keep, send, axis, hold):
    for stage, bit in enumerate(bits_of(lax.axis_size(axis))):
        if stage:
            pairs = keep.reshape((-1, 2, share_of(keep, axis, stage)) + keep.shape[1:])
            keep, send = [pairs[:, part].reshape((-1,) + keep.shape[1:]) for part in (0, 1)]
        keep = hold(stage, keep + swap(send, axis, bit))
    return keep


def share_of(keep, axis, stage):
    return keep.shape[0] * (1 << stage) // lax.axis_size(axis)


def at_ends(axis, low, high):
    odd = lax.axis_index(axis) % 2 == 1
    return jnp.where(odd, low, high), jnp.where(odd, high, low)


def shift_matrix(offsets, cols):
    source = lax.broadcasted_iota(jnp.int32, (cols, cols), 0)
    target = lax.broadcasted_iota(jnp.int32, (cols, cols), 1)
    return jnp.concatenate(
        [(source == target + offset).astype(f32) for offset in offsets], axis=1
    ).astype(bf16)


def rows_at(value, index):
    return jnp.take_along_axis(value, index, axis=0, mode="promise_in_bounds")


def even_odd(base, frac):
    even = (base == -2.0) | (base == 0.0) | (base == 2.0)
    rest = 1.0 - frac
    return jnp.where(even, rest, frac), jnp.where(even, frac, rest)


def warp_slice(shifted, plane, sz, sr, sc, fz, fr, fc):
    rows = sz.shape[0]
    row = lax.broadcasted_iota(jnp.int32, sz.shape, 0).astype(f32) + sr
    top = rows - 1.0
    index0 = jnp.clip(row, 0.0, top).astype(jnp.int32)
    index1 = jnp.clip(row + 1.0, 0.0, top).astype(jnp.int32)
    weight0 = jnp.where((row >= 0.0) & (row <= top), 1.0 - fr, 0.0)
    weight1 = jnp.where((row >= -1.0) & (row <= top - 1.0), fr, 0.0)
    col_e, col_o = even_odd(sc, fc)
    dep_e, dep_o = even_odd(sz, fz)
    c1, c2, c3, c4 = [sc >= edge for edge in (-1.0, 0.0, 1.0, 2.0)]
    z1, z2, z3, z4 = [sz >= edge for edge in (-1.0, 0.0, 1.0, 2.0)]
    picks = {2: (c1, z1), 3: (c2, z2), 4: (c3, z3), 5: (c4, z4)}
    planes = [None, None]
    for kz in range(TAPS):
        corner = [[None, None], [None, None]]
        for kc in range(TAPS):
            value = shifted[kc, plane + kz]
            for b, index in ((0, index0), (1, index1)):
                taken = rows_at(value, index)
                if kc < 2:
                    corner[b][kc] = taken
                else:
                    corner[b][kc % 2] = jnp.where(picks[kc][0], taken, corner[b][kc % 2])
        flat = corner[0] + corner[1]
        if kz < 2:
            planes[kz] = flat
        else:
            mask = picks[kz][1]
            planes[kz % 2] = [jnp.where(mask, new, old) for new, old in zip(flat, planes[kz % 2])]
    parts = []
    for e0, o0, e1, o1 in planes:
        parts.append(
            weight0 * (col_e * e0 + col_o * o0) + weight1 * (col_e * e1 + col_o * o1)
        )
    summed = dep_e * parts[0] + dep_o * parts[1]
    return summed.astype(bf16).astype(f32)


def move_columns(slab, shifted, start, step):
    rows, cols = slab.shape[1:]
    offsets = [k - SHIFT for k in range(TAPS) if k != SHIFT]
    matrix = shift_matrix(offsets, cols)
    block = slab[start : start + step]
    shifted[SHIFT, start : start + step] = block
    moved = jnp.dot(
        block.reshape(step * rows, cols).astype(bf16), matrix, preferred_element_type=f32
    )
    for number, offset in enumerate(offsets):
        shifted[offset + SHIFT, start : start + step] = moved[
            :, number * cols : (number + 1) * cols
        ].reshape(step, rows, cols)


def vmem_specs(count):
    return [pl.BlockSpec(memory_space=pltpu.VMEM)] * count


SMEM_SPEC = pl.BlockSpec(memory_space=pltpu.SMEM)


def local_call(kernel, name, outs, inputs, scratch, flops, scalars=True):
    return pl.pallas_call(
        kernel,
        out_shape=[jax.ShapeDtypeStruct(shape, f32) for shape in outs],
        in_specs=([SMEM_SPEC] if scalars else []) + vmem_specs(inputs),
        out_specs=vmem_specs(len(outs)),
        scratch_shapes=[pltpu.VMEM(shape, f32) for shape in scratch],
        compiler_params=pltpu.CompilerParams(vmem_limit_bytes=VMEM_LIMIT),
        cost_estimate=pl.CostEstimate(flops=flops, bytes_accessed=8_000_000, transcendentals=0),
        name=name,
    )


def slice_fields(shifts, fractions, z):
    return [shifts[axis, z].astype(f32) for axis in range(3)] + [
        fractions[axis, z].astype(f32) for axis in range(3)
    ]


def build_inner_warp(depth, rows, cols, members):
    share = depth // members

    def kernel(place, pieces, shifts, fractions, warped, slab, shifted):
        me = place[1]
        for k in range(members):
            shard = me ^ mirrored(k, members)
            slab[pl.ds(shard * share, share)] = pieces[k * share : (k + 1) * share].astype(f32)
        for start in range(0, depth, depth // 2):
            move_columns(slab, shifted, start, depth // 2)

        def body(i, carry):
            z = i + EDGE
            warped[i] = warp_slice(shifted, z - SHIFT, *slice_fields(shifts, fractions, z))
            return carry

        lax.fori_loop(0, depth - 2 * EDGE, body, 0, unroll=2)

    return local_call(
        kernel, "inner_warp", [(depth - 2 * EDGE, rows, cols)], 3,
        [(depth, rows, cols), (TAPS, depth, rows, cols)], 1_000_000_000,
    )


def build_outer_warp(depth, rows, cols, members):
    share = depth // members
    ext = depth + 2 * EDGE
    planes = 2 * HALO

    def kernel(
        place, low_t, high_t, near_t, far_t, near_m, far_m, shifts, fractions, subjects, inner,
        warped, keep, send, slab, shifted,
    ):
        odd = place[0] % 2 == 1
        me = place[1]
        near, far = near_t[...].astype(f32), far_t[...].astype(f32)
        slab[0:HALO] = jnp.where(odd, near, far)
        slab[HALO:planes] = low_t[...].astype(f32)
        slab[planes : planes + HALO] = high_t[...].astype(f32)
        slab[planes + HALO : 2 * planes] = jnp.where(odd, far, near)
        move_columns(slab, shifted, 0, 2 * planes)
        warped[2 * EDGE : depth] = inner[...]

        def body(z, carry):
            def edge(low):
                fields = []
                for axis in range(6):
                    one, two = near_m[axis, z].astype(f32), far_m[axis, z].astype(f32)
                    fields.append(jnp.where(odd, one, two) if low else jnp.where(odd, two, one))
                return fields

            inside = depth - EDGE + z
            warped[z] = warp_slice(shifted, z + 1, *edge(True))
            warped[z + EDGE] = warp_slice(
                shifted, z + EDGE + 1, *slice_fields(shifts, fractions, z)
            )
            warped[z + depth] = warp_slice(
                shifted, planes + z + 1, *slice_fields(shifts, fractions, inside)
            )
            warped[z + depth + EDGE] = warp_slice(
                shifted, planes + z + EDGE + 1, *edge(False)
            )
            return carry

        lax.fori_loop(0, EDGE, body, 0)

        for k in range(members):
            shard = me ^ k
            target = send if k % 2 else keep
            start = shard * share
            target[(k // 2) * share : (k // 2 + 1) * share] = (
                subjects[pl.ds(start, share)].astype(f32) - warped[pl.ds(EDGE + start, share)]
            )

    half = (depth // 2, rows, cols)
    return local_call(
        kernel, "outer_warp", [(ext, rows, cols), half, half], 10,
        [(2 * planes, rows, cols), (TAPS, 2 * planes, rows, cols)], 600_000_000,
    )


def band(cols, radius):
    apart = jnp.abs(
        lax.broadcasted_iota(jnp.int32, (cols, cols), 0)
        - lax.broadcasted_iota(jnp.int32, (cols, cols), 1)
    )
    return (apart <= radius).astype(f32)


def column_difference(cols):
    apart = lax.broadcasted_iota(jnp.int32, (cols, cols), 0) - lax.broadcasted_iota(
        jnp.int32, (cols, cols), 1
    )
    return jnp.where(apart == 1, 0.5, jnp.where(apart == -1, -0.5, 0.0)).astype(f32)


def gauss_columns(cols):
    apart = jnp.abs(
        lax.broadcasted_iota(jnp.int32, (cols, cols), 0)
        - lax.broadcasted_iota(jnp.int32, (cols, cols), 1)
    )
    result = jnp.zeros((cols, cols), f32)
    for k, tap in enumerate(GAUSS):
        result = jnp.where(apart == k, f32(tap), result)
    return result


def split(value):
    high = value.astype(bf16)
    return high, (value - high.astype(f32)).astype(bf16)


def take_rows(value, index):
    return jnp.take_along_axis(value, index, axis=0, mode="promise_in_bounds")


def row_window(value, row):
    first = row < WIN
    half = value + take_rows(value, row ^ 1)
    half = half + take_rows(half, row ^ 2)
    outer = jnp.clip(jnp.where(first, row - 1, row + 1), 0, 2 * WIN - 1)
    outer_two = jnp.clip(jnp.where(first, row - 2, row + 2), 0, 2 * WIN - 1)
    reach = jnp.where(first, row, 2 * WIN - 1 - row)
    across = take_rows(value, row ^ WIN) + jnp.where(
        reach >= 1, take_rows(value, outer ^ WIN), 0.0
    )
    return half + across + jnp.where(reach >= 2, take_rows(across, outer_two), 0.0)


def z_windows(load, count):
    x = [load(k) for k in range(count + 2 * WIN)]
    two = [x[k] + x[k + 1] for k in range(count + 2 * WIN - 1)]
    four = [two[k] + two[k + 2] for k in range(count + 2 * WIN - 3)]
    return [four[k] + four[k + 4] + x[k + 8] for k in range(count)]


STEP = 8
CHUNK = 16
SCALE = 1.0 / float((2 * WIN + 1) ** 3)


def flat(value):
    return value.reshape(-1, value.shape[-1])


def square_columns(product, twice):
    pair = jnp.concatenate(split(product), axis=1)
    return jnp.dot(pair, twice, preferred_element_type=f32)


def build_image(depth, rows, cols):
    ext, mid = depth + 2 * EDGE, depth + 2 * SMOOTH

    def kernel(place, near_m, far_m, subjects, image, mean, variance, boxes):
        odd = place[0] % 2 == 1
        near, far = near_m[6].astype(f32), far_m[6].astype(f32)
        image[0:EDGE] = jnp.where(odd, near, far)
        image[EDGE : EDGE + depth] = subjects[...].astype(f32)
        image[EDGE + depth : ext] = jnp.where(odd, far, near)
        box = band(cols, WIN).astype(bf16)
        twice = jnp.concatenate([box, box], axis=0)

        def columns(i, carry):
            at = pl.ds(i * CHUNK, CHUNK)
            two = flat(image[at])
            results = [
                jnp.dot(two.astype(bf16), box, preferred_element_type=f32),
                square_columns(two * two, twice),
            ]
            for field, result in enumerate(results):
                boxes[field, at] = result.reshape(CHUNK, rows, cols)
            return carry

        lax.fori_loop(0, ext // CHUNK, columns, 0)
        row = lax.broadcasted_iota(jnp.int32, (rows, cols), 0)

        def local(i, carry):
            start = i * STEP
            one, two = [
                [row_window(v, row) * SCALE for v in z_windows(lambda k: boxes[f, start + k], STEP)]
                for f in range(2)
            ]
            for k in range(STEP):
                mean[start + k] = one[k]
                variance[start + k] = two[k] - one[k] * one[k]
            return carry

        lax.fori_loop(0, mid // STEP, local, 0)

    return local_call(
        kernel, "image",
        [(ext, rows, cols), (mid, rows, cols), (mid, rows, cols)], 3,
        [(2, ext, rows, cols)], 400_000_000,
    )


def build_boxes(depth, rows, cols):
    ext = depth + 2 * EDGE

    def kernel(warped, image, boxes, slope):
        box = band(cols, WIN)
        first = jnp.concatenate([box, column_difference(cols)], axis=1).astype(bf16)
        box = box.astype(bf16)
        twice = jnp.concatenate([box, box], axis=0)

        def columns(i, carry):
            at = pl.ds(i * CHUNK, CHUNK)
            one, two = flat(warped[at]), flat(image[at])
            both = jnp.dot(one.astype(bf16), first, preferred_element_type=f32)
            results = [both[:, :cols], square_columns(one * one, twice), square_columns(one * two, twice)]
            for field, result in enumerate(results):
                boxes[field, at] = result.reshape(CHUNK, rows, cols)
            slope[at] = both[:, cols:].reshape(CHUNK, rows, cols)
            return carry

        lax.fori_loop(0, ext // CHUNK, columns, 0)

    return local_call(
        kernel, "boxes", [(3, ext, rows, cols), (ext, rows, cols)], 2, [], 400_000_000, scalars=False
    )


def build_force(depth, rows, cols, groups):
    mid = depth + 2 * SMOOTH

    def kernel(place, warped, image, mean, variance, boxes, slope, force):
        row = lax.broadcasted_iota(jnp.int32, (rows, cols), 0)

        def local(i, carry):
            start = i * STEP
            means = [
                [row_window(v, row) * SCALE for v in z_windows(lambda k: boxes[f, start + k], STEP)]
                for f in range(3)
            ]
            for k in range(STEP):
                mi, mii, mij = [field[k] for field in means]
                mj, var_j = mean[start + k], variance[start + k]
                at = start + k + WIN
                centre = warped[at]
                var_i = mii - mi * mi
                cov = mij - mi * mj
                factor = (image[at] - mj - cov / (var_i + epsilon) * (centre - mi)) / jnp.sqrt(
                    var_i * var_j + epsilon
                )
                grad_z = 0.5 * (warped[at + 1] - warped[at - 1])
                below = jnp.where(row < rows - 1, pltpu.roll(centre, rows - 1, 0), 0.0)
                above = jnp.where(row > 0, pltpu.roll(centre, 1, 0), 0.0)
                force[0, start + k] = factor * grad_z
                force[1, start + k] = factor * (0.5 * (below - above))
                force[2, start + k] = factor * slope[at]
            return carry

        lax.fori_loop(0, mid // STEP, local, 0)

        @pl.when(place[0] == 0)
        def _():
            force[:, 0:SMOOTH] = jnp.zeros((3, SMOOTH, rows, cols), f32)

        @pl.when(place[0] == groups - 1)
        def _():
            force[:, mid - SMOOTH : mid] = jnp.zeros((3, SMOOTH, rows, cols), f32)

    return local_call(kernel, "force", [(3, mid, rows, cols)], 6, [], 600_000_000)


def build_smooth(depth, rows, cols):
    def kernel(force, velocity, padded):
        g_high, g_low = split(gauss_columns(cols))
        g_all = jnp.concatenate(
            [
                jnp.concatenate([g_high, g_low], axis=1),
                jnp.concatenate([g_high, jnp.zeros_like(g_low)], axis=1),
            ],
            axis=0,
        )
        padded[...] = jnp.zeros(padded.shape, f32)

        def finish(i, carry):
            start = i * STEP
            for axis in range(3):
                x = [force[axis, start + k] for k in range(STEP + 2 * SMOOTH)]
                for k in range(STEP):
                    value = GAUSS[0] * x[k + SMOOTH]
                    for d in range(1, SMOOTH + 1):
                        value = value + GAUSS[d] * (x[k + SMOOTH - d] + x[k + SMOOTH + d])
                    padded[axis, k, SMOOTH : SMOOTH + rows] = value
                mixed = GAUSS[0] * padded[axis, :, SMOOTH : SMOOTH + rows]
                for d in range(1, SMOOTH + 1):
                    mixed = mixed + GAUSS[d] * (
                        padded[axis, :, SMOOTH - d : SMOOTH - d + rows]
                        + padded[axis, :, SMOOTH + d : SMOOTH + d + rows]
                    )
                pair = jnp.concatenate(split(flat(mixed)), axis=1)
                done = jnp.dot(pair, g_all, preferred_element_type=f32)
                velocity[axis, pl.ds(start, STEP)] = (done[:, :cols] + done[:, cols:]).reshape(
                    STEP, rows, cols
                )
            return carry

        lax.fori_loop(0, depth // STEP, finish, 0)

    return local_call(
        kernel, "smooth", [(3, depth, rows, cols)], 1,
        [(3, STEP, rows + 2 * SMOOTH, cols)], 600_000_000, scalars=False,
    )


def per_device(template, subjects, shifts, fractions):
    groups = lax.axis_size("gz")
    members = lax.axis_size("subj")
    subject_count, depth, rows, cols = subjects.shape
    share = depth // members
    me = lax.axis_index("subj")
    place = jnp.stack([lax.axis_index("gz"), me]).astype(jnp.int32)

    pieces = template
    for bit in reversed(bits_of(members)):
        pieces = jnp.concatenate([pieces, swap(pieces, "subj", bit)], axis=0)

    def edge(start):
        parts = [shifts[0, :, start : start + EDGE].astype(bf16)]
        parts += [fractions[0, :, start : start + EDGE], subjects[:, start : start + EDGE]]
        return jnp.concatenate(parts, axis=0)

    to_near, to_far = at_ends("gz", edge(0), edge(depth - EDGE))
    near_m, far_m = swap_near(to_near, "gz"), swap_far(to_far, "gz")

    def shares(numbers):
        starts = [mirrored(me ^ number, members) * share for number in numbers]
        return jnp.concatenate(
            [lax.dynamic_slice_in_dim(pieces, start, share, 0) for start in starts], axis=0
        )

    reach = -(-HALO // share)
    low_t = shares(range(reach))[:HALO]
    high_t = shares(range(members - reach, members))[-HALO:]
    to_near, to_far = at_ends("gz", low_t, high_t)
    near_t, far_t = swap_near(to_near, "gz"), swap_far(to_far, "gz")

    image, mean, variance = build_image(depth, rows, cols)(place, near_m, far_m, subjects[0])
    (inner,) = build_inner_warp(depth, rows, cols, members)(place, pieces, shifts[0], fractions[0])
    warped, keep, send = build_outer_warp(depth, rows, cols, members)(
        place, low_t, high_t, near_t, far_t, near_m, far_m, shifts[0], fractions[0], subjects[0], inner
    )
    boxes, slope = build_boxes(depth, rows, cols)(warped, image)
    waiting = {"boxes": boxes}

    def hold(stage, value):
        if stage == 0:
            value, waiting["boxes"] = lax.optimization_barrier((value, waiting["boxes"]))
            (waiting["force"],) = build_force(depth, rows, cols, groups)(
                place, warped, image, mean, variance, waiting["boxes"], slope
            )
        if stage == 1:
            value, waiting["force"] = lax.optimization_barrier((value, waiting["force"]))
        return value

    own_rows = scatter_sum(keep, send, "subj", hold)
    (velocity,) = build_smooth(depth, rows, cols)(waiting["force"])
    template_force = own_rows * (1.0 / math.sqrt(subject_count * members))
    return (velocity[None], template_force)


def solution(mesh):
    placed = (
        P(("gz", "subj"), None, None),
        P("subj", "gz", None, None),
        P("subj", None, "gz", None, None),
        P("subj", None, "gz", None, None),
    )
    return jax.shard_map(
        per_device,
        mesh=mesh,
        in_specs=placed,
        out_specs=(P("subj", None, "gz", None, None), P(("gz", "subj"), None, None)),
        check_vma=False,
    )
```

time: 150 us -> 39.2 us (0.26)
  the two profiles are of different devices: /device:TPU:0 before, /device:TPU:6 now
where the time goes in v2:
time: 39.2 us; the launch traced here: 38.8 us
  starting transfers between devices  11.7 us (30%)
  waiting for transfers between devices  11.7 us (30%)
  Pallas kernels  11.7 us (30%)
  other arithmetic  2.03 us (5%)
  between operations  0.87 us (2%)
  local copies, waits for them, and re-layouts  0.84 us (2%)
    ppermute x6, waiting for transfers between devices, swap(): return lax.ppermute(block, axis, [(i, i ^ bit) for i in range(count)])  11 us
    ppermute x6, starting transfers between devices, swap(): return lax.ppermute(block, axis, [(i, i ^ bit) for i in range(count)])  7.15 us
    ppermute x2, starting transfers between devices, swap_far(): lax.ppermute(block, axis, ups + [(target, source) for source, target in u...  4.45 us
    pallas_call x1, Pallas kernels, per_device(): velocity, = build_smooth(depth, rows, cols)(waiting['force'])  2.94 us
    pallas_call x1, Pallas kernels, per_device(): build_inner_warp(depth, rows, cols, members)  2.45 us
    pallas_call x1, Pallas kernels, per_device(): build_image(depth, rows, cols)(place, near_m, far_m, subjects[0])  1.86 us
    pallas_call x1, Pallas kernels, per_device(): build_outer_warp(depth, rows, cols, members)  1.83 us
    pallas_call x1, Pallas kernels, hold(): build_force(depth, rows, cols, groups)  1.56 us
  transfers between devices with their start and end apart: 10, of which 6 were waited for; matrix products, arithmetic and copies ran while one was open for 6% of the time, Pallas kernels for 25%

profile of v2, /device:TPU:6, one launch (start us, length us, event | category | flops | bytes accessed | tf_op | source)
XLA Modules:
  0.0 38.8 jit_solution(17722160049513642645)
XLA Ops:
  0.6 2.7 %collective-permute-start = (bf16[8,8,128]{2,1,0:T(8,128)(2,1)}, bf16[8,8,128]{2,1,0:T(8,128)(2,1)S(1)}, u32[]{:S(2)}, u32[]{:S(2)}) collective-permute-start(bf16[8,8,128]{2,1,0:T(8,128)(2,1)} %param.4), channel_id=1, source_target_pairs={{0,4},{1,5},{2,6},{3,7},{4,0},{5,1},{6,2},{7,3},{8,12},{9,13},{10,... | collective-permute-start | bytes 49160 | tf_op jit(solution)/shard_map/ppermute | solution.py:29
  3.3 0.7 %fusion.3 = (bf16[1,8,8,128]{3,2,1,0:T(8,128)(2,1)S(1)}, bf16[1,8,8,128]{3,2,1,0:T(8,128)(2,1)S(1)}) fusion(bf16[1,64,8,128]{3,2,1,0:T(8,128)(2,1)} %param.5), kind=kLoop, calls=%fused_computation.29 | loop fusion | bytes 65536 | tf_op jit(solution)/shard_map/slice | solution.py:490
  4.0 1.2 %convert.4 = bf16[1,3,64,8,128]{4,3,2,1,0:T(8,128)(2,1)S(1)} convert(s32[1,3,64,8,128]{4,3,2,1,0:T(8,128)} %param.6) | non-fusion elementwise | flops 196608 | bytes 1179648 | tf_op jit(solution)/shard_map/convert.1
  5.4 0.1 collective-permute-start.5
  5.4 2.5 %collective-permute-start.6 = (bf16[7,8,8,128]{3,2,1,0:T(8,128)(2,1)S(1)}, bf16[7,8,8,128]{3,2,1,0:T(8,128)(2,1)S(1)}, u32[]{:S(2)}, u32[]{:S(2)}) collective-permute-start(bf16[7,8,8,128]{3,2,1,0:T(8,128)(2,1)S(1)} %get-tuple-element.33), channel_id=1, source_target_pairs={{8,16},{16,8},{9,17},{17,9},{10,18},{18,10},{11,19},{19,11},{12,20... | collective-permute-start | bytes 344072 | tf_op jit(solution)/shard_map/ppermute | solution.py:41
  8.0 0.1 pad_add_fusion.place
  8.1 1.6 %collective-permute-start.1 = (bf16[16,8,128]{2,1,0:T(8,128)(2,1)S(1)}, bf16[16,8,128]{2,1,0:T(8,128)(2,1)S(1)}, u32[]{:S(2)}, u32[]{:S(2)}) collective-permute-start(bf16[16,8,128]{2,1,0:T(8,128)(2,1)S(1)} %pad_maximum_fusion.3), channel_id=1, source_target_pairs={{0,2},{1,3},{2,0},{3,1},{4,6},{5,7},{6,4},{7,5},{8,10},{9,11},{10,... | collective-permute-start | bytes 98312 | tf_op jit(solution)/shard_map/ppermute | solution.py:29
  9.7 2.3 %collective-permute-done.1 = bf16[16,8,128]{2,1,0:T(8,128)(2,1)S(1)} collective-permute-done((bf16[16,8,128]{2,1,0:T(8,128)(2,1)S(1)}, bf16[16,8,128]{2,1,0:T(8,128)(2,1)S(1)}, u32[]{:S(2)}, u32[]{:S(2)}) %collective-permute-start.1) | collective-permute-done | bytes 32800 | tf_op jit(solution)/shard_map/ppermute | solution.py:29
  12.1 0.6 %collective-permute-start.2 = (bf16[32,8,128]{2,1,0:T(8,128)(2,1)S(1)}, bf16[32,8,128]{2,1,0:T(8,128)(2,1)S(1)}, u32[]{:S(2)}, u32[]{:S(2)}) collective-permute-start(bf16[32,8,128]{2,1,0:T(8,128)(2,1)S(1)} %pad_maximum_fusion.2), channel_id=1, source_target_pairs={{0,1},{1,0},{2,3},{3,2},{4,5},{5,4},{6,7},{7,6},{8,9},{9,8},{10,11... | collective-permute-start | bytes 196616 | tf_op jit(solution)/shard_map/ppermute | solution.py:29
  12.7 3.7 %collective-permute-done.2 = bf16[32,8,128]{2,1,0:T(8,128)(2,1)S(1)} collective-permute-done((bf16[32,8,128]{2,1,0:T(8,128)(2,1)S(1)}, bf16[32,8,128]{2,1,0:T(8,128)(2,1)S(1)}, u32[]{:S(2)}, u32[]{:S(2)}) %collective-permute-start.2) | collective-permute-done | bytes 65568 | tf_op jit(solution)/shard_map/ppermute | solution.py:29
  16.6 1.9 %collective-permute-start.4 = (bf16[11,8,128]{2,1,0:T(8,128)(2,1)S(1)}, bf16[11,8,128]{2,1,0:T(8,128)(2,1)S(1)}, u32[]{:S(2)}, u32[]{:S(2)}) collective-permute-start(bf16[11,8,128]{2,1,0:T(8,128)(2,1)S(1)} %get-tuple-element.26), channel_id=1, source_target_pairs={{8,16},{16,8},{9,17},{17,9},{10,18},{18,10},{11,19},{19,11},{12,20... | collective-permute-start | bytes 67592 | tf_op jit(solution)/shard_map/ppermute | solution.py:41
  18.5 2.5 %inner_warp.1.inner = f32[48,8,128]{2,1,0:T(8,128)S(1)} custom-call(s32[2]{0:T(128)S(1)} %pad_add_fusion.place, bf16[64,8,128]{2,1,0:T(8,128)(2,1)S(1)} %constant_dynamic-update-slice_fusion.pieces, s32[3,64,8,128]{3,2,1,0:T(8,128)S(1)} %bitcast.27, bf16[3,64,8,128]{3,2,1,0:T(8,128)(2,1)S(1)} %bitcast.29), custom_call_target="tpu_custom_call" | custom-call | flops 1000000000 | bytes 8000000 | tf_op jit(solution)/shard_map/inner_warp/pallas_call | solution.py:509
  21.0 0.7 %collective-permute-done.4.far_t = bf16[11,8,128]{2,1,0:T(8,128)(2,1)S(1)} collective-permute-done((bf16[11,8,128]{2,1,0:T(8,128)(2,1)S(1)}, bf16[11,8,128]{2,1,0:T(8,128)(2,1)S(1)}, u32[]{:S(2)}, u32[]{:S(2)}) %collective-permute-start.4) | collective-permute-done | bytes 22560 | tf_op jit(solution)/shard_map/ppermute | solution.py:41
  21.7 1.8 %outer_warp.1 = (f32[80,8,128]{2,1,0:T(8,128)S(1)}, f32[32,8,128]{2,1,0:T(8,128)S(1)}, f32[32,8,128]{2,1,0:T(8,128)S(1)}) custom-call(s32[2]{0:T(128)S(1)} %pad_add_fusion.place, bf16[11,8,128]{2,1,0:T(8,128)(2,1)S(1)} %get-tuple-element.28.low_t, bf16[11,8,128]{2,1,0:T(8,128)(2,1)S(1)} %get-tuple-element.27.high_t, ...), custom_call_target="tpu_custom_call" | custom-call | flops 600000000 | bytes 8000000 | tf_op jit(solution)/shard_map/outer_warp/pallas_call | solution.py:510
  23.5 0.6 %collective-permute-start.7 = (f32[32,8,128]{2,1,0:T(8,128)S(1)}, f32[32,8,128]{2,1,0:T(8,128)S(1)}, u32[]{:S(2)}, u32[]{:S(2)}) collective-permute-start(f32[32,8,128]{2,1,0:T(8,128)S(1)} %get-tuple-element.15), channel_id=1, source_target_pairs={{0,1},{1,0},{2,3},{3,2},{4,5},{5,4},{6,7},{7,6},{8,9},{9,8},{10,11... | collective-permute-start | bytes 393224 | tf_op jit(solution)/shard_map/ppermute | solution.py:29
  24.1 1.9 %image.1 = (f32[80,8,128]{2,1,0:T(8,128)S(1)}, f32[72,8,128]{2,1,0:T(8,128)S(1)}, f32[72,8,128]{2,1,0:T(8,128)S(1)}) custom-call(s32[2]{0:T(128)S(1)} %pad_add_fusion.place, bf16[7,8,8,128]{3,2,1,0:T(8,128)(2,1)S(1)} %collective-permute-done.5.near_m, bf16[7,8,8,128]{3,2,1,0:T(8,128)(2,1)S(1)} %collective-permute-done.6.far_m, bf16[64,8,128]{2,1,0:T(8,128)(2,1)S(1)} %bitcast.32), custom_call_target="tpu_custom_call" | custom-call | flops 400000000 | bytes 8000000 | tf_op jit(solution)/shard_map/image/pallas_call | solution.py:508
  26.0 1.0 %boxes.1 = (f32[3,80,8,128]{3,2,1,0:T(8,128)S(1)}, f32[80,8,128]{2,1,0:T(8,128)S(1)}) custom-call(f32[80,8,128]{2,1,0:T(8,128)S(1)} %get-tuple-element.16.warped, f32[80,8,128]{2,1,0:T(8,128)S(1)} %get-tuple-element.17.image), custom_call_target="tpu_custom_call" | custom-call | flops 400000000 | bytes 8000000 | tf_op jit(solution)/shard_map/boxes/pallas_call | solution.py:513
  27.0 1.6 %collective-permute-done.7 = f32[32,8,128]{2,1,0:T(8,128)S(1)} collective-permute-done((f32[32,8,128]{2,1,0:T(8,128)S(1)}, f32[32,8,128]{2,1,0:T(8,128)S(1)}, u32[]{:S(2)}, u32[]{:S(2)}) %collective-permute-start.7) | collective-permute-done | bytes 131104 | tf_op jit(solution)/shard_map/ppermute | solution.py:29
  28.6 1.6 %collective-permute-start.8 = (f32[16,8,128]{2,1,0:T(8,128)S(1)}, f32[16,8,128]{2,1,0:T(8,128)S(1)}, u32[]{:S(2)}, u32[]{:S(2)}) collective-permute-start(f32[16,8,128]{2,1,0:T(8,128)S(1)} %bitcast.36), channel_id=1, source_target_pairs={{0,2},{1,3},{2,0},{3,1},{4,6},{5,7},{6,4},{7,5},{8,10},{9,11},{10,... | collective-permute-start | bytes 196616 | tf_op jit(solution)/shard_map/ppermute | solution.py:29
  30.3 1.6 %force.1 = f32[3,72,8,128]{3,2,1,0:T(8,128)S(1)} custom-call(s32[2]{0:T(128)S(1)} %pad_add_fusion.place, f32[80,8,128]{2,1,0:T(8,128)S(1)} %get-tuple-element.16.warped, f32[80,8,128]{2,1,0:T(8,128)S(1)} %get-tuple-element.17.image, f32[72,8,128]{2,1,0:T(8,128)S(1)} %get-tuple-element.20.mean, f32[72,8,128]{2,1,0:T(8,128)S(1)} %get-tuple-element.21.variance, ...), custom_call_target="tpu_custom_call" | custom-call | flops 600000000 | bytes 8000000 | tf_op jit(solution)/shard_map/force/pallas_call | solution.py:519
  31.8 1.5 %collective-permute-done.8 = f32[16,8,128]{2,1,0:T(8,128)S(1)} collective-permute-done((f32[16,8,128]{2,1,0:T(8,128)S(1)}, f32[16,8,128]{2,1,0:T(8,128)S(1)}, u32[]{:S(2)}, u32[]{:S(2)}) %collective-permute-start.8) | collective-permute-done | bytes 65568 | tf_op jit(solution)/shard_map/ppermute | solution.py:29
  33.4 2.9 %smooth.1 = f32[3,64,8,128]{3,2,1,0:T(8,128)} custom-call(f32[3,72,8,128]{3,2,1,0:T(8,128)S(1)} %force.1), custom_call_target="tpu_custom_call" | custom-call | flops 600000000 | bytes 8000000 | tf_op jit(solution)/shard_map/smooth/pallas_call | solution.py:527
  36.3 1.9 %collective-permute-done.9 = f32[8,8,128]{2,1,0:T(8,128)S(1)} collective-permute-done((f32[8,8,128]{2,1,0:T(8,128)S(1)}, f32[8,8,128]{2,1,0:T(8,128)S(1)}, u32[]{:S(2)}, u32[]{:S(2)}) %collective-permute-start.9) | collective-permute-done | bytes 32800 | tf_op jit(solution)/shard_map/ppermute | solution.py:29
  38.2 0.6 %fusion.1 = f32[8,8,128]{2,1,0:T(8,128)} fusion(f32[8,8,128]{2,1,0:T(8,128)S(1)} %collective-permute-done.9, f32[1,2,8,8,128]{4,3,2,1,0:T(8,128)S(1)} %bitcast.35), kind=kLoop, calls=%fused_computation.13 | loop fusion | flops 16384 | bytes 98304 | tf_op jit(solution)/shard_map/mul | solution.py:528
  (29 shorter events, 0.4 us)
Async XLA Ops:
  0.6 7.5 %collective-permute-start = (bf16[8,8,128]{2,1,0:T(8,128)(2,1)}, bf16[8,8,128]{2,1,0:T(8,128)(2,1)S(1)}, u32[]{:S(2)}, u32[]{:S(2)}) collective-permute-start(bf16[8,8,128]{2,1,0:T(8,128)(2,1)} %param.4), channel_id=1, source_target_pairs={{0,4},{1,5},{2,6},{3,7},{4,0},{5,1},{6,2},{7,3},{8,12},{9,13},{10,... | collective-permute-start | bytes 49160 | tf_op jit(solution)/shard_map/ppermute | solution.py:29
  4.0 1.2 %copy-start.1 = (bf16[1,3,64,8,128]{4,3,2,1,0:T(8,128)(2,1)S(1)}, bf16[1,3,64,8,128]{4,3,2,1,0:T(8,128)(2,1)}, u32[]{:S(2)}) copy-start(bf16[1,3,64,8,128]{4,3,2,1,0:T(8,128)(2,1)} %param.7) | copy-start | bytes 1179652
  5.3 2.7 %copy-start.3 = (bf16[8,8,128]{2,1,0:T(8,128)(2,1)S(1)}, bf16[8,8,128]{2,1,0:T(8,128)(2,1)}, u32[]{:S(2)}) copy-start(bf16[8,8,128]{2,1,0:T(8,128)(2,1)} %param.4) | copy-start | bytes 49156
  5.3 13.2 %copy-start = (s32[1,3,64,8,128]{4,3,2,1,0:T(8,128)S(1)}, s32[1,3,64,8,128]{4,3,2,1,0:T(8,128)}, u32[]{:S(2)}) copy-start(s32[1,3,64,8,128]{4,3,2,1,0:T(8,128)} %param.6) | copy-start | bytes 2359300
  5.4 15.6 %collective-permute-start.5 = (bf16[7,8,8,128]{3,2,1,0:T(8,128)(2,1)S(1)}, bf16[7,8,8,128]{3,2,1,0:T(8,128)(2,1)S(1)}, u32[]{:S(2)}, u32[]{:S(2)}) collective-permute-start(bf16[7,8,8,128]{3,2,1,0:T(8,128)(2,1)S(1)} %get-tuple-element.34), channel_id=1, source_target_pairs={{0,8},{8,0},{16,24},{24,16},{1,9},{9,1},{17,25},{25,17},{2,10},{10... | collective-permute-start | bytes 344072 | tf_op jit(solution)/shard_map/ppermute | solution.py:35
  5.4 15.6 %collective-permute-start.6 = (bf16[7,8,8,128]{3,2,1,0:T(8,128)(2,1)S(1)}, bf16[7,8,8,128]{3,2,1,0:T(8,128)(2,1)S(1)}, u32[]{:S(2)}, u32[]{:S(2)}) collective-permute-start(bf16[7,8,8,128]{3,2,1,0:T(8,128)(2,1)S(1)} %get-tuple-element.33), channel_id=1, source_target_pairs={{8,16},{16,8},{9,17},{17,9},{10,18},{18,10},{11,19},{19,11},{12,20... | collective-permute-start | bytes 344072 | tf_op jit(solution)/shard_map/ppermute | solution.py:41
  8.1 4.0 %collective-permute-start.1 = (bf16[16,8,128]{2,1,0:T(8,128)(2,1)S(1)}, bf16[16,8,128]{2,1,0:T(8,128)(2,1)S(1)}, u32[]{:S(2)}, u32[]{:S(2)}) collective-permute-start(bf16[16,8,128]{2,1,0:T(8,128)(2,1)S(1)} %pad_maximum_fusion.3), channel_id=1, source_target_pairs={{0,2},{1,3},{2,0},{3,1},{4,6},{5,7},{6,4},{7,5},{8,10},{9,11},{10,... | collective-permute-start | bytes 98312 | tf_op jit(solution)/shard_map/ppermute | solution.py:29
  12.1 4.3 %collective-permute-start.2 = (bf16[32,8,128]{2,1,0:T(8,128)(2,1)S(1)}, bf16[32,8,128]{2,1,0:T(8,128)(2,1)S(1)}, u32[]{:S(2)}, u32[]{:S(2)}) collective-permute-start(bf16[32,8,128]{2,1,0:T(8,128)(2,1)S(1)} %pad_maximum_fusion.2), channel_id=1, source_target_pairs={{0,1},{1,0},{2,3},{3,2},{4,5},{5,4},{6,7},{7,6},{8,9},{9,8},{10,11... | collective-permute-start | bytes 196616 | tf_op jit(solution)/shard_map/ppermute | solution.py:29
  16.5 4.5 %collective-permute-start.3 = (bf16[11,8,128]{2,1,0:T(8,128)(2,1)S(1)}, bf16[11,8,128]{2,1,0:T(8,128)(2,1)S(1)}, u32[]{:S(2)}, u32[]{:S(2)}) collective-permute-start(bf16[11,8,128]{2,1,0:T(8,128)(2,1)S(1)} %broadcast_select_fusion.3), channel_id=1, source_target_pairs={{0,8},{8,0},{16,24},{24,16},{1,9},{9,1},{17,25},{25,17},{2,10},{10... | collective-permute-start | bytes 67592 | tf_op jit(solution)/shard_map/ppermute | solution.py:35
  16.6 5.1 %collective-permute-start.4 = (bf16[11,8,128]{2,1,0:T(8,128)(2,1)S(1)}, bf16[11,8,128]{2,1,0:T(8,128)(2,1)S(1)}, u32[]{:S(2)}, u32[]{:S(2)}) collective-permute-start(bf16[11,8,128]{2,1,0:T(8,128)(2,1)S(1)} %get-tuple-element.26), channel_id=1, source_target_pairs={{8,16},{16,8},{9,17},{17,9},{10,18},{18,10},{11,19},{19,11},{12,20... | collective-permute-start | bytes 67592 | tf_op jit(solution)/shard_map/ppermute | solution.py:41
  18.5 3.2 %copy-start.2 = (bf16[1,64,8,128]{3,2,1,0:T(8,128)(2,1)S(1)}, bf16[1,64,8,128]{3,2,1,0:T(8,128)(2,1)}, u32[]{:S(2)}) copy-start(bf16[1,64,8,128]{3,2,1,0:T(8,128)(2,1)} %param.5) | copy-start | bytes 393220
  23.5 5.0 %collective-permute-start.7 = (f32[32,8,128]{2,1,0:T(8,128)S(1)}, f32[32,8,128]{2,1,0:T(8,128)S(1)}, u32[]{:S(2)}, u32[]{:S(2)}) collective-permute-start(f32[32,8,128]{2,1,0:T(8,128)S(1)} %get-tuple-element.15), channel_id=1, source_target_pairs={{0,1},{1,0},{2,3},{3,2},{4,5},{5,4},{6,7},{7,6},{8,9},{9,8},{10,11... | collective-permute-start | bytes 393224 | tf_op jit(solution)/shard_map/ppermute | solution.py:29
  28.6 4.7 %collective-permute-start.8 = (f32[16,8,128]{2,1,0:T(8,128)S(1)}, f32[16,8,128]{2,1,0:T(8,128)S(1)}, u32[]{:S(2)}, u32[]{:S(2)}) collective-permute-start(f32[16,8,128]{2,1,0:T(8,128)S(1)} %bitcast.36), channel_id=1, source_target_pairs={{0,2},{1,3},{2,0},{3,1},{4,6},{5,7},{6,4},{7,5},{8,10},{9,11},{10,... | collective-permute-start | bytes 196616 | tf_op jit(solution)/shard_map/ppermute | solution.py:29
  33.3 4.9 %collective-permute-start.9 = (f32[8,8,128]{2,1,0:T(8,128)S(1)}, f32[8,8,128]{2,1,0:T(8,128)S(1)}, u32[]{:S(2)}, u32[]{:S(2)}) collective-permute-start(f32[8,8,128]{2,1,0:T(8,128)S(1)} %slice_bitcast_fusion.4), channel_id=1, source_target_pairs={{0,4},{1,5},{2,6},{3,7},{4,0},{5,1},{6,2},{7,3},{8,12},{9,13},{10,... | collective-permute-start | bytes 98312 | tf_op jit(solution)/shard_map/ppermute | solution.py:29

commit v3 on v2

--- a/solution.py
+++ b/solution.py
@@ -17,6 +17,7 @@
 epsilon = 1e-05
 f32 = jnp.float32
 bf16 = jnp.bfloat16
+PEERS = 4
 VMEM_LIMIT = 48 * 1024 * 1024
 
 raw = [math.exp(-k * k / (2 * sigma * sigma)) for k in range(SMOOTH + 1)]
@@ -37,8 +38,14 @@
 
 def swap_far(block, axis):
     count = lax.axis_size(axis)
-    ups = [(i, i + 1) for i in range(1, count - 1, 2)]
-    return lax.ppermute(block, axis, ups + [(target, source) for source, target in ups])
+    assert count % 2 == 0
+    return lax.ppermute(
+        block, axis, [(i, (i + 1 if i % 2 else i - 1) % count) for i in range(count)]
+    )
+
+
+def has_far(group, groups):
+    return (group != 0) & (group != groups - 1)
 
 
 def bits_of(count):
@@ -48,19 +55,6 @@
 def mirrored(number, count):
     places = count.bit_length() - 1
     return sum(((number >> place) & 1) << (places - 1 - place) for place in range(places))
-
-
-def scatter_sum(keep, send, axis, hold):
-    for stage, bit in enumerate(bits_of(lax.axis_size(axis))):
-        if stage:
-            pairs = keep.reshape((-1, 2, share_of(keep, axis, stage)) + keep.shape[1:])
-            keep, send = [pairs[:, part].reshape((-1,) + keep.shape[1:]) for part in (0, 1)]
-        keep = hold(stage, keep + swap(send, axis, bit))
-    return keep
-
-
-def share_of(keep, axis, stage):
-    return keep.shape[0] * (1 << stage) // lax.axis_size(axis)
 
 
 def at_ends(axis, low, high):
@@ -166,13 +160,64 @@
     ]
 
 
+def place_of_shard(me, shard, members):
+    apart = me ^ shard
+    quarter = members // PEERS
+    return (apart & (PEERS - 1)) * quarter + mirrored(apart // PEERS, quarter)
+
+
+def build_pack(depth, rows, cols, share):
+    def kernel(place, template, shifts, fractions, subjects, near, far, mine, whole, parts, done):
+        odd = place[0] % 2 == 1
+        starts = (0, depth - EDGE)
+        copies = [pltpu.make_async_copy(template, mine, done.at[6])]
+        for end, start in enumerate(starts):
+            at = pl.ds(start, EDGE)
+            copies.append(pltpu.make_async_copy(shifts.at[:, at], whole.at[end], done.at[3 * end]))
+            copies.append(
+                pltpu.make_async_copy(fractions.at[:, at], parts.at[end, 0:3], done.at[3 * end + 1])
+            )
+            copies.append(
+                pltpu.make_async_copy(subjects.at[at], parts.at[end, 3], done.at[3 * end + 2])
+            )
+        for copy in copies:
+            copy.start()
+        for copy in copies:
+            copy.wait()
+        for axis in range(7):
+            if axis < 3:
+                low, high = whole[0, axis].astype(f32), whole[1, axis].astype(f32)
+            else:
+                low, high = parts[0, axis - 3].astype(f32), parts[1, axis - 3].astype(f32)
+            near[axis] = jnp.where(odd, low, high).astype(bf16)
+            far[axis] = jnp.where(odd, high, low).astype(bf16)
+
+    any_spec = pl.BlockSpec(memory_space=pl.ANY)
+    message = jax.ShapeDtypeStruct((7, EDGE, rows, cols), bf16)
+    return pl.pallas_call(
+        kernel,
+        out_shape=[message, message, jax.ShapeDtypeStruct((share, rows, cols), bf16)],
+        in_specs=[SMEM_SPEC] + [any_spec] * 4,
+        out_specs=vmem_specs(3),
+        scratch_shapes=[
+            pltpu.VMEM((2, 3, EDGE, rows, cols), jnp.int32),
+            pltpu.VMEM((2, 4, EDGE, rows, cols), bf16),
+            pltpu.SemaphoreType.DMA((7,)),
+        ],
+        compiler_params=pltpu.CompilerParams(vmem_limit_bytes=VMEM_LIMIT),
+        cost_estimate=pl.CostEstimate(flops=1_000_000, bytes_accessed=2_000_000, transcendentals=0),
+        name="pack",
+    )
+
+
 def build_inner_warp(depth, rows, cols, members):
     share = depth // members
 
     def kernel(place, pieces, shifts, fractions, warped, slab, shifted):
         me = place[1]
+        quarter = members // PEERS
         for k in range(members):
-            shard = me ^ mirrored(k, members)
+            shard = me ^ (k // quarter + PEERS * mirrored(k % quarter, quarter))
             slab[pl.ds(shard * share, share)] = pieces[k * share : (k + 1) * share].astype(f32)
         for start in range(0, depth, depth // 2):
             move_columns(slab, shifted, start, depth // 2)
@@ -190,18 +235,19 @@
     )
 
 
-def build_outer_warp(depth, rows, cols, members):
+def build_outer_warp(depth, rows, cols, members, groups):
     share = depth // members
     ext = depth + 2 * EDGE
     planes = 2 * HALO
 
     def kernel(
         place, low_t, high_t, near_t, far_t, near_m, far_m, shifts, fractions, subjects, inner,
-        warped, keep, send, slab, shifted,
+        warped, keep, send1, send2, send3, slab, shifted,
     ):
         odd = place[0] % 2 == 1
         me = place[1]
-        near, far = near_t[...].astype(f32), far_t[...].astype(f32)
+        inside = has_far(place[0], groups)
+        near, far = near_t[...].astype(f32), jnp.where(inside, far_t[...].astype(f32), 0.0)
         slab[0:HALO] = jnp.where(odd, near, far)
         slab[HALO:planes] = low_t[...].astype(f32)
         slab[planes : planes + HALO] = high_t[...].astype(f32)
@@ -213,17 +259,18 @@
             def edge(low):
                 fields = []
                 for axis in range(6):
-                    one, two = near_m[axis, z].astype(f32), far_m[axis, z].astype(f32)
+                    one = near_m[axis, z].astype(f32)
+                    two = jnp.where(inside, far_m[axis, z].astype(f32), 0.0)
                     fields.append(jnp.where(odd, one, two) if low else jnp.where(odd, two, one))
                 return fields
 
-            inside = depth - EDGE + z
+            last = depth - EDGE + z
             warped[z] = warp_slice(shifted, z + 1, *edge(True))
             warped[z + EDGE] = warp_slice(
                 shifted, z + EDGE + 1, *slice_fields(shifts, fractions, z)
             )
             warped[z + depth] = warp_slice(
-                shifted, planes + z + 1, *slice_fields(shifts, fractions, inside)
+                shifted, planes + z + 1, *slice_fields(shifts, fractions, last)
             )
             warped[z + depth + EDGE] = warp_slice(
                 shifted, planes + z + EDGE + 1, *edge(False)
@@ -234,15 +281,15 @@
 
         for k in range(members):
             shard = me ^ k
-            target = send if k % 2 else keep
+            target = (keep, send1, send2, send3)[k % PEERS]
             start = shard * share
-            target[(k // 2) * share : (k // 2 + 1) * share] = (
+            target[(k // PEERS) * share : (k // PEERS + 1) * share] = (
                 subjects[pl.ds(start, share)].astype(f32) - warped[pl.ds(EDGE + start, share)]
             )
 
-    half = (depth // 2, rows, cols)
+    part = (depth // PEERS, rows, cols)
     return local_call(
-        kernel, "outer_warp", [(ext, rows, cols), half, half], 10,
+        kernel, "outer_warp", [(ext, rows, cols)] + [part] * PEERS, 10,
         [(2 * planes, rows, cols), (TAPS, 2 * planes, rows, cols)], 600_000_000,
     )
 
@@ -316,12 +363,13 @@
     return jnp.dot(pair, twice, preferred_element_type=f32)
 
 
-def build_image(depth, rows, cols):
+def build_image(depth, rows, cols, groups):
     ext, mid = depth + 2 * EDGE, depth + 2 * SMOOTH
 
     def kernel(place, near_m, far_m, subjects, image, mean, variance, boxes):
         odd = place[0] % 2 == 1
-        near, far = near_m[6].astype(f32), far_m[6].astype(f32)
+        near = near_m[6].astype(f32)
+        far = jnp.where(has_far(place[0], groups), far_m[6].astype(f32), 0.0)
         image[0:EDGE] = jnp.where(odd, near, far)
         image[EDGE : EDGE + depth] = subjects[...].astype(f32)
         image[EDGE + depth : ext] = jnp.where(odd, far, near)
@@ -362,10 +410,10 @@
     )
 
 
-def build_boxes(depth, rows, cols):
-    ext = depth + 2 * EDGE
-
-    def kernel(warped, image, boxes, slope):
+def build_force(depth, rows, cols, groups):
+    ext, mid = depth + 2 * EDGE, depth + 2 * SMOOTH
+
+    def kernel(place, warped, image, mean, variance, force, boxes, slope):
         box = band(cols, WIN)
         first = jnp.concatenate([box, column_difference(cols)], axis=1).astype(bf16)
         box = box.astype(bf16)
@@ -382,16 +430,6 @@
             return carry
 
         lax.fori_loop(0, ext // CHUNK, columns, 0)
-
-    return local_call(
-        kernel, "boxes", [(3, ext, rows, cols), (ext, rows, cols)], 2, [], 400_000_000, scalars=False
-    )
-
-
-def build_force(depth, rows, cols, groups):
-    mid = depth + 2 * SMOOTH
-
-    def kernel(place, warped, image, mean, variance, boxes, slope, force):
         row = lax.broadcasted_iota(jnp.int32, (rows, cols), 0)
 
         def local(i, carry):
@@ -428,7 +466,10 @@
         def _():
             force[:, mid - SMOOTH : mid] = jnp.zeros((3, SMOOTH, rows, cols), f32)
 
-    return local_call(kernel, "force", [(3, mid, rows, cols)], 6, [], 600_000_000)
+    return local_call(
+        kernel, "force", [(3, mid, rows, cols)], 4,
+        [(3, ext, rows, cols), (ext, rows, cols)], 1_000_000_000,
+    )
 
 
 def build_smooth(depth, rows, cols):
@@ -478,54 +519,53 @@
     members = lax.axis_size("subj")
     subject_count, depth, rows, cols = subjects.shape
     share = depth // members
+    reach = -(-HALO // share)
     me = lax.axis_index("subj")
     place = jnp.stack([lax.axis_index("gz"), me]).astype(jnp.int32)
-
-    pieces = template
-    for bit in reversed(bits_of(members)):
+    bits = bits_of(members)[2:]
+    subject, shift, fraction = subjects[0], shifts[0], fractions[0]
+
+    arrived = swap(template, "subj", bits[-1])
+    to_near, to_far, mine = build_pack(depth, rows, cols, share)(
+        place, template, shift, fraction, subject
+    )
+    pieces = jnp.concatenate([mine, arrived], axis=0)
+    near_m, far_m = swap_near(to_near, "gz"), swap_far(to_far, "gz")
+    pieces, subject = lax.optimization_barrier((pieces, subject))
+    for bit in bits[-2::-1]:
         pieces = jnp.concatenate([pieces, swap(pieces, "subj", bit)], axis=0)
-
-    def edge(start):
-        parts = [shifts[0, :, start : start + EDGE].astype(bf16)]
-        parts += [fractions[0, :, start : start + EDGE], subjects[:, start : start + EDGE]]
-        return jnp.concatenate(parts, axis=0)
-
-    to_near, to_far = at_ends("gz", edge(0), edge(depth - EDGE))
-    near_m, far_m = swap_near(to_near, "gz"), swap_far(to_far, "gz")
+    pieces = jnp.concatenate(
+        [pieces] + [swap(pieces, "subj", k) for k in range(1, PEERS)], axis=0
+    )
 
     def shares(numbers):
-        starts = [mirrored(me ^ number, members) * share for number in numbers]
+        starts = [place_of_shard(me, number, members) * share for number in numbers]
         return jnp.concatenate(
             [lax.dynamic_slice_in_dim(pieces, start, share, 0) for start in starts], axis=0
         )
 
-    reach = -(-HALO // share)
     low_t = shares(range(reach))[:HALO]
     high_t = shares(range(members - reach, members))[-HALO:]
     to_near, to_far = at_ends("gz", low_t, high_t)
     near_t, far_t = swap_near(to_near, "gz"), swap_far(to_far, "gz")
 
-    image, mean, variance = build_image(depth, rows, cols)(place, near_m, far_m, subjects[0])
-    (inner,) = build_inner_warp(depth, rows, cols, members)(place, pieces, shifts[0], fractions[0])
-    warped, keep, send = build_outer_warp(depth, rows, cols, members)(
-        place, low_t, high_t, near_t, far_t, near_m, far_m, shifts[0], fractions[0], subjects[0], inner
-    )
-    boxes, slope = build_boxes(depth, rows, cols)(warped, image)
-    waiting = {"boxes": boxes}
-
-    def hold(stage, value):
-        if stage == 0:
-            value, waiting["boxes"] = lax.optimization_barrier((value, waiting["boxes"]))
-            (waiting["force"],) = build_force(depth, rows, cols, groups)(
-                place, warped, image, mean, variance, waiting["boxes"], slope
-            )
-        if stage == 1:
-            value, waiting["force"] = lax.optimization_barrier((value, waiting["force"]))
-        return value
-
-    own_rows = scatter_sum(keep, send, "subj", hold)
-    (velocity,) = build_smooth(depth, rows, cols)(waiting["force"])
-    template_force = own_rows * (1.0 / math.sqrt(subject_count * members))
+    (inner,) = build_inner_warp(depth, rows, cols, members)(place, pieces, shift, fraction)
+    warped, keep, *sends = build_outer_warp(depth, rows, cols, members, groups)(
+        place, low_t, high_t, near_t, far_t, near_m, far_m, shift, fraction, subject, inner
+    )
+
+    parts = [swap(send, "subj", k) for k, send in zip(range(1, PEERS), sends)]
+    near_m, far_m, subject, warped = lax.optimization_barrier((near_m, far_m, subject, warped))
+    image, mean, variance = build_image(depth, rows, cols, groups)(place, near_m, far_m, subject)
+    (force,) = build_force(depth, rows, cols, groups)(place, warped, image, mean, variance)
+    *parts, force = lax.optimization_barrier((*parts, force))
+    keep = keep + parts[0] + parts[1] + parts[2]
+    for bit in bits:
+        pairs = keep.reshape((-1, 2, share) + keep.shape[1:])
+        keep, send = [pairs[:, part].reshape((-1,) + keep.shape[1:]) for part in (0, 1)]
+        keep = keep + swap(send, "subj", bit)
+    (velocity,) = build_smooth(depth, rows, cols)(force)
+    template_force = keep * (1.0 / math.sqrt(subject_count * members))
     return (velocity[None], template_force)
 
 

time: 39.2 us -> 36.6 us (0.934)
  the two profiles are of different devices: /device:TPU:6 before, /device:TPU:0 now
where the time goes in v3:
time: 36.6 us; the launch traced here: 36.4 us
  starting transfers between devices  14.2 us (39%)
  Pallas kernels  12.6 us (34%)
  waiting for transfers between devices  4.92 us (13%)
  local copies, waits for them, and re-layouts  3.11 us (8%)
  between operations  0.81 us (2%)
  other arithmetic  0.74 us (2%)
    ppermute x8, starting transfers between devices, swap(): return lax.ppermute(block, axis, [(i, i ^ bit) for i in range(count)])  11.8 us
    ppermute x8, waiting for transfers between devices, swap(): return lax.ppermute(block, axis, [(i, i ^ bit) for i in range(count)])  4.73 us
    unnamed x17, local copies, waits for them, and re-layouts  3.07 us
    pallas_call x1, Pallas kernels, per_device(): velocity, = build_smooth(depth, rows, cols)(force)  2.94 us
    pallas_call x1, Pallas kernels, per_device(): build_force(depth, rows, cols, groups)(place, warped, image, mean, variance)  2.62 us
    pallas_call x1, Pallas kernels, per_device(): build_inner_warp(depth, rows, cols, members)(place, pieces, shift, fraction)  2.45 us
    ppermute x2, starting transfers between devices, swap_far(): lax.ppermute(block, axis, [(i, (i + 1 if i % 2 else i - 1) % count) for i...  2.25 us
    pallas_call x1, Pallas kernels, per_device(): build_image(depth, rows, cols, groups)(place, near_m, far_m, subject)  1.86 us
  transfers between devices with their start and end apart: 12, of which 3 were waited for; matrix products, arithmetic and copies ran while one was open for 0% of the time, Pallas kernels for 29%

profile of v3, /device:TPU:0, one launch (start us, length us, event | category | flops | bytes accessed | tf_op | source)
XLA Modules:
  0.0 36.4 jit_solution(1072670914754597353)
XLA Ops:
  0.6 4.1 %collective-permute-start = (bf16[8,8,128]{2,1,0:T(8,128)(2,1)}, bf16[8,8,128]{2,1,0:T(8,128)(2,1)S(1)}, u32[]{:S(2)}, u32[]{:S(2)}) collective-permute-start(bf16[8,8,128]{2,1,0:T(8,128)(2,1)} %template.1), channel_id=1, source_target_pairs={{0,4},{1,5},{2,6},{3,7},{4,0},{5,1},{6,2},{7,3},{8,12},{9,13},{10,... | collective-permute-start | bytes 49160 | tf_op jit(solution)/shard_map/ppermute | solution.py:30
  4.7 0.1 pad_add_fusion.place
  4.8 1.1 %copy-done = s32[1,3,64,8,128]{4,3,2,1,0:T(8,128)S(1)} copy-done((s32[1,3,64,8,128]{4,3,2,1,0:T(8,128)S(1)}, s32[1,3,64,8,128]{4,3,2,1,0:T(8,128)}, u32[]{:S(2)}) %copy-start) | copy-done | bytes 786456
  6.0 1.0 %copy-done.2 = bf16[1,3,64,8,128]{4,3,2,1,0:T(8,128)(2,1)S(1)} copy-done((bf16[1,3,64,8,128]{4,3,2,1,0:T(8,128)(2,1)S(1)}, bf16[1,3,64,8,128]{4,3,2,1,0:T(8,128)(2,1)}, u32[]{:S(2)}) %copy-start.2) | copy-done | bytes 393240
  7.0 0.9 %copy-done.4 = bf16[1,64,8,128]{3,2,1,0:T(8,128)(2,1)S(1)} copy-done((bf16[1,64,8,128]{3,2,1,0:T(8,128)(2,1)S(1)}, bf16[1,64,8,128]{3,2,1,0:T(8,128)(2,1)}, u32[]{:S(2)}) %copy-start.4) | copy-done | bytes 131096
  7.9 0.8 %pack.1 = (bf16[7,8,8,128]{3,2,1,0:T(8,128)(2,1)S(1)}, bf16[7,8,8,128]{3,2,1,0:T(8,128)(2,1)S(1)}, bf16[8,8,128]{2,1,0:T(8,128)(2,1)S(1)}) custom-call(s32[2]{0:T(128)S(1)} %pad_add_fusion.place, bf16[8,8,128]{2,1,0:T(8,128)(2,1)S(1)} %copy-done.6, s32[3,64,8,128]{3,2,1,0:T(8,128)S(1)} %bitcast.15, bf16[3,64,8,128]{3,2,1,0:T(8,128)(2,1)S(1)} %bitcast.18, ...), custom_call_target="tpu_custom_call" | custom-call | flops 1000000 | bytes 2000000 | tf_op jit(solution)/shard_map/pack/pallas_call | solution.py:529
  8.8 1.6 %collective-permute-start.7 = (bf16[7,8,8,128]{3,2,1,0:T(8,128)(2,1)S(1)}, bf16[7,8,8,128]{3,2,1,0:T(8,128)(2,1)S(1)}, u32[]{:S(2)}, u32[]{:S(2)}) collective-permute-start(bf16[7,8,8,128]{3,2,1,0:T(8,128)(2,1)S(1)} %get-tuple-element.26), channel_id=1, source_target_pairs={{0,24},{8,16},{16,8},{24,0},{1,25},{9,17},{17,9},{25,1},{2,26},{10... | collective-permute-start | bytes 344072 | tf_op jit(solution)/shard_map/ppermute | solution.py:42
  10.4 2.6 %collective-permute-start.3 = (bf16[16,8,128]{2,1,0:T(8,128)(2,1)S(1)}, bf16[16,8,128]{2,1,0:T(8,128)(2,1)S(1)}, u32[]{:S(2)}, u32[]{:S(2)}) collective-permute-start(bf16[16,8,128]{2,1,0:T(8,128)(2,1)S(1)} %pad_maximum_fusion), channel_id=1, source_target_pairs={{0,3},{1,2},{2,1},{3,0},{4,7},{5,6},{6,5},{7,4},{8,11},{9,10},{10,... | collective-permute-start | bytes 98312 | tf_op jit(solution)/shard_map/ppermute | solution.py:30
  13.0 0.4 %collective-permute-start.2 = (bf16[16,8,128]{2,1,0:T(8,128)(2,1)S(1)}, bf16[16,8,128]{2,1,0:T(8,128)(2,1)S(1)}, u32[]{:S(2)}, u32[]{:S(2)}) collective-permute-start(bf16[16,8,128]{2,1,0:T(8,128)(2,1)S(1)} %pad_maximum_fusion), channel_id=1, source_target_pairs={{0,2},{1,3},{2,0},{3,1},{4,6},{5,7},{6,4},{7,5},{8,10},{9,11},{10,... | collective-permute-start | bytes 98312 | tf_op jit(solution)/shard_map/ppermute | solution.py:30
  13.5 0.5 %collective-permute-start.1 = (bf16[16,8,128]{2,1,0:T(8,128)(2,1)S(1)}, bf16[16,8,128]{2,1,0:T(8,128)(2,1)S(1)}, u32[]{:S(2)}, u32[]{:S(2)}) collective-permute-start(bf16[16,8,128]{2,1,0:T(8,128)(2,1)S(1)} %pad_maximum_fusion), channel_id=1, source_target_pairs={{0,1},{1,0},{2,3},{3,2},{4,5},{5,4},{6,7},{7,6},{8,9},{9,8},{10,11... | collective-permute-start | bytes 98312 | tf_op jit(solution)/shard_map/ppermute | solution.py:30
  14.0 3.4 %collective-permute-done.1 = bf16[16,8,128]{2,1,0:T(8,128)(2,1)S(1)} collective-permute-done((bf16[16,8,128]{2,1,0:T(8,128)(2,1)S(1)}, bf16[16,8,128]{2,1,0:T(8,128)(2,1)S(1)}, u32[]{:S(2)}, u32[]{:S(2)}) %collective-permute-start.1) | collective-permute-done | bytes 32800 | tf_op jit(solution)/shard_map/ppermute | solution.py:30
  17.6 0.6 %collective-permute-start.5 = (bf16[11,8,128]{2,1,0:T(8,128)(2,1)S(1)}, bf16[11,8,128]{2,1,0:T(8,128)(2,1)S(1)}, u32[]{:S(2)}, u32[]{:S(2)}) collective-permute-start(bf16[11,8,128]{2,1,0:T(8,128)(2,1)S(1)} %get-tuple-element.44), channel_id=1, source_target_pairs={{0,24},{8,16},{16,8},{24,0},{1,25},{9,17},{17,9},{25,1},{2,26},{10... | collective-permute-start | bytes 67592 | tf_op jit(solution)/shard_map/ppermute | solution.py:42
  18.2 2.4 %inner_warp.1.inner = f32[48,8,128]{2,1,0:T(8,128)S(1)} custom-call(s32[2]{0:T(128)S(1)} %pad_add_fusion.place, bf16[64,8,128]{2,1,0:T(8,128)(2,1)S(1)} %constant_dynamic-update-slice_fusion.pieces, s32[3,64,8,128]{3,2,1,0:T(8,128)S(1)} %bitcast.16, bf16[3,64,8,128]{3,2,1,0:T(8,128)(2,1)S(1)} %bitcast.19), custom_call_target="tpu_custom_call" | custom-call | flops 1000000000 | bytes 8000000 | tf_op jit(solution)/shard_map/inner_warp/pallas_call | solution.py:552
  20.7 0.2 collective-permute-done.5.far_t
  20.9 1.9 %outer_warp.1 = (f32[80,8,128]{2,1,0:T(8,128)S(1)}, f32[16,8,128]{2,1,0:T(8,128)S(1)}, f32[16,8,128]{2,1,0:T(8,128)S(1)}, f32[16,8,128]{2,1,0:T(8,128)S(1)}, f32[16,8,128]{2,1,0:T(8,128)S(1)}) custom-call(s32[2]{0:T(128)S(1)} %pad_add_fusion.place, bf16[11,8,128]{2,1,0:T(8,128)(2,1)S(1)} %get-tuple-element.46.low_t, ...), custom_call_target="tpu_custom_call" | custom-call | flops 600000000 | bytes 8000000 | tf_op jit(solution)/shard_map/outer_warp/pallas_call | solution.py:553
  22.8 0.6 %collective-permute-start.8 = (f32[16,8,128]{2,1,0:T(8,128)S(1)}, f32[16,8,128]{2,1,0:T(8,128)S(1)}, u32[]{:S(2)}, u32[]{:S(2)}) collective-permute-start(f32[16,8,128]{2,1,0:T(8,128)S(1)} %get-tuple-element.28), channel_id=1, source_target_pairs={{0,1},{1,0},{2,3},{3,2},{4,5},{5,4},{6,7},{7,6},{8,9},{9,8},{10,11... | collective-permute-start | bytes 196616 | tf_op jit(solution)/shard_map/ppermute | solution.py:30
  23.3 1.6 %collective-permute-start.9 = (f32[16,8,128]{2,1,0:T(8,128)S(1)}, f32[16,8,128]{2,1,0:T(8,128)S(1)}, u32[]{:S(2)}, u32[]{:S(2)}) collective-permute-start(f32[16,8,128]{2,1,0:T(8,128)S(1)} %get-tuple-element.29), channel_id=1, source_target_pairs={{0,2},{1,3},{2,0},{3,1},{4,6},{5,7},{6,4},{7,5},{8,10},{9,11},{10,... | collective-permute-start | bytes 196616 | tf_op jit(solution)/shard_map/ppermute | solution.py:30
  24.9 1.4 %collective-permute-start.10 = (f32[16,8,128]{2,1,0:T(8,128)S(1)}, f32[16,8,128]{2,1,0:T(8,128)S(1)}, u32[]{:S(2)}, u32[]{:S(2)}) collective-permute-start(f32[16,8,128]{2,1,0:T(8,128)S(1)} %get-tuple-element.30), channel_id=1, source_target_pairs={{0,3},{1,2},{2,1},{3,0},{4,7},{5,6},{6,5},{7,4},{8,11},{9,10},{10,... | collective-permute-start | bytes 196616 | tf_op jit(solution)/shard_map/ppermute | solution.py:30
  26.3 1.9 %image.1 = (f32[80,8,128]{2,1,0:T(8,128)S(1)}, f32[72,8,128]{2,1,0:T(8,128)S(1)}, f32[72,8,128]{2,1,0:T(8,128)S(1)}) custom-call(s32[2]{0:T(128)S(1)} %pad_add_fusion.place, bf16[7,8,8,128]{3,2,1,0:T(8,128)(2,1)S(1)} %collective-permute-done.6.near_m, bf16[7,8,8,128]{3,2,1,0:T(8,128)(2,1)S(1)} %collective-permute-done.7.far_m, bf16[64,8,128]{2,1,0:T(8,128)(2,1)S(1)} %bitcast.23), custom_call_target="tpu_custom_call" | custom-call | flops 400000000 | bytes 8000000 | tf_op jit(solution)/shard_map/image/pallas_call | solution.py:559
  28.2 2.6 %force.1 = f32[3,72,8,128]{3,2,1,0:T(8,128)S(1)} custom-call(s32[2]{0:T(128)S(1)} %pad_add_fusion.place, f32[80,8,128]{2,1,0:T(8,128)S(1)} %get-tuple-element.32.warped, f32[80,8,128]{2,1,0:T(8,128)S(1)} %get-tuple-element.36.image, f32[72,8,128]{2,1,0:T(8,128)S(1)} %get-tuple-element.37.mean, f32[72,8,128]{2,1,0:T(8,128)S(1)} %get-tuple-element.38.variance), custom_call_target="tpu_custom_call" | custom-call | flops 1000000000 | bytes 8000000 | tf_op jit(solution)/shard_map/force/pallas_call | solution.py:560
  30.9 0.6 %collective-permute-start.11 = (f32[8,8,128]{2,1,0:T(8,128)S(1)}, f32[8,8,128]{2,1,0:T(8,128)S(1)}, u32[]{:S(2)}, u32[]{:S(2)}) collective-permute-start(f32[8,8,128]{2,1,0:T(8,128)S(1)} %slice_bitcast_fusion), channel_id=1, source_target_pairs={{0,4},{1,5},{2,6},{3,7},{4,0},{5,1},{6,2},{7,3},{8,12},{9,13},{10,... | collective-permute-start | bytes 98312 | tf_op jit(solution)/shard_map/ppermute | solution.py:30
  31.5 2.9 %smooth.1 = f32[3,64,8,128]{3,2,1,0:T(8,128)} custom-call(f32[3,72,8,128]{3,2,1,0:T(8,128)S(1)} %force.1), custom_call_target="tpu_custom_call" | custom-call | flops 600000000 | bytes 8000000 | tf_op jit(solution)/shard_map/smooth/pallas_call | solution.py:567
  34.5 1.3 %collective-permute-done.11 = f32[8,8,128]{2,1,0:T(8,128)S(1)} collective-permute-done((f32[8,8,128]{2,1,0:T(8,128)S(1)}, f32[8,8,128]{2,1,0:T(8,128)S(1)}, u32[]{:S(2)}, u32[]{:S(2)}) %collective-permute-start.11) | collective-permute-done | bytes 32800 | tf_op jit(solution)/shard_map/ppermute | solution.py:30
  35.8 0.6 %fusion.1 = f32[8,8,128]{2,1,0:T(8,128)} fusion(f32[8,8,128]{2,1,0:T(8,128)S(1)} %collective-permute-done.11, f32[1,2,8,8,128]{4,3,2,1,0:T(8,128)S(1)} %bitcast.25), kind=kLoop, calls=%fused_computation.4 | loop fusion | flops 16384 | bytes 98304 | tf_op jit(solution)/shard_map/mul | solution.py:568
  (32 shorter events, 0.3 us)
Async XLA Ops:
  0.6 4.2 %copy-start.6 = (bf16[8,8,128]{2,1,0:T(8,128)(2,1)S(1)}, bf16[8,8,128]{2,1,0:T(8,128)(2,1)}, u32[]{:S(2)}) copy-start(bf16[8,8,128]{2,1,0:T(8,128)(2,1)} %template.1) | copy-start | bytes 49156
  0.6 9.8 %collective-permute-start = (bf16[8,8,128]{2,1,0:T(8,128)(2,1)}, bf16[8,8,128]{2,1,0:T(8,128)(2,1)S(1)}, u32[]{:S(2)}, u32[]{:S(2)}) collective-permute-start(bf16[8,8,128]{2,1,0:T(8,128)(2,1)} %template.1), channel_id=1, source_target_pairs={{0,4},{1,5},{2,6},{3,7},{4,0},{5,1},{6,2},{7,3},{8,12},{9,13},{10,... | collective-permute-start | bytes 49160 | tf_op jit(solution)/shard_map/ppermute | solution.py:30
  4.8 1.1 %copy-start = (s32[1,3,64,8,128]{4,3,2,1,0:T(8,128)S(1)}, s32[1,3,64,8,128]{4,3,2,1,0:T(8,128)}, u32[]{:S(2)}) copy-start(s32[1,3,64,8,128]{4,3,2,1,0:T(8,128)} %param.6) | copy-start | bytes 2359300
  6.0 1.0 %copy-start.2 = (bf16[1,3,64,8,128]{4,3,2,1,0:T(8,128)(2,1)S(1)}, bf16[1,3,64,8,128]{4,3,2,1,0:T(8,128)(2,1)}, u32[]{:S(2)}) copy-start(bf16[1,3,64,8,128]{4,3,2,1,0:T(8,128)(2,1)} %param.7) | copy-start | bytes 1179652
  6.9 0.9 %copy-start.4 = (bf16[1,64,8,128]{3,2,1,0:T(8,128)(2,1)S(1)}, bf16[1,64,8,128]{3,2,1,0:T(8,128)(2,1)}, u32[]{:S(2)}) copy-start(bf16[1,64,8,128]{3,2,1,0:T(8,128)(2,1)} %param.5) | copy-start | bytes 393220
  7.9 10.4 %copy-start.1 = (s32[1,3,64,8,128]{4,3,2,1,0:T(8,128)S(1)}, s32[1,3,64,8,128]{4,3,2,1,0:T(8,128)}, u32[]{:S(2)}) copy-start(s32[1,3,64,8,128]{4,3,2,1,0:T(8,128)} %param.6) | copy-start | bytes 2359300
  8.7 12.2 %collective-permute-start.6 = (bf16[7,8,8,128]{3,2,1,0:T(8,128)(2,1)S(1)}, bf16[7,8,8,128]{3,2,1,0:T(8,128)(2,1)S(1)}, u32[]{:S(2)}, u32[]{:S(2)}) collective-permute-start(bf16[7,8,8,128]{3,2,1,0:T(8,128)(2,1)S(1)} %get-tuple-element.25), channel_id=1, source_target_pairs={{0,8},{8,0},{16,24},{24,16},{1,9},{9,1},{17,25},{25,17},{2,10},{10... | collective-permute-start | bytes 344072 | tf_op jit(solution)/shard_map/ppermute | solution.py:36
  8.8 12.1 %collective-permute-start.7 = (bf16[7,8,8,128]{3,2,1,0:T(8,128)(2,1)S(1)}, bf16[7,8,8,128]{3,2,1,0:T(8,128)(2,1)S(1)}, u32[]{:S(2)}, u32[]{:S(2)}) collective-permute-start(bf16[7,8,8,128]{3,2,1,0:T(8,128)(2,1)S(1)} %get-tuple-element.26), channel_id=1, source_target_pairs={{0,24},{8,16},{16,8},{24,0},{1,25},{9,17},{17,9},{25,1},{2,26},{10... | collective-permute-start | bytes 344072 | tf_op jit(solution)/shard_map/ppermute | solution.py:42
  10.4 7.8 %copy-start.3 = (bf16[1,3,64,8,128]{4,3,2,1,0:T(8,128)(2,1)S(1)}, bf16[1,3,64,8,128]{4,3,2,1,0:T(8,128)(2,1)}, u32[]{:S(2)}) copy-start(bf16[1,3,64,8,128]{4,3,2,1,0:T(8,128)(2,1)} %param.7) | copy-start | bytes 1179652
  10.4 7.0 %collective-permute-start.3 = (bf16[16,8,128]{2,1,0:T(8,128)(2,1)S(1)}, bf16[16,8,128]{2,1,0:T(8,128)(2,1)S(1)}, u32[]{:S(2)}, u32[]{:S(2)}) collective-permute-start(bf16[16,8,128]{2,1,0:T(8,128)(2,1)S(1)} %pad_maximum_fusion), channel_id=1, source_target_pairs={{0,3},{1,2},{2,1},{3,0},{4,7},{5,6},{6,5},{7,4},{8,11},{9,10},{10,... | collective-permute-start | bytes 98312 | tf_op jit(solution)/shard_map/ppermute | solution.py:30
  13.0 4.4 %collective-permute-start.2 = (bf16[16,8,128]{2,1,0:T(8,128)(2,1)S(1)}, bf16[16,8,128]{2,1,0:T(8,128)(2,1)S(1)}, u32[]{:S(2)}, u32[]{:S(2)}) collective-permute-start(bf16[16,8,128]{2,1,0:T(8,128)(2,1)S(1)} %pad_maximum_fusion), channel_id=1, source_target_pairs={{0,2},{1,3},{2,0},{3,1},{4,6},{5,7},{6,4},{7,5},{8,10},{9,11},{10,... | collective-permute-start | bytes 98312 | tf_op jit(solution)/shard_map/ppermute | solution.py:30
  13.5 3.9 %collective-permute-start.1 = (bf16[16,8,128]{2,1,0:T(8,128)(2,1)S(1)}, bf16[16,8,128]{2,1,0:T(8,128)(2,1)S(1)}, u32[]{:S(2)}, u32[]{:S(2)}) collective-permute-start(bf16[16,8,128]{2,1,0:T(8,128)(2,1)S(1)} %pad_maximum_fusion), channel_id=1, source_target_pairs={{0,1},{1,0},{2,3},{3,2},{4,5},{5,4},{6,7},{7,6},{8,9},{9,8},{10,11... | collective-permute-start | bytes 98312 | tf_op jit(solution)/shard_map/ppermute | solution.py:30
  17.5 3.2 %collective-permute-start.4 = (bf16[11,8,128]{2,1,0:T(8,128)(2,1)S(1)}, bf16[11,8,128]{2,1,0:T(8,128)(2,1)S(1)}, u32[]{:S(2)}, u32[]{:S(2)}) collective-permute-start(bf16[11,8,128]{2,1,0:T(8,128)(2,1)S(1)} %broadcast_select_fusion.1), channel_id=1, source_target_pairs={{0,8},{8,0},{16,24},{24,16},{1,9},{9,1},{17,25},{25,17},{2,10},{10... | collective-permute-start | bytes 67592 | tf_op jit(solution)/shard_map/ppermute | solution.py:36
  17.6 3.3 %copy-start.5 = (bf16[1,64,8,128]{3,2,1,0:T(8,128)(2,1)S(1)}, bf16[1,64,8,128]{3,2,1,0:T(8,128)(2,1)}, u32[]{:S(2)}) copy-start(bf16[1,64,8,128]{3,2,1,0:T(8,128)(2,1)} %param.5) | copy-start | bytes 393220
  17.6 3.3 %collective-permute-start.5 = (bf16[11,8,128]{2,1,0:T(8,128)(2,1)S(1)}, bf16[11,8,128]{2,1,0:T(8,128)(2,1)S(1)}, u32[]{:S(2)}, u32[]{:S(2)}) collective-permute-start(bf16[11,8,128]{2,1,0:T(8,128)(2,1)S(1)} %get-tuple-element.44), channel_id=1, source_target_pairs={{0,24},{8,16},{16,8},{24,0},{1,25},{9,17},{17,9},{25,1},{2,26},{10... | collective-permute-start | bytes 67592 | tf_op jit(solution)/shard_map/ppermute | solution.py:42
  22.8 8.1 %collective-permute-start.8 = (f32[16,8,128]{2,1,0:T(8,128)S(1)}, f32[16,8,128]{2,1,0:T(8,128)S(1)}, u32[]{:S(2)}, u32[]{:S(2)}) collective-permute-start(f32[16,8,128]{2,1,0:T(8,128)S(1)} %get-tuple-element.28), channel_id=1, source_target_pairs={{0,1},{1,0},{2,3},{3,2},{4,5},{5,4},{6,7},{7,6},{8,9},{9,8},{10,11... | collective-permute-start | bytes 196616 | tf_op jit(solution)/shard_map/ppermute | solution.py:30
  23.3 7.5 %collective-permute-start.9 = (f32[16,8,128]{2,1,0:T(8,128)S(1)}, f32[16,8,128]{2,1,0:T(8,128)S(1)}, u32[]{:S(2)}, u32[]{:S(2)}) collective-permute-start(f32[16,8,128]{2,1,0:T(8,128)S(1)} %get-tuple-element.29), channel_id=1, source_target_pairs={{0,2},{1,3},{2,0},{3,1},{4,6},{5,7},{6,4},{7,5},{8,10},{9,11},{10,... | collective-permute-start | bytes 196616 | tf_op jit(solution)/shard_map/ppermute | solution.py:30
  24.9 5.9 %collective-permute-start.10 = (f32[16,8,128]{2,1,0:T(8,128)S(1)}, f32[16,8,128]{2,1,0:T(8,128)S(1)}, u32[]{:S(2)}, u32[]{:S(2)}) collective-permute-start(f32[16,8,128]{2,1,0:T(8,128)S(1)} %get-tuple-element.30), channel_id=1, source_target_pairs={{0,3},{1,2},{2,1},{3,0},{4,7},{5,6},{6,5},{7,4},{8,11},{9,10},{10,... | collective-permute-start | bytes 196616 | tf_op jit(solution)/shard_map/ppermute | solution.py:30
  30.9 4.9 %collective-permute-start.11 = (f32[8,8,128]{2,1,0:T(8,128)S(1)}, f32[8,8,128]{2,1,0:T(8,128)S(1)}, u32[]{:S(2)}, u32[]{:S(2)}) collective-permute-start(f32[8,8,128]{2,1,0:T(8,128)S(1)} %slice_bitcast_fusion), channel_id=1, source_target_pairs={{0,4},{1,5},{2,6},{3,7},{4,0},{5,1},{6,2},{7,3},{8,12},{9,13},{10,... | collective-permute-start | bytes 98312 | tf_op jit(solution)/shard_map/ppermute | solution.py:30

commit v4 on v3

--- a/solution.py
+++ b/solution.py
@@ -138,14 +138,11 @@
     return [pl.BlockSpec(memory_space=pltpu.VMEM)] * count
 
 
-SMEM_SPEC = pl.BlockSpec(memory_space=pltpu.SMEM)
-
-
-def local_call(kernel, name, outs, inputs, scratch, flops, scalars=True):
+def local_call(kernel, name, outs, inputs, scratch, flops):
     return pl.pallas_call(
         kernel,
         out_shape=[jax.ShapeDtypeStruct(shape, f32) for shape in outs],
-        in_specs=([SMEM_SPEC] if scalars else []) + vmem_specs(inputs),
+        in_specs=vmem_specs(inputs),
         out_specs=vmem_specs(len(outs)),
         scratch_shapes=[pltpu.VMEM(shape, f32) for shape in scratch],
         compiler_params=pltpu.CompilerParams(vmem_limit_bytes=VMEM_LIMIT),
@@ -167,8 +164,8 @@
 
 
 def build_pack(depth, rows, cols, share):
-    def kernel(place, template, shifts, fractions, subjects, near, far, mine, whole, parts, done):
-        odd = place[0] % 2 == 1
+    def kernel(template, shifts, fractions, subjects, near, far, mine, whole, parts, done):
+        odd = lax.axis_index("gz") % 2 == 1
         starts = (0, depth - EDGE)
         copies = [pltpu.make_async_copy(template, mine, done.at[6])]
         for end, start in enumerate(starts):
@@ -197,7 +194,7 @@
     return pl.pallas_call(
         kernel,
         out_shape=[message, message, jax.ShapeDtypeStruct((share, rows, cols), bf16)],
-        in_specs=[SMEM_SPEC] + [any_spec] * 4,
+        in_specs=[any_spec] * 4,
         out_specs=vmem_specs(3),
         scratch_shapes=[
             pltpu.VMEM((2, 3, EDGE, rows, cols), jnp.int32),
@@ -213,8 +210,8 @@
 def build_inner_warp(depth, rows, cols, members):
     share = depth // members
 
-    def kernel(place, pieces, shifts, fractions, warped, slab, shifted):
-        me = place[1]
+    def kernel(pieces, shifts, fractions, warped, slab, shifted):
+        me = lax.axis_index("subj")
         quarter = members // PEERS
         for k in range(members):
             shard = me ^ (k // quarter + PEERS * mirrored(k % quarter, quarter))
@@ -241,12 +238,12 @@
     planes = 2 * HALO
 
     def kernel(
-        place, low_t, high_t, near_t, far_t, near_m, far_m, shifts, fractions, subjects, inner,
+        low_t, high_t, near_t, far_t, near_m, far_m, shifts, fractions, subjects, inner,
         warped, keep, send1, send2, send3, slab, shifted,
     ):
-        odd = place[0] % 2 == 1
-        me = place[1]
-        inside = has_far(place[0], groups)
+        odd = lax.axis_index("gz") % 2 == 1
+        me = lax.axis_index("subj")
+        inside = has_far(lax.axis_index("gz"), groups)
         near, far = near_t[...].astype(f32), jnp.where(inside, far_t[...].astype(f32), 0.0)
         slab[0:HALO] = jnp.where(odd, near, far)
         slab[HALO:planes] = low_t[...].astype(f32)
@@ -366,10 +363,10 @@
 def build_image(depth, rows, cols, groups):
     ext, mid = depth + 2 * EDGE, depth + 2 * SMOOTH
 
-    def kernel(place, near_m, far_m, subjects, image, mean, variance, boxes):
-        odd = place[0] % 2 == 1
+    def kernel(near_m, far_m, subjects, image, mean, variance, boxes):
+        odd = lax.axis_index("gz") % 2 == 1
         near = near_m[6].astype(f32)
-        far = jnp.where(has_far(place[0], groups), far_m[6].astype(f32), 0.0)
+        far = jnp.where(has_far(lax.axis_index("gz"), groups), far_m[6].astype(f32), 0.0)
         image[0:EDGE] = jnp.where(odd, near, far)
         image[EDGE : EDGE + depth] = subjects[...].astype(f32)
         image[EDGE + depth : ext] = jnp.where(odd, far, near)
@@ -413,7 +410,7 @@
 def build_force(depth, rows, cols, groups):
     ext, mid = depth + 2 * EDGE, depth + 2 * SMOOTH
 
-    def kernel(place, warped, image, mean, variance, force, boxes, slope):
+    def kernel(warped, image, mean, variance, force, boxes, slope):
         box = band(cols, WIN)
         first = jnp.concatenate([box, column_difference(cols)], axis=1).astype(bf16)
         box = box.astype(bf16)
@@ -458,11 +455,11 @@
 
         lax.fori_loop(0, mid // STEP, local, 0)
 
-        @pl.when(place[0] == 0)
+        @pl.when(lax.axis_index("gz") == 0)
         def _():
             force[:, 0:SMOOTH] = jnp.zeros((3, SMOOTH, rows, cols), f32)
 
-        @pl.when(place[0] == groups - 1)
+        @pl.when(lax.axis_index("gz") == groups - 1)
         def _():
             force[:, mid - SMOOTH : mid] = jnp.zeros((3, SMOOTH, rows, cols), f32)
 
@@ -510,7 +507,7 @@
 
     return local_call(
         kernel, "smooth", [(3, depth, rows, cols)], 1,
-        [(3, STEP, rows + 2 * SMOOTH, cols)], 600_000_000, scalars=False,
+        [(3, STEP, rows + 2 * SMOOTH, cols)], 600_000_000,
     )
 
 
@@ -521,17 +518,16 @@
     share = depth // members
     reach = -(-HALO // share)
     me = lax.axis_index("subj")
-    place = jnp.stack([lax.axis_index("gz"), me]).astype(jnp.int32)
     bits = bits_of(members)[2:]
     subject, shift, fraction = subjects[0], shifts[0], fractions[0]
 
     arrived = swap(template, "subj", bits[-1])
     to_near, to_far, mine = build_pack(depth, rows, cols, share)(
-        place, template, shift, fraction, subject
+        template, shift, fraction, subject
     )
     pieces = jnp.concatenate([mine, arrived], axis=0)
+    pieces, to_near, to_far = lax.optimization_barrier((pieces, to_near, to_far))
     near_m, far_m = swap_near(to_near, "gz"), swap_far(to_far, "gz")
-    pieces, subject = lax.optimization_barrier((pieces, subject))
     for bit in bits[-2::-1]:
         pieces = jnp.concatenate([pieces, swap(pieces, "subj", bit)], axis=0)
     pieces = jnp.concatenate(
@@ -549,15 +545,15 @@
     to_near, to_far = at_ends("gz", low_t, high_t)
     near_t, far_t = swap_near(to_near, "gz"), swap_far(to_far, "gz")
 
-    (inner,) = build_inner_warp(depth, rows, cols, members)(place, pieces, shift, fraction)
+    (inner,) = build_inner_warp(depth, rows, cols, members)(pieces, shift, fraction)
     warped, keep, *sends = build_outer_warp(depth, rows, cols, members, groups)(
-        place, low_t, high_t, near_t, far_t, near_m, far_m, shift, fraction, subject, inner
+        low_t, high_t, near_t, far_t, near_m, far_m, shift, fraction, subject, inner
     )
 
     parts = [swap(send, "subj", k) for k, send in zip(range(1, PEERS), sends)]
     near_m, far_m, subject, warped = lax.optimization_barrier((near_m, far_m, subject, warped))
-    image, mean, variance = build_image(depth, rows, cols, groups)(place, near_m, far_m, subject)
-    (force,) = build_force(depth, rows, cols, groups)(place, warped, image, mean, variance)
+    image, mean, variance = build_image(depth, rows, cols, groups)(near_m, far_m, subject)
+    (force,) = build_force(depth, rows, cols, groups)(warped, image, mean, variance)
     *parts, force = lax.optimization_barrier((*parts, force))
     keep = keep + parts[0] + parts[1] + parts[2]
     for bit in bits:

time: 36.6 us -> 33.1 us (0.904)
  Pallas kernels: 12.6 us -> 9.81 us
  waiting for transfers between devices: 4.92 us -> 2.41 us
  starting transfers between devices: 14.2 us -> 16.2 us
    ppermute x8, waiting for transfers between devices: 4.73 us -> 2.4 us  [swap(): return lax.ppermute(block, axis, [(i, i ^ bit) for i in range(count)])]
    pallas_call x4, Pallas kernels: 7.78 us -> 5.58 us  [the longest x1 2.07 us: per_device(): build_force(depth, rows, cols, groups)(warped, image, mean, variance)]
    ppermute x8, starting transfers between devices: 11.8 us -> 12.9 us  [swap(): return lax.ppermute(block, axis, [(i, i ^ bit) for i in range(count)])]
    ppermute x2, starting transfers between devices: 2.25 us -> 3.21 us  [swap_far(): lax.ppermute(block, axis, [(i, (i + 1 if i % 2 else i - 1) % count) for i...]
    pallas_call x1, Pallas kernels: 1.85 us -> 1.31 us  [per_device(): build_outer_warp(depth, rows, cols, members, groups)]
    unnamed x17 -> x15, local copies, waits for them, and re-layouts: 3.07 us -> 2.91 us
  transfers between devices with their start and end apart: 12 -> 12, of which waited for: 3 -> 3; matrix products, arithmetic and copies ran while one was open for 0% -> 0% of each run, Pallas kernels for 29% -> 26%
where the time goes in v4:
time: 33.1 us; the launch traced here: 32.9 us
  starting transfers between devices  16.2 us (49%)
  Pallas kernels  9.81 us (30%)
  local copies, waits for them, and re-layouts  2.95 us (9%)
  waiting for transfers between devices  2.41 us (7%)
  between operations  0.82 us (2%)
  other arithmetic  0.67 us (2%)
    ppermute x8, starting transfers between devices, swap(): return lax.ppermute(block, axis, [(i, i ^ bit) for i in range(count)])  12.9 us
    ppermute x2, starting transfers between devices, swap_far(): lax.ppermute(block, axis, [(i, (i + 1 if i % 2 else i - 1) % count) for i...  3.21 us
    pallas_call x1, Pallas kernels, per_device(): velocity, = build_smooth(depth, rows, cols)(force)  2.91 us
    unnamed x15, local copies, waits for them, and re-layouts  2.91 us
    ppermute x8, waiting for transfers between devices, swap(): return lax.ppermute(block, axis, [(i, i ^ bit) for i in range(count)])  2.4 us
    pallas_call x1, Pallas kernels, per_device(): build_force(depth, rows, cols, groups)(warped, image, mean, variance)  2.07 us
    pallas_call x1, Pallas kernels, per_device(): build_inner_warp(depth, rows, cols, members)(pieces, shift, fraction)  1.91 us
    pallas_call x1, Pallas kernels, per_device(): build_image(depth, rows, cols, groups)(near_m, far_m, subject)  1.32 us
  transfers between devices with their start and end apart: 12, of which 3 were waited for; matrix products, arithmetic and copies ran while one was open for 0% of the time, Pallas kernels for 26%

profile of v4, /device:TPU:0, one launch (start us, length us, event | category | flops | bytes accessed | tf_op | source)
XLA Modules:
  0.0 32.9 jit_solution(15603301089936722564)
XLA Ops:
  0.6 4.1 %collective-permute-start = (bf16[8,8,128]{2,1,0:T(8,128)(2,1)}, bf16[8,8,128]{2,1,0:T(8,128)(2,1)S(1)}, u32[]{:S(2)}, u32[]{:S(2)}) collective-permute-start(bf16[8,8,128]{2,1,0:T(8,128)(2,1)} %template.1), channel_id=1, source_target_pairs={{0,4},{1,5},{2,6},{3,7},{4,0},{5,1},{6,2},{7,3},{8,12},{9,13},{10,... | collective-permute-start | bytes 49160 | tf_op jit(solution)/shard_map/ppermute | solution.py:30
  4.7 0.7 %copy-done.5 = bf16[8,8,128]{2,1,0:T(8,128)(2,1)S(1)} copy-done((bf16[8,8,128]{2,1,0:T(8,128)(2,1)S(1)}, bf16[8,8,128]{2,1,0:T(8,128)(2,1)}, u32[]{:S(2)}) %copy-start.5) | copy-done | bytes 16408
  5.5 1.1 %copy-done = s32[1,3,64,8,128]{4,3,2,1,0:T(8,128)S(1)} copy-done((s32[1,3,64,8,128]{4,3,2,1,0:T(8,128)S(1)}, s32[1,3,64,8,128]{4,3,2,1,0:T(8,128)}, u32[]{:S(2)}) %copy-start) | copy-done | bytes 786456
  6.6 1.0 %copy-done.2 = bf16[1,3,64,8,128]{4,3,2,1,0:T(8,128)(2,1)S(1)} copy-done((bf16[1,3,64,8,128]{4,3,2,1,0:T(8,128)(2,1)S(1)}, bf16[1,3,64,8,128]{4,3,2,1,0:T(8,128)(2,1)}, u32[]{:S(2)}) %copy-start.2) | copy-done | bytes 393240
  7.6 0.3 pack.1
  8.0 2.6 %collective-permute-start.3 = (bf16[16,8,128]{2,1,0:T(8,128)(2,1)S(1)}, bf16[16,8,128]{2,1,0:T(8,128)(2,1)S(1)}, u32[]{:S(2)}, u32[]{:S(2)}) collective-permute-start(bf16[16,8,128]{2,1,0:T(8,128)(2,1)S(1)} %pad_maximum_fusion), channel_id=1, source_target_pairs={{0,3},{1,2},{2,1},{3,0},{4,7},{5,6},{6,5},{7,4},{8,11},{9,10},{10,... | collective-permute-start | bytes 98312 | tf_op jit(solution)/shard_map/ppermute | solution.py:30
  10.5 0.4 %collective-permute-start.2 = (bf16[16,8,128]{2,1,0:T(8,128)(2,1)S(1)}, bf16[16,8,128]{2,1,0:T(8,128)(2,1)S(1)}, u32[]{:S(2)}, u32[]{:S(2)}) collective-permute-start(bf16[16,8,128]{2,1,0:T(8,128)(2,1)S(1)} %pad_maximum_fusion), channel_id=1, source_target_pairs={{0,2},{1,3},{2,0},{3,1},{4,6},{5,7},{6,4},{7,5},{8,10},{9,11},{10,... | collective-permute-start | bytes 98312 | tf_op jit(solution)/shard_map/ppermute | solution.py:30
  11.0 0.5 %collective-permute-start.1 = (bf16[16,8,128]{2,1,0:T(8,128)(2,1)S(1)}, bf16[16,8,128]{2,1,0:T(8,128)(2,1)S(1)}, u32[]{:S(2)}, u32[]{:S(2)}) collective-permute-start(bf16[16,8,128]{2,1,0:T(8,128)(2,1)S(1)} %pad_maximum_fusion), channel_id=1, source_target_pairs={{0,1},{1,0},{2,3},{3,2},{4,5},{5,4},{6,7},{7,6},{8,9},{9,8},{10,11... | collective-permute-start | bytes 98312 | tf_op jit(solution)/shard_map/ppermute | solution.py:30
  11.5 1.6 %collective-permute-start.7 = (bf16[7,8,8,128]{3,2,1,0:T(8,128)(2,1)S(1)}, bf16[7,8,8,128]{3,2,1,0:T(8,128)(2,1)S(1)}, u32[]{:S(2)}, u32[]{:S(2)}) collective-permute-start(bf16[7,8,8,128]{3,2,1,0:T(8,128)(2,1)S(1)} %get-tuple-element.29), channel_id=1, source_target_pairs={{0,24},{8,16},{16,8},{24,0},{1,25},{9,17},{17,9},{25,1},{2,26},{10... | collective-permute-start | bytes 344072 | tf_op jit(solution)/shard_map/ppermute | solution.py:42
  13.1 1.8 %collective-permute-done.1 = bf16[16,8,128]{2,1,0:T(8,128)(2,1)S(1)} collective-permute-done((bf16[16,8,128]{2,1,0:T(8,128)(2,1)S(1)}, bf16[16,8,128]{2,1,0:T(8,128)(2,1)S(1)}, u32[]{:S(2)}, u32[]{:S(2)}) %collective-permute-start.1) | collective-permute-done | bytes 32800 | tf_op jit(solution)/shard_map/ppermute | solution.py:30
  15.0 0.1 collective-permute-start.4
  15.1 1.6 %collective-permute-start.5 = (bf16[11,8,128]{2,1,0:T(8,128)(2,1)S(1)}, bf16[11,8,128]{2,1,0:T(8,128)(2,1)S(1)}, u32[]{:S(2)}, u32[]{:S(2)}) collective-permute-start(bf16[11,8,128]{2,1,0:T(8,128)(2,1)S(1)} %get-tuple-element.46), channel_id=1, source_target_pairs={{0,24},{8,16},{16,8},{24,0},{1,25},{9,17},{17,9},{25,1},{2,26},{10... | collective-permute-start | bytes 67592 | tf_op jit(solution)/shard_map/ppermute | solution.py:42
  16.7 1.9 %inner_warp.1.inner = f32[48,8,128]{2,1,0:T(8,128)S(1)} custom-call(bf16[64,8,128]{2,1,0:T(8,128)(2,1)S(1)} %constant_dynamic-update-slice_fusion.pieces, s32[3,64,8,128]{3,2,1,0:T(8,128)S(1)} %bitcast.14, bf16[3,64,8,128]{3,2,1,0:T(8,128)(2,1)S(1)} %bitcast.17), custom_call_target="tpu_custom_call" | custom-call | flops 1000000000 | bytes 8000000 | tf_op jit(solution)/shard_map/inner_warp/pallas_call | solution.py:548
  18.7 1.3 %outer_warp.1 = (f32[80,8,128]{2,1,0:T(8,128)S(1)}, f32[16,8,128]{2,1,0:T(8,128)S(1)}, f32[16,8,128]{2,1,0:T(8,128)S(1)}, f32[16,8,128]{2,1,0:T(8,128)S(1)}, f32[16,8,128]{2,1,0:T(8,128)S(1)}) custom-call(bf16[11,8,128]{2,1,0:T(8,128)(2,1)S(1)} %get-tuple-element.48.low_t, bf16[11,8,128]{2,1,0:T(8,128)(2,1)S(1)} %get-tuple-element.47.high_t, ...), custom_call_target="tpu_custom_call" | custom-call | flops 600000000 | bytes 8000000 | tf_op jit(solution)/shard_map/outer_warp/pallas_call | solution.py:549
  20.0 0.6 %collective-permute-start.8 = (f32[16,8,128]{2,1,0:T(8,128)S(1)}, f32[16,8,128]{2,1,0:T(8,128)S(1)}, u32[]{:S(2)}, u32[]{:S(2)}) collective-permute-start(f32[16,8,128]{2,1,0:T(8,128)S(1)} %get-tuple-element.30), channel_id=1, source_target_pairs={{0,1},{1,0},{2,3},{3,2},{4,5},{5,4},{6,7},{7,6},{8,9},{9,8},{10,11... | collective-permute-start | bytes 196616 | tf_op jit(solution)/shard_map/ppermute | solution.py:30
  20.6 1.6 %collective-permute-start.9 = (f32[16,8,128]{2,1,0:T(8,128)S(1)}, f32[16,8,128]{2,1,0:T(8,128)S(1)}, u32[]{:S(2)}, u32[]{:S(2)}) collective-permute-start(f32[16,8,128]{2,1,0:T(8,128)S(1)} %get-tuple-element.31), channel_id=1, source_target_pairs={{0,2},{1,3},{2,0},{3,1},{4,6},{5,7},{6,4},{7,5},{8,10},{9,11},{10,... | collective-permute-start | bytes 196616 | tf_op jit(solution)/shard_map/ppermute | solution.py:30
  22.2 1.4 %collective-permute-start.10 = (f32[16,8,128]{2,1,0:T(8,128)S(1)}, f32[16,8,128]{2,1,0:T(8,128)S(1)}, u32[]{:S(2)}, u32[]{:S(2)}) collective-permute-start(f32[16,8,128]{2,1,0:T(8,128)S(1)} %get-tuple-element.32), channel_id=1, source_target_pairs={{0,3},{1,2},{2,1},{3,0},{4,7},{5,6},{6,5},{7,4},{8,11},{9,10},{10,... | collective-permute-start | bytes 196616 | tf_op jit(solution)/shard_map/ppermute | solution.py:30
  23.6 1.3 %image.1 = (f32[80,8,128]{2,1,0:T(8,128)S(1)}, f32[72,8,128]{2,1,0:T(8,128)S(1)}, f32[72,8,128]{2,1,0:T(8,128)S(1)}) custom-call(bf16[7,8,8,128]{3,2,1,0:T(8,128)(2,1)S(1)} %collective-permute-done.6.near_m, bf16[7,8,8,128]{3,2,1,0:T(8,128)(2,1)S(1)} %collective-permute-done.7.far_m, bf16[64,8,128]{2,1,0:T(8,128)(2,1)S(1)} %bitcast.21), custom_call_target="tpu_custom_call" | custom-call | flops 400000000 | bytes 8000000 | tf_op jit(solution)/shard_map/image/pallas_call | solution.py:555
  24.9 2.1 %force.1 = f32[3,72,8,128]{3,2,1,0:T(8,128)S(1)} custom-call(f32[80,8,128]{2,1,0:T(8,128)S(1)} %get-tuple-element.34.warped, f32[80,8,128]{2,1,0:T(8,128)S(1)} %get-tuple-element.38.image, f32[72,8,128]{2,1,0:T(8,128)S(1)} %get-tuple-element.39.mean, f32[72,8,128]{2,1,0:T(8,128)S(1)} %get-tuple-element.40.variance), custom_call_target="tpu_custom_call" | custom-call | flops 1000000000 | bytes 8000000 | tf_op jit(solution)/shard_map/force/pallas_call | solution.py:556
  27.0 0.3 %collective-permute-done.10 = f32[16,8,128]{2,1,0:T(8,128)S(1)} collective-permute-done((f32[16,8,128]{2,1,0:T(8,128)S(1)}, f32[16,8,128]{2,1,0:T(8,128)S(1)}, u32[]{:S(2)}, u32[]{:S(2)}) %collective-permute-start.10) | collective-permute-done | bytes 65568 | tf_op jit(solution)/shard_map/ppermute | solution.py:30
  27.4 1.7 %collective-permute-start.11 = (f32[8,8,128]{2,1,0:T(8,128)S(1)}, f32[8,8,128]{2,1,0:T(8,128)S(1)}, u32[]{:S(2)}, u32[]{:S(2)}) collective-permute-start(f32[8,8,128]{2,1,0:T(8,128)S(1)} %slice_bitcast_fusion), channel_id=1, source_target_pairs={{0,4},{1,5},{2,6},{3,7},{4,0},{5,1},{6,2},{7,3},{8,12},{9,13},{10,... | collective-permute-start | bytes 98312 | tf_op jit(solution)/shard_map/ppermute | solution.py:30
  29.1 2.9 %smooth.1 = f32[3,64,8,128]{3,2,1,0:T(8,128)} custom-call(f32[3,72,8,128]{3,2,1,0:T(8,128)S(1)} %force.1), custom_call_target="tpu_custom_call" | custom-call | flops 600000000 | bytes 8000000 | tf_op jit(solution)/shard_map/smooth/pallas_call | solution.py:563
  32.0 0.3 collective-permute-done.11
  32.2 0.6 %fusion.1 = f32[8,8,128]{2,1,0:T(8,128)} fusion(f32[8,8,128]{2,1,0:T(8,128)S(1)} %collective-permute-done.11, f32[1,2,8,8,128]{4,3,2,1,0:T(8,128)S(1)} %bitcast.23), kind=kLoop, calls=%fused_computation.4 | loop fusion | flops 16384 | bytes 98304 | tf_op jit(solution)/shard_map/mul | solution.py:564
  (29 shorter events, 0.1 us)
Async XLA Ops:
  0.6 4.1 %copy-start.4 = (bf16[1,64,8,128]{3,2,1,0:T(8,128)(2,1)S(1)}, bf16[1,64,8,128]{3,2,1,0:T(8,128)(2,1)}, u32[]{:S(2)}) copy-start(bf16[1,64,8,128]{3,2,1,0:T(8,128)(2,1)} %param.5) | copy-start | bytes 393220
  0.6 7.3 %collective-permute-start = (bf16[8,8,128]{2,1,0:T(8,128)(2,1)}, bf16[8,8,128]{2,1,0:T(8,128)(2,1)S(1)}, u32[]{:S(2)}, u32[]{:S(2)}) collective-permute-start(bf16[8,8,128]{2,1,0:T(8,128)(2,1)} %template.1), channel_id=1, source_target_pairs={{0,4},{1,5},{2,6},{3,7},{4,0},{5,1},{6,2},{7,3},{8,12},{9,13},{10,... | collective-permute-start | bytes 49160 | tf_op jit(solution)/shard_map/ppermute | solution.py:30
  4.7 0.8 %copy-start.5 = (bf16[8,8,128]{2,1,0:T(8,128)(2,1)S(1)}, bf16[8,8,128]{2,1,0:T(8,128)(2,1)}, u32[]{:S(2)}) copy-start(bf16[8,8,128]{2,1,0:T(8,128)(2,1)} %template.1) | copy-start | bytes 49156
  5.5 1.1 %copy-start = (s32[1,3,64,8,128]{4,3,2,1,0:T(8,128)S(1)}, s32[1,3,64,8,128]{4,3,2,1,0:T(8,128)}, u32[]{:S(2)}) copy-start(s32[1,3,64,8,128]{4,3,2,1,0:T(8,128)} %param.6) | copy-start | bytes 2359300
  6.6 1.0 %copy-start.2 = (bf16[1,3,64,8,128]{4,3,2,1,0:T(8,128)(2,1)S(1)}, bf16[1,3,64,8,128]{4,3,2,1,0:T(8,128)(2,1)}, u32[]{:S(2)}) copy-start(bf16[1,3,64,8,128]{4,3,2,1,0:T(8,128)(2,1)} %param.7) | copy-start | bytes 1179652
  7.6 9.1 %copy-start.1 = (s32[1,3,64,8,128]{4,3,2,1,0:T(8,128)S(1)}, s32[1,3,64,8,128]{4,3,2,1,0:T(8,128)}, u32[]{:S(2)}) copy-start(s32[1,3,64,8,128]{4,3,2,1,0:T(8,128)} %param.6) | copy-start | bytes 2359300
  7.9 8.8 %copy-start.3 = (bf16[1,3,64,8,128]{4,3,2,1,0:T(8,128)(2,1)S(1)}, bf16[1,3,64,8,128]{4,3,2,1,0:T(8,128)(2,1)}, u32[]{:S(2)}) copy-start(bf16[1,3,64,8,128]{4,3,2,1,0:T(8,128)(2,1)} %param.7) | copy-start | bytes 1179652
  8.0 7.0 %collective-permute-start.3 = (bf16[16,8,128]{2,1,0:T(8,128)(2,1)S(1)}, bf16[16,8,128]{2,1,0:T(8,128)(2,1)S(1)}, u32[]{:S(2)}, u32[]{:S(2)}) collective-permute-start(bf16[16,8,128]{2,1,0:T(8,128)(2,1)S(1)} %pad_maximum_fusion), channel_id=1, source_target_pairs={{0,3},{1,2},{2,1},{3,0},{4,7},{5,6},{6,5},{7,4},{8,11},{9,10},{10,... | collective-permute-start | bytes 98312 | tf_op jit(solution)/shard_map/ppermute | solution.py:30
  10.5 4.4 %collective-permute-start.2 = (bf16[16,8,128]{2,1,0:T(8,128)(2,1)S(1)}, bf16[16,8,128]{2,1,0:T(8,128)(2,1)S(1)}, u32[]{:S(2)}, u32[]{:S(2)}) collective-permute-start(bf16[16,8,128]{2,1,0:T(8,128)(2,1)S(1)} %pad_maximum_fusion), channel_id=1, source_target_pairs={{0,2},{1,3},{2,0},{3,1},{4,6},{5,7},{6,4},{7,5},{8,10},{9,11},{10,... | collective-permute-start | bytes 98312 | tf_op jit(solution)/shard_map/ppermute | solution.py:30
  11.0 3.9 %collective-permute-start.1 = (bf16[16,8,128]{2,1,0:T(8,128)(2,1)S(1)}, bf16[16,8,128]{2,1,0:T(8,128)(2,1)S(1)}, u32[]{:S(2)}, u32[]{:S(2)}) collective-permute-start(bf16[16,8,128]{2,1,0:T(8,128)(2,1)S(1)} %pad_maximum_fusion), channel_id=1, source_target_pairs={{0,1},{1,0},{2,3},{3,2},{4,5},{5,4},{6,7},{7,6},{8,9},{9,8},{10,11... | collective-permute-start | bytes 98312 | tf_op jit(solution)/shard_map/ppermute | solution.py:30
  11.5 7.2 %collective-permute-start.6 = (bf16[7,8,8,128]{3,2,1,0:T(8,128)(2,1)S(1)}, bf16[7,8,8,128]{3,2,1,0:T(8,128)(2,1)S(1)}, u32[]{:S(2)}, u32[]{:S(2)}) collective-permute-start(bf16[7,8,8,128]{3,2,1,0:T(8,128)(2,1)S(1)} %get-tuple-element.28), channel_id=1, source_target_pairs={{0,8},{8,0},{16,24},{24,16},{1,9},{9,1},{17,25},{25,17},{2,10},{10... | collective-permute-start | bytes 344072 | tf_op jit(solution)/shard_map/ppermute | solution.py:36
  11.5 7.2 %collective-permute-start.7 = (bf16[7,8,8,128]{3,2,1,0:T(8,128)(2,1)S(1)}, bf16[7,8,8,128]{3,2,1,0:T(8,128)(2,1)S(1)}, u32[]{:S(2)}, u32[]{:S(2)}) collective-permute-start(bf16[7,8,8,128]{3,2,1,0:T(8,128)(2,1)S(1)} %get-tuple-element.29), channel_id=1, source_target_pairs={{0,24},{8,16},{16,8},{24,0},{1,25},{9,17},{17,9},{25,1},{2,26},{10... | collective-permute-start | bytes 344072 | tf_op jit(solution)/shard_map/ppermute | solution.py:42
  15.0 3.6 %collective-permute-start.4 = (bf16[11,8,128]{2,1,0:T(8,128)(2,1)S(1)}, bf16[11,8,128]{2,1,0:T(8,128)(2,1)S(1)}, u32[]{:S(2)}, u32[]{:S(2)}) collective-permute-start(bf16[11,8,128]{2,1,0:T(8,128)(2,1)S(1)} %broadcast_select_fusion.1), channel_id=1, source_target_pairs={{0,8},{8,0},{16,24},{24,16},{1,9},{9,1},{17,25},{25,17},{2,10},{10... | collective-permute-start | bytes 67592 | tf_op jit(solution)/shard_map/ppermute | solution.py:36
  15.1 3.5 %collective-permute-start.5 = (bf16[11,8,128]{2,1,0:T(8,128)(2,1)S(1)}, bf16[11,8,128]{2,1,0:T(8,128)(2,1)S(1)}, u32[]{:S(2)}, u32[]{:S(2)}) collective-permute-start(bf16[11,8,128]{2,1,0:T(8,128)(2,1)S(1)} %get-tuple-element.46), channel_id=1, source_target_pairs={{0,24},{8,16},{16,8},{24,0},{1,25},{9,17},{17,9},{25,1},{2,26},{10... | collective-permute-start | bytes 67592 | tf_op jit(solution)/shard_map/ppermute | solution.py:42
  20.0 7.0 %collective-permute-start.8 = (f32[16,8,128]{2,1,0:T(8,128)S(1)}, f32[16,8,128]{2,1,0:T(8,128)S(1)}, u32[]{:S(2)}, u32[]{:S(2)}) collective-permute-start(f32[16,8,128]{2,1,0:T(8,128)S(1)} %get-tuple-element.30), channel_id=1, source_target_pairs={{0,1},{1,0},{2,3},{3,2},{4,5},{5,4},{6,7},{7,6},{8,9},{9,8},{10,11... | collective-permute-start | bytes 196616 | tf_op jit(solution)/shard_map/ppermute | solution.py:30
  20.6 6.4 %collective-permute-start.9 = (f32[16,8,128]{2,1,0:T(8,128)S(1)}, f32[16,8,128]{2,1,0:T(8,128)S(1)}, u32[]{:S(2)}, u32[]{:S(2)}) collective-permute-start(f32[16,8,128]{2,1,0:T(8,128)S(1)} %get-tuple-element.31), channel_id=1, source_target_pairs={{0,2},{1,3},{2,0},{3,1},{4,6},{5,7},{6,4},{7,5},{8,10},{9,11},{10,... | collective-permute-start | bytes 196616 | tf_op jit(solution)/shard_map/ppermute | solution.py:30
  22.2 5.2 %collective-permute-start.10 = (f32[16,8,128]{2,1,0:T(8,128)S(1)}, f32[16,8,128]{2,1,0:T(8,128)S(1)}, u32[]{:S(2)}, u32[]{:S(2)}) collective-permute-start(f32[16,8,128]{2,1,0:T(8,128)S(1)} %get-tuple-element.32), channel_id=1, source_target_pairs={{0,3},{1,2},{2,1},{3,0},{4,7},{5,6},{6,5},{7,4},{8,11},{9,10},{10,... | collective-permute-start | bytes 196616 | tf_op jit(solution)/shard_map/ppermute | solution.py:30
  27.4 4.9 %collective-permute-start.11 = (f32[8,8,128]{2,1,0:T(8,128)S(1)}, f32[8,8,128]{2,1,0:T(8,128)S(1)}, u32[]{:S(2)}, u32[]{:S(2)}) collective-permute-start(f32[8,8,128]{2,1,0:T(8,128)S(1)} %slice_bitcast_fusion), channel_id=1, source_target_pairs={{0,4},{1,5},{2,6},{3,7},{4,0},{5,1},{6,2},{7,3},{8,12},{9,13},{10,... | collective-permute-start | bytes 98312 | tf_op jit(solution)/shard_map/ppermute | solution.py:30

commit v5 on v4

--- a/solution.py
+++ b/solution.py
@@ -18,6 +18,7 @@
 f32 = jnp.float32
 bf16 = jnp.bfloat16
 PEERS = 4
+ORDER = (0, 1, 3, 2)
 VMEM_LIMIT = 48 * 1024 * 1024
 
 raw = [math.exp(-k * k / (2 * sigma * sigma)) for k in range(SMOOTH + 1)]
@@ -75,24 +76,21 @@
 
 
 def even_odd(base, frac):
-    even = (base == -2.0) | (base == 0.0) | (base == 2.0)
+    even = (base & 1) == 0
     rest = 1.0 - frac
     return jnp.where(even, rest, frac), jnp.where(even, frac, rest)
 
 
 def warp_slice(shifted, plane, sz, sr, sc, fz, fr, fc):
     rows = sz.shape[0]
-    row = lax.broadcasted_iota(jnp.int32, sz.shape, 0).astype(f32) + sr
-    top = rows - 1.0
-    index0 = jnp.clip(row, 0.0, top).astype(jnp.int32)
-    index1 = jnp.clip(row + 1.0, 0.0, top).astype(jnp.int32)
-    weight0 = jnp.where((row >= 0.0) & (row <= top), 1.0 - fr, 0.0)
-    weight1 = jnp.where((row >= -1.0) & (row <= top - 1.0), fr, 0.0)
+    row = lax.broadcasted_iota(jnp.int32, sz.shape, 0) + sr
+    after = row + 1
+    index0, index1 = row & (rows - 1), after & (rows - 1)
+    weight0 = jnp.where(index0 == row, 1.0 - fr, 0.0)
+    weight1 = jnp.where(index1 == after, fr, 0.0)
     col_e, col_o = even_odd(sc, fc)
     dep_e, dep_o = even_odd(sz, fz)
-    c1, c2, c3, c4 = [sc >= edge for edge in (-1.0, 0.0, 1.0, 2.0)]
-    z1, z2, z3, z4 = [sz >= edge for edge in (-1.0, 0.0, 1.0, 2.0)]
-    picks = {2: (c1, z1), 3: (c2, z2), 4: (c3, z3), 5: (c4, z4)}
+    picks = {k: (sc >= k - 3, sz >= k - 3) for k in range(2, TAPS)}
     planes = [None, None]
     for kz in range(TAPS):
         corner = [[None, None], [None, None]]
@@ -152,7 +150,7 @@
 
 
 def slice_fields(shifts, fractions, z):
-    return [shifts[axis, z].astype(f32) for axis in range(3)] + [
+    return [shifts[axis, z] for axis in range(3)] + [
         fractions[axis, z].astype(f32) for axis in range(3)
     ]
 
@@ -160,7 +158,9 @@
 def place_of_shard(me, shard, members):
     apart = me ^ shard
     quarter = members // PEERS
-    return (apart & (PEERS - 1)) * quarter + mirrored(apart // PEERS, quarter)
+    peer = apart & (PEERS - 1)
+    block = sum(jnp.where(peer == k, c, 0) for c, k in enumerate(ORDER))
+    return block * quarter + mirrored(apart // PEERS, quarter)
 
 
 def build_pack(depth, rows, cols, share):
@@ -207,87 +207,143 @@
     )
 
 
+def peer_shard(i, me, share, members, first):
+    quarter = members // PEERS
+    block = i // share
+    return (me ^ (first + block // quarter + PEERS * (block % quarter))) * share + i % share
+
+
+def end_slices(depth):
+    return [*range(SHIFT), *range(depth - SHIFT - 1, depth)]
+
+
 def build_inner_warp(depth, rows, cols, members):
     share = depth // members
-
-    def kernel(pieces, shifts, fractions, warped, slab, shifted):
+    away = depth - depth // PEERS
+    front, count = SHIFT, depth + 2 * SHIFT + 2
+
+    def kernel(pieces, shifts, fractions, subjects, sent, send, shifted, slab):
         me = lax.axis_index("subj")
         quarter = members // PEERS
+        slab[0:front] = jnp.zeros((front, rows, cols), f32)
+        slab[front + depth : count] = jnp.zeros((count - front - depth, rows, cols), f32)
         for k in range(members):
-            shard = me ^ (k // quarter + PEERS * mirrored(k % quarter, quarter))
-            slab[pl.ds(shard * share, share)] = pieces[k * share : (k + 1) * share].astype(f32)
-        for start in range(0, depth, depth // 2):
-            move_columns(slab, shifted, start, depth // 2)
+            shard = me ^ (ORDER[k // quarter] + PEERS * mirrored(k % quarter, quarter))
+            slab[pl.ds(front + shard * share, share)] = pieces[k * share : (k + 1) * share].astype(f32)
+        for start in range(0, count, count // 2):
+            move_columns(slab, shifted, start, count // 2)
 
         def body(i, carry):
-            z = i + EDGE
-            warped[i] = warp_slice(shifted, z - SHIFT, *slice_fields(shifts, fractions, z))
-            return carry
-
-        lax.fori_loop(0, depth - 2 * EDGE, body, 0, unroll=2)
-
+            z = peer_shard(i, me, share, members, 1)
+            out = warp_slice(shifted, front + z - SHIFT, *slice_fields(shifts, fractions, z))
+            sent[i] = out
+            send[i] = subjects[z].astype(f32) - out
+            return carry
+
+        lax.fori_loop(0, away, body, 0, unroll=6)
+
+    part = (away, rows, cols)
     return local_call(
-        kernel, "inner_warp", [(depth - 2 * EDGE, rows, cols)], 3,
-        [(depth, rows, cols), (TAPS, depth, rows, cols)], 1_000_000_000,
-    )
-
-
-def build_outer_warp(depth, rows, cols, members, groups):
+        kernel, "inner_warp", [part, part, (TAPS, count, rows, cols)], 4,
+        [(count, rows, cols)], 1_000_000_000,
+    )
+
+
+def build_end_warp(depth, rows, cols, members, groups):
     share = depth // members
-    ext = depth + 2 * EDGE
-    planes = 2 * HALO
+    quarter, kept = members // PEERS, depth // PEERS
+    away = depth - kept
+    inner = SHIFT + EDGE
+    planes = HALO + inner
 
     def kernel(
-        low_t, high_t, near_t, far_t, near_m, far_m, shifts, fractions, subjects, inner,
-        warped, keep, send1, send2, send3, slab, shifted,
+        low_t, high_t, near_t, far_t, shifts, fractions, subjects, send_in, *outs_and_scratch
     ):
+        *sends, ends, shifted, slab = outs_and_scratch
         odd = lax.axis_index("gz") % 2 == 1
         me = lax.axis_index("subj")
         inside = has_far(lax.axis_index("gz"), groups)
         near, far = near_t[...].astype(f32), jnp.where(inside, far_t[...].astype(f32), 0.0)
         slab[0:HALO] = jnp.where(odd, near, far)
-        slab[HALO:planes] = low_t[...].astype(f32)
-        slab[planes : planes + HALO] = high_t[...].astype(f32)
-        slab[planes + HALO : 2 * planes] = jnp.where(odd, far, near)
+        slab[HALO:planes] = low_t[0:inner].astype(f32)
+        slab[planes : planes + inner] = high_t[HALO - inner : HALO].astype(f32)
+        slab[planes + inner : 2 * planes] = jnp.where(odd, far, near)
         move_columns(slab, shifted, 0, 2 * planes)
-        warped[2 * EDGE : depth] = inner[...]
-
-        def body(z, carry):
-            def edge(low):
+        for number, send in enumerate(sends):
+            send[...] = send_in[number * kept : (number + 1) * kept]
+        for number, z in enumerate(end_slices(depth)):
+            plane = HALO + z if z < SHIFT else 2 * planes - HALO - depth + z
+            out = warp_slice(shifted, plane - SHIFT, *slice_fields(shifts, fractions, z))
+            ends[number] = out
+            residual = subjects[z].astype(f32) - out
+            apart = me ^ (z // share)
+            index = (apart // PEERS) * share + z % share
+            for k, send in enumerate(sends, 1):
+
+                @pl.when(apart % PEERS == k)
+                def _():
+                    send[index] = residual
+
+    part = (kept, rows, cols)
+    count = len(end_slices(depth))
+    return local_call(
+        kernel, "end_warp",
+        [part] * (PEERS - 1) + [(count, rows, cols), (TAPS, 2 * planes, rows, cols)], 8,
+        [(2 * planes, rows, cols)], 300_000_000,
+    )
+
+
+def build_rest_warp(depth, rows, cols, members, groups):
+    share = depth // members
+    kept = depth // PEERS
+    planes = HALO + SHIFT + EDGE
+
+    def kernel(
+        moved, moved_ends, sent, ends, near_m, far_m, shifts, fractions, subjects, warped, keep
+    ):
+        me = lax.axis_index("subj")
+        odd = lax.axis_index("gz") % 2 == 1
+        inside = has_far(lax.axis_index("gz"), groups)
+
+        def body(i, carry):
+            z = peer_shard(i, me, share, members, 0)
+            out = warp_slice(moved, z, *slice_fields(shifts, fractions, z))
+            warped[EDGE + z] = out
+            keep[i] = subjects[z].astype(f32) - out
+            for part in range(PEERS - 1):
+                number = part * kept + i
+                warped[EDGE + peer_shard(number, me, share, members, 1)] = sent[number]
+            return carry
+
+        lax.fori_loop(0, kept, body, 0, unroll=4)
+        for number, z in enumerate(end_slices(depth)):
+            out = ends[number]
+            warped[EDGE + z] = out
+            apart = me ^ (z // share)
+
+            @pl.when(apart % PEERS == 0)
+            def _():
+                keep[(apart // PEERS) * share + z % share] = subjects[z].astype(f32) - out
+
+        def outside(z, carry):
+            for low in (True, False):
                 fields = []
                 for axis in range(6):
                     one = near_m[axis, z].astype(f32)
                     two = jnp.where(inside, far_m[axis, z].astype(f32), 0.0)
-                    fields.append(jnp.where(odd, one, two) if low else jnp.where(odd, two, one))
-                return fields
-
-            last = depth - EDGE + z
-            warped[z] = warp_slice(shifted, z + 1, *edge(True))
-            warped[z + EDGE] = warp_slice(
-                shifted, z + EDGE + 1, *slice_fields(shifts, fractions, z)
-            )
-            warped[z + depth] = warp_slice(
-                shifted, planes + z + 1, *slice_fields(shifts, fractions, last)
-            )
-            warped[z + depth + EDGE] = warp_slice(
-                shifted, planes + z + EDGE + 1, *edge(False)
-            )
-            return carry
-
-        lax.fori_loop(0, EDGE, body, 0)
-
-        for k in range(members):
-            shard = me ^ k
-            target = (keep, send1, send2, send3)[k % PEERS]
-            start = shard * share
-            target[(k // PEERS) * share : (k // PEERS + 1) * share] = (
-                subjects[pl.ds(start, share)].astype(f32) - warped[pl.ds(EDGE + start, share)]
-            )
-
-    part = (depth // PEERS, rows, cols)
+                    field = jnp.where(odd, one, two) if low else jnp.where(odd, two, one)
+                    fields.append(field.astype(jnp.int32) if axis < 3 else field)
+                plane = HALO - EDGE + z if low else 2 * planes - HALO + z
+                warped[z if low else depth + EDGE + z] = warp_slice(
+                    moved_ends, plane - SHIFT, *fields
+                )
+            return carry
+
+        lax.fori_loop(0, EDGE, outside, 0, unroll=2)
+
     return local_call(
-        kernel, "outer_warp", [(ext, rows, cols)] + [part] * PEERS, 10,
-        [(2 * planes, rows, cols), (TAPS, 2 * planes, rows, cols)], 600_000_000,
+        kernel, "rest_warp", [(depth + 2 * EDGE, rows, cols), (kept, rows, cols)], 9, [],
+        600_000_000,
     )
 
 
@@ -348,6 +404,7 @@
 
 STEP = 8
 CHUNK = 16
+PART = 32
 SCALE = 1.0 / float((2 * WIN + 1) ** 3)
 
 
@@ -384,7 +441,7 @@
                 boxes[field, at] = result.reshape(CHUNK, rows, cols)
             return carry
 
-        lax.fori_loop(0, ext // CHUNK, columns, 0)
+        lax.fori_loop(0, ext // CHUNK, columns, 0, unroll=True)
         row = lax.broadcasted_iota(jnp.int32, (rows, cols), 0)
 
         def local(i, carry):
@@ -398,7 +455,7 @@
                 variance[start + k] = two[k] - one[k] * one[k]
             return carry
 
-        lax.fori_loop(0, mid // STEP, local, 0)
+        lax.fori_loop(0, mid // STEP, local, 0, unroll=True)
 
     return local_call(
         kernel, "image",
@@ -426,7 +483,7 @@
             slope[at] = both[:, cols:].reshape(CHUNK, rows, cols)
             return carry
 
-        lax.fori_loop(0, ext // CHUNK, columns, 0)
+        lax.fori_loop(0, ext // CHUNK, columns, 0, unroll=True)
         row = lax.broadcasted_iota(jnp.int32, (rows, cols), 0)
 
         def local(i, carry):
@@ -453,7 +510,7 @@
                 force[2, start + k] = factor * slope[at]
             return carry
 
-        lax.fori_loop(0, mid // STEP, local, 0)
+        lax.fori_loop(0, mid // STEP, local, 0, unroll=True)
 
         @pl.when(lax.axis_index("gz") == 0)
         def _():
@@ -470,7 +527,9 @@
 
 
 def build_smooth(depth, rows, cols):
-    def kernel(force, velocity, padded):
+    chunks = depth // PART
+
+    def kernel(force, velocity, padded, result, done):
         g_high, g_low = split(gauss_columns(cols))
         g_all = jnp.concatenate(
             [
@@ -481,33 +540,60 @@
         )
         padded[...] = jnp.zeros(padded.shape, f32)
 
+        def sent(i):
+            at = pl.ds(i * PART, PART)
+            return pltpu.make_async_copy(result.at[:, at], velocity.at[:, at], done.at[i])
+
         def finish(i, carry):
-            start = i * STEP
+            start = i * PART
             for axis in range(3):
-                x = [force[axis, start + k] for k in range(STEP + 2 * SMOOTH)]
-                for k in range(STEP):
+                x = [force[axis, start + k] for k in range(PART + 2 * SMOOTH)]
+                for k in range(PART):
                     value = GAUSS[0] * x[k + SMOOTH]
                     for d in range(1, SMOOTH + 1):
                         value = value + GAUSS[d] * (x[k + SMOOTH - d] + x[k + SMOOTH + d])
                     padded[axis, k, SMOOTH : SMOOTH + rows] = value
-                mixed = GAUSS[0] * padded[axis, :, SMOOTH : SMOOTH + rows]
-                for d in range(1, SMOOTH + 1):
-                    mixed = mixed + GAUSS[d] * (
-                        padded[axis, :, SMOOTH - d : SMOOTH - d + rows]
-                        + padded[axis, :, SMOOTH + d : SMOOTH + d + rows]
-                    )
-                pair = jnp.concatenate(split(flat(mixed)), axis=1)
-                done = jnp.dot(pair, g_all, preferred_element_type=f32)
-                velocity[axis, pl.ds(start, STEP)] = (done[:, :cols] + done[:, cols:]).reshape(
-                    STEP, rows, cols
+                highs, lows = [], []
+                for k in range(0, PART, 2):
+                    both = []
+                    for n in (k, k + 1):
+                        value = GAUSS[0] * padded[axis, n, SMOOTH : SMOOTH + rows]
+                        for d in range(1, SMOOTH + 1):
+                            value = value + GAUSS[d] * (
+                                padded[axis, n, SMOOTH - d : SMOOTH - d + rows]
+                                + padded[axis, n, SMOOTH + d : SMOOTH + d + rows]
+                            )
+                        both.append(value)
+                    high, low = split(jnp.concatenate(both, axis=0))
+                    highs.append(high)
+                    lows.append(low)
+                pair = jnp.concatenate(
+                    [jnp.concatenate(highs, axis=0), jnp.concatenate(lows, axis=0)], axis=1
                 )
-            return carry
-
-        lax.fori_loop(0, depth // STEP, finish, 0)
-
-    return local_call(
-        kernel, "smooth", [(3, depth, rows, cols)], 1,
-        [(3, STEP, rows + 2 * SMOOTH, cols)], 600_000_000,
+                mixed = jnp.dot(pair, g_all, preferred_element_type=f32)
+                result[axis, pl.ds(start, PART)] = (mixed[:, :cols] + mixed[:, cols:]).reshape(
+                    PART, rows, cols
+                )
+            sent(i).start()
+            return carry
+
+        lax.fori_loop(0, chunks, finish, 0, unroll=True)
+        for i in range(chunks):
+            sent(i).wait()
+
+    return pl.pallas_call(
+        kernel,
+        out_shape=[jax.ShapeDtypeStruct((3, depth, rows, cols), f32)],
+        in_specs=vmem_specs(1),
+        out_specs=[pl.BlockSpec(memory_space=pl.ANY)],
+        scratch_shapes=[
+            pltpu.VMEM((3, PART, rows + 2 * SMOOTH, cols), f32),
+            pltpu.VMEM((3, depth, rows, cols), f32),
+            pltpu.SemaphoreType.DMA((chunks,)),
+        ],
+        compiler_params=pltpu.CompilerParams(vmem_limit_bytes=VMEM_LIMIT),
+        cost_estimate=pl.CostEstimate(flops=600_000_000, bytes_accessed=8_000_000, transcendentals=0),
+        name="smooth",
     )
 
 
@@ -531,7 +617,7 @@
     for bit in bits[-2::-1]:
         pieces = jnp.concatenate([pieces, swap(pieces, "subj", bit)], axis=0)
     pieces = jnp.concatenate(
-        [pieces] + [swap(pieces, "subj", k) for k in range(1, PEERS)], axis=0
+        [pieces] + [swap(pieces, "subj", k) for k in ORDER[1:]], axis=0
     )
 
     def shares(numbers):
@@ -545,12 +631,15 @@
     to_near, to_far = at_ends("gz", low_t, high_t)
     near_t, far_t = swap_near(to_near, "gz"), swap_far(to_far, "gz")
 
-    (inner,) = build_inner_warp(depth, rows, cols, members)(pieces, shift, fraction)
-    warped, keep, *sends = build_outer_warp(depth, rows, cols, members, groups)(
-        low_t, high_t, near_t, far_t, near_m, far_m, shift, fraction, subject, inner
-    )
-
-    parts = [swap(send, "subj", k) for k, send in zip(range(1, PEERS), sends)]
+    sent, send, moved = build_inner_warp(depth, rows, cols, members)(pieces, shift, fraction, subject)
+    *sends, ends, moved_ends = build_end_warp(depth, rows, cols, members, groups)(
+        low_t, high_t, near_t, far_t, shift, fraction, subject, send
+    )
+
+    parts = [swap(sends[k - 1], "subj", k) for k in (3, 1, 2)]
+    warped, keep = build_rest_warp(depth, rows, cols, members, groups)(
+        moved, moved_ends, sent, ends, near_m, far_m, shift, fraction, subject
+    )
     near_m, far_m, subject, warped = lax.optimization_barrier((near_m, far_m, subject, warped))
     image, mean, variance = build_image(depth, rows, cols, groups)(near_m, far_m, subject)
     (force,) = build_force(depth, rows, cols, groups)(warped, image, mean, variance)

time: 33.1 us -> 32.5 us (0.982)
  Pallas kernels: 9.81 us -> 7.27 us
  waiting for transfers between devices: 2.41 us -> 4.36 us
  starting transfers between devices: 16.2 us -> 15.3 us
  local copies, waits for them, and re-layouts: 2.95 us -> 3.8 us
    ppermute x8, waiting for transfers between devices: 2.4 us -> 4.35 us  [swap(): return lax.ppermute(block, axis, [(i, i ^ bit) for i in range(count)])]
    pallas_call x1, Pallas kernels: 2.91 us -> 1.84 us  [per_device(): velocity, = build_smooth(depth, rows, cols)(force)]
    pallas_call x1, Pallas kernels: 2.07 us -> 1.11 us  [per_device(): build_force(depth, rows, cols, groups)(warped, image, mean, variance)]
    unnamed x15 -> x17, local copies, waits for them, and re-layouts: 2.91 us -> 3.78 us
    ppermute x8, starting transfers between devices: 12.9 us -> 12.1 us  [swap(): return lax.ppermute(block, axis, [(i, i ^ bit) for i in range(count)])]
    pallas_call x1, Pallas kernels: 1.32 us -> 0.54 us  [per_device(): build_image(depth, rows, cols, groups)(near_m, far_m, subject)]
    pallas_call x2 -> x3, Pallas kernels: 3.22 us -> 3.5 us  [the longest x1 1.81 us: per_device(): build_inner_warp(depth, rows, cols, members)]
  transfers between devices with their start and end apart: 12 -> 12, of which waited for: 3 -> 5; matrix products, arithmetic and copies ran while one was open for 0% -> 0% of each run, Pallas kernels for 26% -> 23%
where the time goes in v5:
time: 32.5 us; the launch traced here: 32.2 us
  starting transfers between devices  15.3 us (47%)
  Pallas kernels  7.27 us (22%)
  waiting for transfers between devices  4.36 us (13%)
  local copies, waits for them, and re-layouts  3.8 us (12%)
  between operations  0.78 us (2%)
  other arithmetic  0.67 us (2%)
    ppermute x8, starting transfers between devices, swap(): return lax.ppermute(block, axis, [(i, i ^ bit) for i in range(count)])  12.1 us
    ppermute x8, waiting for transfers between devices, swap(): return lax.ppermute(block, axis, [(i, i ^ bit) for i in range(count)])  4.35 us
    unnamed x17, local copies, waits for them, and re-layouts  3.78 us
    ppermute x2, starting transfers between devices, swap_far(): lax.ppermute(block, axis, [(i, (i + 1 if i % 2 else i - 1) % count) for i...  3.21 us
    pallas_call x1, Pallas kernels, per_device(): velocity, = build_smooth(depth, rows, cols)(force)  1.84 us
    pallas_call x1, Pallas kernels, per_device(): build_inner_warp(depth, rows, cols, members)  1.81 us
    pallas_call x1, Pallas kernels, per_device(): build_rest_warp(depth, rows, cols, members, groups)  1.23 us
    pallas_call x1, Pallas kernels, per_device(): build_force(depth, rows, cols, groups)(warped, image, mean, variance)  1.11 us
  transfers between devices with their start and end apart: 12, of which 5 were waited for; matrix products, arithmetic and copies ran while one was open for 0% of the time, Pallas kernels for 23%

profile of v5, /device:TPU:0, one launch (start us, length us, event | category | flops | bytes accessed | tf_op | source)
XLA Modules:
  0.0 32.2 jit_solution(17575944790068796523)
XLA Ops:
  0.6 4.1 %collective-permute-start = (bf16[8,8,128]{2,1,0:T(8,128)(2,1)}, bf16[8,8,128]{2,1,0:T(8,128)(2,1)S(1)}, u32[]{:S(2)}, u32[]{:S(2)}) collective-permute-start(bf16[8,8,128]{2,1,0:T(8,128)(2,1)} %template.1), channel_id=1, source_target_pairs={{0,4},{1,5},{2,6},{3,7},{4,0},{5,1},{6,2},{7,3},{8,12},{9,13},{10,... | collective-permute-start | bytes 49160 | tf_op jit(solution)/shard_map/ppermute | solution.py:31
  4.7 1.1 %copy-done = s32[1,3,64,8,128]{4,3,2,1,0:T(8,128)S(1)} copy-done((s32[1,3,64,8,128]{4,3,2,1,0:T(8,128)S(1)}, s32[1,3,64,8,128]{4,3,2,1,0:T(8,128)}, u32[]{:S(2)}) %copy-start) | copy-done | bytes 786456
  5.9 1.0 %copy-done.2 = bf16[1,3,64,8,128]{4,3,2,1,0:T(8,128)(2,1)S(1)} copy-done((bf16[1,3,64,8,128]{4,3,2,1,0:T(8,128)(2,1)S(1)}, bf16[1,3,64,8,128]{4,3,2,1,0:T(8,128)(2,1)}, u32[]{:S(2)}) %copy-start.2) | copy-done | bytes 393240
  6.9 0.9 %copy-done.4 = bf16[1,64,8,128]{3,2,1,0:T(8,128)(2,1)S(1)} copy-done((bf16[1,64,8,128]{3,2,1,0:T(8,128)(2,1)S(1)}, bf16[1,64,8,128]{3,2,1,0:T(8,128)(2,1)}, u32[]{:S(2)}) %copy-start.4) | copy-done | bytes 131096
  7.8 0.7 %copy-done.6 = bf16[8,8,128]{2,1,0:T(8,128)(2,1)S(1)} copy-done((bf16[8,8,128]{2,1,0:T(8,128)(2,1)S(1)}, bf16[8,8,128]{2,1,0:T(8,128)(2,1)}, u32[]{:S(2)}) %copy-start.6) | copy-done | bytes 16408
  8.8 1.6 %collective-permute-start.1 = (bf16[16,8,128]{2,1,0:T(8,128)(2,1)S(1)}, bf16[16,8,128]{2,1,0:T(8,128)(2,1)S(1)}, u32[]{:S(2)}, u32[]{:S(2)}) collective-permute-start(bf16[16,8,128]{2,1,0:T(8,128)(2,1)S(1)} %pad_maximum_fusion), channel_id=1, source_target_pairs={{0,1},{1,0},{2,3},{3,2},{4,5},{5,4},{6,7},{7,6},{8,9},{9,8},{10,11... | collective-permute-start | bytes 98312 | tf_op jit(solution)/shard_map/ppermute | solution.py:31
  10.4 1.5 %collective-permute-start.2 = (bf16[16,8,128]{2,1,0:T(8,128)(2,1)S(1)}, bf16[16,8,128]{2,1,0:T(8,128)(2,1)S(1)}, u32[]{:S(2)}, u32[]{:S(2)}) collective-permute-start(bf16[16,8,128]{2,1,0:T(8,128)(2,1)S(1)} %pad_maximum_fusion), channel_id=1, source_target_pairs={{0,3},{1,2},{2,1},{3,0},{4,7},{5,6},{6,5},{7,4},{8,11},{9,10},{10,... | collective-permute-start | bytes 98312 | tf_op jit(solution)/shard_map/ppermute | solution.py:31
  11.9 0.4 %collective-permute-start.3 = (bf16[16,8,128]{2,1,0:T(8,128)(2,1)S(1)}, bf16[16,8,128]{2,1,0:T(8,128)(2,1)S(1)}, u32[]{:S(2)}, u32[]{:S(2)}) collective-permute-start(bf16[16,8,128]{2,1,0:T(8,128)(2,1)S(1)} %pad_maximum_fusion), channel_id=1, source_target_pairs={{0,2},{1,3},{2,0},{3,1},{4,6},{5,7},{6,4},{7,5},{8,10},{9,11},{10,... | collective-permute-start | bytes 98312 | tf_op jit(solution)/shard_map/ppermute | solution.py:31
  12.4 1.6 %collective-permute-start.10 = (bf16[7,8,8,128]{3,2,1,0:T(8,128)(2,1)S(1)}, bf16[7,8,8,128]{3,2,1,0:T(8,128)(2,1)S(1)}, u32[]{:S(2)}, u32[]{:S(2)}) collective-permute-start(bf16[7,8,8,128]{3,2,1,0:T(8,128)(2,1)S(1)} %get-tuple-element.38), channel_id=1, source_target_pairs={{0,24},{8,16},{16,8},{24,0},{1,25},{9,17},{17,9},{25,1},{2,26},{10... | collective-permute-start | bytes 344072 | tf_op jit(solution)/shard_map/ppermute | solution.py:43
  14.0 1.2 %collective-permute-done.2 = bf16[16,8,128]{2,1,0:T(8,128)(2,1)S(1)} collective-permute-done((bf16[16,8,128]{2,1,0:T(8,128)(2,1)S(1)}, bf16[16,8,128]{2,1,0:T(8,128)(2,1)S(1)}, u32[]{:S(2)}, u32[]{:S(2)}) %collective-permute-start.2) | collective-permute-done | bytes 32800 | tf_op jit(solution)/shard_map/ppermute | solution.py:31
  15.2 0.6 %collective-permute-done.3 = bf16[16,8,128]{2,1,0:T(8,128)(2,1)S(1)} collective-permute-done((bf16[16,8,128]{2,1,0:T(8,128)(2,1)S(1)}, bf16[16,8,128]{2,1,0:T(8,128)(2,1)S(1)}, u32[]{:S(2)}, u32[]{:S(2)}) %collective-permute-start.3) | collective-permute-done | bytes 32800 | tf_op jit(solution)/shard_map/ppermute | solution.py:31
  16.0 1.6 %collective-permute-start.5 = (bf16[11,8,128]{2,1,0:T(8,128)(2,1)S(1)}, bf16[11,8,128]{2,1,0:T(8,128)(2,1)S(1)}, u32[]{:S(2)}, u32[]{:S(2)}) collective-permute-start(bf16[11,8,128]{2,1,0:T(8,128)(2,1)S(1)} %get-tuple-element.56), channel_id=1, source_target_pairs={{0,24},{8,16},{16,8},{24,0},{1,25},{9,17},{17,9},{25,1},{2,26},{10... | collective-permute-start | bytes 67592 | tf_op jit(solution)/shard_map/ppermute | solution.py:43
  17.6 1.8 %inner_warp.1 = (f32[48,8,128]{2,1,0:T(8,128)S(1)}, f32[48,8,128]{2,1,0:T(8,128)S(1)}, f32[6,70,8,128]{3,2,1,0:T(8,128)S(1)}) custom-call(bf16[64,8,128]{2,1,0:T(8,128)(2,1)S(1)} %constant_dynamic-update-slice_fusion.pieces, s32[3,64,8,128]{3,2,1,0:T(8,128)S(1)} %bitcast.14, bf16[3,64,8,128]{3,2,1,0:T(8,128)(2,1)S(1)} %bitcast.18, ...), custom_call_target="tpu_custom_call" | custom-call | flops 1000000000 | bytes 8000000 | tf_op jit(solution)/shard_map/inner_warp/pallas_call | solution.py:634
  19.4 0.5 %end_warp.1 = (f32[16,8,128]{2,1,0:T(8,128)S(1)}, f32[16,8,128]{2,1,0:T(8,128)S(1)}, f32[16,8,128]{2,1,0:T(8,128)S(1)}, f32[5,8,128]{2,1,0:T(8,128)S(1)}, f32[6,42,8,128]{3,2,1,0:T(8,128)S(1)}) custom-call(bf16[11,8,128]{2,1,0:T(8,128)(2,1)S(1)} %get-tuple-element.58.low_t, bf16[11,8,128]{2,1,0:T(8,128)(2,1)S(1)} %get-tuple-element.57.high_t, ...), custom_call_target="tpu_custom_call" | custom-call | flops 300000000 | bytes 8000000 | tf_op jit(solution)/shard_map/end_warp/pallas_call | solution.py:635
  19.9 1.5 %collective-permute-start.6 = (f32[16,8,128]{2,1,0:T(8,128)S(1)}, f32[16,8,128]{2,1,0:T(8,128)S(1)}, u32[]{:S(2)}, u32[]{:S(2)}) collective-permute-start(f32[16,8,128]{2,1,0:T(8,128)S(1)} %get-tuple-element.34), channel_id=1, source_target_pairs={{0,3},{1,2},{2,1},{3,0},{4,7},{5,6},{6,5},{7,4},{8,11},{9,10},{10,... | collective-permute-start | bytes 196616 | tf_op jit(solution)/shard_map/ppermute | solution.py:31
  21.4 1.1 %collective-permute-start.7 = (f32[16,8,128]{2,1,0:T(8,128)S(1)}, f32[16,8,128]{2,1,0:T(8,128)S(1)}, u32[]{:S(2)}, u32[]{:S(2)}) collective-permute-start(f32[16,8,128]{2,1,0:T(8,128)S(1)} %get-tuple-element.35), channel_id=1, source_target_pairs={{0,1},{1,0},{2,3},{3,2},{4,5},{5,4},{6,7},{7,6},{8,9},{9,8},{10,11... | collective-permute-start | bytes 196616 | tf_op jit(solution)/shard_map/ppermute | solution.py:31
  22.4 1.0 %collective-permute-start.8 = (f32[16,8,128]{2,1,0:T(8,128)S(1)}, f32[16,8,128]{2,1,0:T(8,128)S(1)}, u32[]{:S(2)}, u32[]{:S(2)}) collective-permute-start(f32[16,8,128]{2,1,0:T(8,128)S(1)} %get-tuple-element.36), channel_id=1, source_target_pairs={{0,2},{1,3},{2,0},{3,1},{4,6},{5,7},{6,4},{7,5},{8,10},{9,11},{10,... | collective-permute-start | bytes 196616 | tf_op jit(solution)/shard_map/ppermute | solution.py:31
  23.5 1.2 %rest_warp.1 = (f32[80,8,128]{2,1,0:T(8,128)S(1)}, f32[16,8,128]{2,1,0:T(8,128)S(1)}) custom-call(f32[6,70,8,128]{3,2,1,0:T(8,128)S(1)} %get-tuple-element.39.moved, f32[6,42,8,128]{3,2,1,0:T(8,128)S(1)} %get-tuple-element.40.moved_ends, f32[48,8,128]{2,1,0:T(8,128)S(1)} %get-tuple-element.41.sent, f32[5,8,128]{2,1,0:T(8,128)S(1)} %get-tuple-element.42.ends, ...), custom_call_target="tpu_custom_call" | custom-call | flops 600000000 | bytes 8000000 | tf_op jit(solution)/shard_map/rest_warp/pallas_call | solution.py:640
  24.7 0.5 %image.1 = (f32[80,8,128]{2,1,0:T(8,128)S(1)}, f32[72,8,128]{2,1,0:T(8,128)S(1)}, f32[72,8,128]{2,1,0:T(8,128)S(1)}) custom-call(bf16[7,8,8,128]{3,2,1,0:T(8,128)(2,1)S(1)} %collective-permute-done.9.near_m, bf16[7,8,8,128]{3,2,1,0:T(8,128)(2,1)S(1)} %collective-permute-done.10.far_m, bf16[64,8,128]{2,1,0:T(8,128)(2,1)S(1)} %bitcast.25), custom_call_target="tpu_custom_call" | custom-call | flops 400000000 | bytes 8000000 | tf_op jit(solution)/shard_map/image/pallas_call | solution.py:644
  25.2 1.1 %force.1 = f32[3,72,8,128]{3,2,1,0:T(8,128)S(1)} custom-call(f32[80,8,128]{2,1,0:T(8,128)S(1)} %get-tuple-element.44.warped, f32[80,8,128]{2,1,0:T(8,128)S(1)} %get-tuple-element.48.image, f32[72,8,128]{2,1,0:T(8,128)S(1)} %get-tuple-element.49.mean, f32[72,8,128]{2,1,0:T(8,128)S(1)} %get-tuple-element.50.variance), custom_call_target="tpu_custom_call" | custom-call | flops 1000000000 | bytes 8000000 | tf_op jit(solution)/shard_map/force/pallas_call | solution.py:645
  26.7 0.8 %collective-permute-start.11 = (f32[8,8,128]{2,1,0:T(8,128)S(1)}, f32[8,8,128]{2,1,0:T(8,128)S(1)}, u32[]{:S(2)}, u32[]{:S(2)}) collective-permute-start(f32[8,8,128]{2,1,0:T(8,128)S(1)} %slice_bitcast_fusion), channel_id=1, source_target_pairs={{0,4},{1,5},{2,6},{3,7},{4,0},{5,1},{6,2},{7,3},{8,12},{9,13},{10,... | collective-permute-start | bytes 98312 | tf_op jit(solution)/shard_map/ppermute | solution.py:31
  27.6 1.8 %smooth.1 = f32[3,64,8,128]{3,2,1,0:T(8,128)} custom-call(f32[3,72,8,128]{3,2,1,0:T(8,128)S(1)} %force.1), custom_call_target="tpu_custom_call" | custom-call | flops 600000000 | bytes 8000000 | tf_op jit(solution)/shard_map/smooth/pallas_call | solution.py:652
  29.4 2.2 %collective-permute-done.11 = f32[8,8,128]{2,1,0:T(8,128)S(1)} collective-permute-done((f32[8,8,128]{2,1,0:T(8,128)S(1)}, f32[8,8,128]{2,1,0:T(8,128)S(1)}, u32[]{:S(2)}, u32[]{:S(2)}) %collective-permute-start.11) | collective-permute-done | bytes 32800 | tf_op jit(solution)/shard_map/ppermute | solution.py:31
  31.6 0.6 %fusion.1 = f32[8,8,128]{2,1,0:T(8,128)} fusion(f32[8,8,128]{2,1,0:T(8,128)S(1)} %collective-permute-done.11, f32[1,2,8,8,128]{4,3,2,1,0:T(8,128)S(1)} %bitcast.27), kind=kLoop, calls=%fused_computation.4 | loop fusion | flops 16384 | bytes 98304 | tf_op jit(solution)/shard_map/mul | solution.py:653
  (32 shorter events, 0.8 us)
Async XLA Ops:
  0.6 17.0 %copy-start.5 = (bf16[1,64,8,128]{3,2,1,0:T(8,128)(2,1)S(1)}, bf16[1,64,8,128]{3,2,1,0:T(8,128)(2,1)}, u32[]{:S(2)}) copy-start(bf16[1,64,8,128]{3,2,1,0:T(8,128)(2,1)} %param.5) | copy-start | bytes 393220
  0.6 8.2 %collective-permute-start = (bf16[8,8,128]{2,1,0:T(8,128)(2,1)}, bf16[8,8,128]{2,1,0:T(8,128)(2,1)S(1)}, u32[]{:S(2)}, u32[]{:S(2)}) collective-permute-start(bf16[8,8,128]{2,1,0:T(8,128)(2,1)} %template.1), channel_id=1, source_target_pairs={{0,4},{1,5},{2,6},{3,7},{4,0},{5,1},{6,2},{7,3},{8,12},{9,13},{10,... | collective-permute-start | bytes 49160 | tf_op jit(solution)/shard_map/ppermute | solution.py:31
  4.7 1.1 %copy-start = (s32[1,3,64,8,128]{4,3,2,1,0:T(8,128)S(1)}, s32[1,3,64,8,128]{4,3,2,1,0:T(8,128)}, u32[]{:S(2)}) copy-start(s32[1,3,64,8,128]{4,3,2,1,0:T(8,128)} %param.6) | copy-start | bytes 2359300
  5.9 1.0 %copy-start.2 = (bf16[1,3,64,8,128]{4,3,2,1,0:T(8,128)(2,1)S(1)}, bf16[1,3,64,8,128]{4,3,2,1,0:T(8,128)(2,1)}, u32[]{:S(2)}) copy-start(bf16[1,3,64,8,128]{4,3,2,1,0:T(8,128)(2,1)} %param.7) | copy-start | bytes 1179652
  6.9 0.9 %copy-start.4 = (bf16[1,64,8,128]{3,2,1,0:T(8,128)(2,1)S(1)}, bf16[1,64,8,128]{3,2,1,0:T(8,128)(2,1)}, u32[]{:S(2)}) copy-start(bf16[1,64,8,128]{3,2,1,0:T(8,128)(2,1)} %param.5) | copy-start | bytes 393220
  7.8 0.7 %copy-start.6 = (bf16[8,8,128]{2,1,0:T(8,128)(2,1)S(1)}, bf16[8,8,128]{2,1,0:T(8,128)(2,1)}, u32[]{:S(2)}) copy-start(bf16[8,8,128]{2,1,0:T(8,128)(2,1)} %template.1) | copy-start | bytes 49156
  8.5 9.1 %copy-start.1 = (s32[1,3,64,8,128]{4,3,2,1,0:T(8,128)S(1)}, s32[1,3,64,8,128]{4,3,2,1,0:T(8,128)}, u32[]{:S(2)}) copy-start(s32[1,3,64,8,128]{4,3,2,1,0:T(8,128)} %param.6) | copy-start | bytes 2359300
  8.5 9.1 %copy-start.3 = (bf16[1,3,64,8,128]{4,3,2,1,0:T(8,128)(2,1)S(1)}, bf16[1,3,64,8,128]{4,3,2,1,0:T(8,128)(2,1)}, u32[]{:S(2)}) copy-start(bf16[1,3,64,8,128]{4,3,2,1,0:T(8,128)(2,1)} %param.7) | copy-start | bytes 1179652
  8.8 5.2 %collective-permute-start.1 = (bf16[16,8,128]{2,1,0:T(8,128)(2,1)S(1)}, bf16[16,8,128]{2,1,0:T(8,128)(2,1)S(1)}, u32[]{:S(2)}, u32[]{:S(2)}) collective-permute-start(bf16[16,8,128]{2,1,0:T(8,128)(2,1)S(1)} %pad_maximum_fusion), channel_id=1, source_target_pairs={{0,1},{1,0},{2,3},{3,2},{4,5},{5,4},{6,7},{7,6},{8,9},{9,8},{10,11... | collective-permute-start | bytes 98312 | tf_op jit(solution)/shard_map/ppermute | solution.py:31
  10.4 4.8 %collective-permute-start.2 = (bf16[16,8,128]{2,1,0:T(8,128)(2,1)S(1)}, bf16[16,8,128]{2,1,0:T(8,128)(2,1)S(1)}, u32[]{:S(2)}, u32[]{:S(2)}) collective-permute-start(bf16[16,8,128]{2,1,0:T(8,128)(2,1)S(1)} %pad_maximum_fusion), channel_id=1, source_target_pairs={{0,3},{1,2},{2,1},{3,0},{4,7},{5,6},{6,5},{7,4},{8,11},{9,10},{10,... | collective-permute-start | bytes 98312 | tf_op jit(solution)/shard_map/ppermute | solution.py:31
  11.9 3.9 %collective-permute-start.3 = (bf16[16,8,128]{2,1,0:T(8,128)(2,1)S(1)}, bf16[16,8,128]{2,1,0:T(8,128)(2,1)S(1)}, u32[]{:S(2)}, u32[]{:S(2)}) collective-permute-start(bf16[16,8,128]{2,1,0:T(8,128)(2,1)S(1)} %pad_maximum_fusion), channel_id=1, source_target_pairs={{0,2},{1,3},{2,0},{3,1},{4,6},{5,7},{6,4},{7,5},{8,10},{9,11},{10,... | collective-permute-start | bytes 98312 | tf_op jit(solution)/shard_map/ppermute | solution.py:31
  12.4 11.1 %collective-permute-start.9 = (bf16[7,8,8,128]{3,2,1,0:T(8,128)(2,1)S(1)}, bf16[7,8,8,128]{3,2,1,0:T(8,128)(2,1)S(1)}, u32[]{:S(2)}, u32[]{:S(2)}) collective-permute-start(bf16[7,8,8,128]{3,2,1,0:T(8,128)(2,1)S(1)} %get-tuple-element.37), channel_id=1, source_target_pairs={{0,8},{8,0},{16,24},{24,16},{1,9},{9,1},{17,25},{25,17},{2,10},{10... | collective-permute-start | bytes 344072 | tf_op jit(solution)/shard_map/ppermute | solution.py:37
  12.4 11.1 %collective-permute-start.10 = (bf16[7,8,8,128]{3,2,1,0:T(8,128)(2,1)S(1)}, bf16[7,8,8,128]{3,2,1,0:T(8,128)(2,1)S(1)}, u32[]{:S(2)}, u32[]{:S(2)}) collective-permute-start(bf16[7,8,8,128]{3,2,1,0:T(8,128)(2,1)S(1)} %get-tuple-element.38), channel_id=1, source_target_pairs={{0,24},{8,16},{16,8},{24,0},{1,25},{9,17},{17,9},{25,1},{2,26},{10... | collective-permute-start | bytes 344072 | tf_op jit(solution)/shard_map/ppermute | solution.py:43
  15.9 3.5 %collective-permute-start.4 = (bf16[11,8,128]{2,1,0:T(8,128)(2,1)S(1)}, bf16[11,8,128]{2,1,0:T(8,128)(2,1)S(1)}, u32[]{:S(2)}, u32[]{:S(2)}) collective-permute-start(bf16[11,8,128]{2,1,0:T(8,128)(2,1)S(1)} %broadcast_select_fusion.1), channel_id=1, source_target_pairs={{0,8},{8,0},{16,24},{24,16},{1,9},{9,1},{17,25},{25,17},{2,10},{10... | collective-permute-start | bytes 67592 | tf_op jit(solution)/shard_map/ppermute | solution.py:37
  16.0 3.4 %collective-permute-start.5 = (bf16[11,8,128]{2,1,0:T(8,128)(2,1)S(1)}, bf16[11,8,128]{2,1,0:T(8,128)(2,1)S(1)}, u32[]{:S(2)}, u32[]{:S(2)}) collective-permute-start(bf16[11,8,128]{2,1,0:T(8,128)(2,1)S(1)} %get-tuple-element.56), channel_id=1, source_target_pairs={{0,24},{8,16},{16,8},{24,0},{1,25},{9,17},{17,9},{25,1},{2,26},{10... | collective-permute-start | bytes 67592 | tf_op jit(solution)/shard_map/ppermute | solution.py:43
  19.9 6.5 %collective-permute-start.6 = (f32[16,8,128]{2,1,0:T(8,128)S(1)}, f32[16,8,128]{2,1,0:T(8,128)S(1)}, u32[]{:S(2)}, u32[]{:S(2)}) collective-permute-start(f32[16,8,128]{2,1,0:T(8,128)S(1)} %get-tuple-element.34), channel_id=1, source_target_pairs={{0,3},{1,2},{2,1},{3,0},{4,7},{5,6},{6,5},{7,4},{8,11},{9,10},{10,... | collective-permute-start | bytes 196616 | tf_op jit(solution)/shard_map/ppermute | solution.py:31
  21.4 5.2 %collective-permute-start.7 = (f32[16,8,128]{2,1,0:T(8,128)S(1)}, f32[16,8,128]{2,1,0:T(8,128)S(1)}, u32[]{:S(2)}, u32[]{:S(2)}) collective-permute-start(f32[16,8,128]{2,1,0:T(8,128)S(1)} %get-tuple-element.35), channel_id=1, source_target_pairs={{0,1},{1,0},{2,3},{3,2},{4,5},{5,4},{6,7},{7,6},{8,9},{9,8},{10,11... | collective-permute-start | bytes 196616 | tf_op jit(solution)/shard_map/ppermute | solution.py:31
  22.4 4.3 %collective-permute-start.8 = (f32[16,8,128]{2,1,0:T(8,128)S(1)}, f32[16,8,128]{2,1,0:T(8,128)S(1)}, u32[]{:S(2)}, u32[]{:S(2)}) collective-permute-start(f32[16,8,128]{2,1,0:T(8,128)S(1)} %get-tuple-element.36), channel_id=1, source_target_pairs={{0,2},{1,3},{2,0},{3,1},{4,6},{5,7},{6,4},{7,5},{8,10},{9,11},{10,... | collective-permute-start | bytes 196616 | tf_op jit(solution)/shard_map/ppermute | solution.py:31
  26.7 4.9 %collective-permute-start.11 = (f32[8,8,128]{2,1,0:T(8,128)S(1)}, f32[8,8,128]{2,1,0:T(8,128)S(1)}, u32[]{:S(2)}, u32[]{:S(2)}) collective-permute-start(f32[8,8,128]{2,1,0:T(8,128)S(1)} %slice_bitcast_fusion), channel_id=1, source_target_pairs={{0,4},{1,5},{2,6},{3,7},{4,0},{5,1},{6,2},{7,3},{8,12},{9,13},{10,... | collective-permute-start | bytes 98312 | tf_op jit(solution)/shard_map/ppermute | solution.py:31

commit v6 on v5

--- a/solution.py
+++ b/solution.py
@@ -163,12 +163,26 @@
     return block * quarter + mirrored(apart // PEERS, quarter)
 
 
-def build_pack(depth, rows, cols, share):
-    def kernel(template, shifts, fractions, subjects, near, far, mine, whole, parts, done):
+def build_copy(share, rows, cols):
+    def kernel(template, mine):
+        mine[...] = template[...]
+
+    return pl.pallas_call(
+        kernel,
+        out_shape=jax.ShapeDtypeStruct((share, rows, cols), bf16),
+        in_specs=vmem_specs(1),
+        out_specs=vmem_specs(1)[0],
+        compiler_params=pltpu.CompilerParams(vmem_limit_bytes=VMEM_LIMIT),
+        cost_estimate=pl.CostEstimate(flops=1_000, bytes_accessed=50_000, transcendentals=0),
+        name="own_share",
+    )
+
+
+def build_pack(depth, rows, cols):
+    def kernel(shifts, fractions, subjects, near, far, whole, parts, done):
         odd = lax.axis_index("gz") % 2 == 1
-        starts = (0, depth - EDGE)
-        copies = [pltpu.make_async_copy(template, mine, done.at[6])]
-        for end, start in enumerate(starts):
+        copies = []
+        for end, start in enumerate((0, depth - EDGE)):
             at = pl.ds(start, EDGE)
             copies.append(pltpu.make_async_copy(shifts.at[:, at], whole.at[end], done.at[3 * end]))
             copies.append(
@@ -182,26 +196,25 @@
         for copy in copies:
             copy.wait()
         for axis in range(7):
-            if axis < 3:
-                low, high = whole[0, axis].astype(f32), whole[1, axis].astype(f32)
-            else:
-                low, high = parts[0, axis - 3].astype(f32), parts[1, axis - 3].astype(f32)
+            low, high = [
+                (whole[end, axis] if axis < 3 else parts[end, axis - 3]).astype(f32)
+                for end in range(2)
+            ]
             near[axis] = jnp.where(odd, low, high).astype(bf16)
             far[axis] = jnp.where(odd, high, low).astype(bf16)
 
-    any_spec = pl.BlockSpec(memory_space=pl.ANY)
     message = jax.ShapeDtypeStruct((7, EDGE, rows, cols), bf16)
     return pl.pallas_call(
         kernel,
-        out_shape=[message, message, jax.ShapeDtypeStruct((share, rows, cols), bf16)],
-        in_specs=[any_spec] * 4,
-        out_specs=vmem_specs(3),
+        out_shape=[message, message],
+        in_specs=[pl.BlockSpec(memory_space=pl.ANY)] * 3,
+        out_specs=vmem_specs(2),
         scratch_shapes=[
             pltpu.VMEM((2, 3, EDGE, rows, cols), jnp.int32),
             pltpu.VMEM((2, 4, EDGE, rows, cols), bf16),
-            pltpu.SemaphoreType.DMA((7,)),
+            pltpu.SemaphoreType.DMA((6,)),
         ],
-        compiler_params=pltpu.CompilerParams(vmem_limit_bytes=VMEM_LIMIT),
+        compiler_params=pltpu.CompilerParams(vmem_limit_bytes=62 * 1024 * 1024),
         cost_estimate=pl.CostEstimate(flops=1_000_000, bytes_accessed=2_000_000, transcendentals=0),
         name="pack",
     )
@@ -608,9 +621,8 @@
     subject, shift, fraction = subjects[0], shifts[0], fractions[0]
 
     arrived = swap(template, "subj", bits[-1])
-    to_near, to_far, mine = build_pack(depth, rows, cols, share)(
-        template, shift, fraction, subject
-    )
+    mine = build_copy(share, rows, cols)(template)
+    to_near, to_far = build_pack(depth, rows, cols)(shift, fraction, subject)
     pieces = jnp.concatenate([mine, arrived], axis=0)
     pieces, to_near, to_far = lax.optimization_barrier((pieces, to_near, to_far))
     near_m, far_m = swap_near(to_near, "gz"), swap_far(to_far, "gz")

time: 32.5 us -> 31 us (0.954)
  local copies, waits for them, and re-layouts: 3.8 us -> 0.81 us
  starting transfers between devices: 15.3 us -> 16.9 us
  waiting for transfers between devices: 4.36 us -> 2.82 us
  Pallas kernels: 7.27 us -> 8.76 us
    unnamed x17 -> x11, local copies, waits for them, and re-layouts: 3.78 us -> 0.79 us
    ppermute x8, waiting for transfers between devices: 4.35 us -> 2.81 us  [swap(): return lax.ppermute(block, axis, [(i, i ^ bit) for i in range(count)])]
    ppermute x8, starting transfers between devices: 12.1 us -> 13.6 us  [swap(): return lax.ppermute(block, axis, [(i, i ^ bit) for i in range(count)])]
    pallas_call x1 -> x2, Pallas kernels: 0.28 us -> 1.76 us  [the longest x1 1.76 us: per_device(): to_near, to_far = build_pack(depth, rows, cols)(shift, fraction, subject)]
  transfers between devices with their start and end apart: 12 -> 12, of which waited for: 5 -> 5; matrix products, arithmetic and copies ran while one was open for 0% -> 0% of each run, Pallas kernels for 23% -> 29%
where the time goes in v6:
time: 31 us; the launch traced here: 30.7 us
  starting transfers between devices  16.9 us (55%)
  Pallas kernels  8.76 us (28%)
  waiting for transfers between devices  2.82 us (9%)
  local copies, waits for them, and re-layouts  0.81 us (3%)
  between operations  0.79 us (3%)
  other arithmetic  0.67 us (2%)
    ppermute x8, starting transfers between devices, swap(): return lax.ppermute(block, axis, [(i, i ^ bit) for i in range(count)])  13.6 us
    ppermute x2, starting transfers between devices, swap_far(): lax.ppermute(block, axis, [(i, (i + 1 if i % 2 else i - 1) % count) for i...  3.21 us
    ppermute x8, waiting for transfers between devices, swap(): return lax.ppermute(block, axis, [(i, i ^ bit) for i in range(count)])  2.81 us
    pallas_call x1, Pallas kernels, per_device(): velocity, = build_smooth(depth, rows, cols)(force)  1.84 us
    pallas_call x1, Pallas kernels, per_device(): build_inner_warp(depth, rows, cols, members)  1.82 us
    pallas_call x1, Pallas kernels, per_device(): to_near, to_far = build_pack(depth, rows, cols)(shift, fraction, subject)  1.76 us
    pallas_call x1, Pallas kernels, per_device(): build_rest_warp(depth, rows, cols, members, groups)  1.23 us
    pallas_call x1, Pallas kernels, per_device(): build_force(depth, rows, cols, groups)(warped, image, mean, variance)  1.12 us
  transfers between devices with their start and end apart: 12, of which 5 were waited for; matrix products, arithmetic and copies ran while one was open for 0% of the time, Pallas kernels for 29%

profile of v6, /device:TPU:0, one launch (start us, length us, event | category | flops | bytes accessed | tf_op | source)
XLA Modules:
  0.0 30.7 jit_solution(9124347620308646774)
XLA Ops:
  0.7 4.1 %collective-permute-start = (bf16[8,8,128]{2,1,0:T(8,128)(2,1)}, bf16[8,8,128]{2,1,0:T(8,128)(2,1)S(1)}, u32[]{:S(2)}, u32[]{:S(2)}) collective-permute-start(bf16[8,8,128]{2,1,0:T(8,128)(2,1)} %template.1), channel_id=1, source_target_pairs={{0,4},{1,5},{2,6},{3,7},{4,0},{5,1},{6,2},{7,3},{8,12},{9,13},{10,... | collective-permute-start | bytes 49160 | tf_op jit(solution)/shard_map/ppermute | solution.py:31
  4.8 0.7 %copy-done.3 = bf16[8,8,128]{2,1,0:T(8,128)(2,1)S(1)} copy-done((bf16[8,8,128]{2,1,0:T(8,128)(2,1)S(1)}, bf16[8,8,128]{2,1,0:T(8,128)(2,1)}, u32[]{:S(2)}) %copy-start.3) | copy-done | bytes 16408
  5.5 1.8 %pack.1 = (bf16[7,8,8,128]{3,2,1,0:T(8,128)(2,1)}, bf16[7,8,8,128]{3,2,1,0:T(8,128)(2,1)}) custom-call(s32[3,64,8,128]{3,2,1,0:T(8,128)} %bitcast.13, bf16[3,64,8,128]{3,2,1,0:T(8,128)(2,1)} %bitcast.17, bf16[64,8,128]{2,1,0:T(8,128)(2,1)} %bitcast.21), custom_call_target="tpu_custom_call" | custom-call | flops 1000000 | bytes 2000000 | tf_op jit(solution)/shard_map/pack/pallas_call | solution.py:625
  7.3 1.6 %collective-permute-start.1 = (bf16[16,8,128]{2,1,0:T(8,128)(2,1)S(1)}, bf16[16,8,128]{2,1,0:T(8,128)(2,1)S(1)}, u32[]{:S(2)}, u32[]{:S(2)}) collective-permute-start(bf16[16,8,128]{2,1,0:T(8,128)(2,1)S(1)} %pad_maximum_fusion), channel_id=1, source_target_pairs={{0,1},{1,0},{2,3},{3,2},{4,5},{5,4},{6,7},{7,6},{8,9},{9,8},{10,11... | collective-permute-start | bytes 98312 | tf_op jit(solution)/shard_map/ppermute | solution.py:31
  8.9 1.5 %collective-permute-start.2 = (bf16[16,8,128]{2,1,0:T(8,128)(2,1)S(1)}, bf16[16,8,128]{2,1,0:T(8,128)(2,1)S(1)}, u32[]{:S(2)}, u32[]{:S(2)}) collective-permute-start(bf16[16,8,128]{2,1,0:T(8,128)(2,1)S(1)} %pad_maximum_fusion), channel_id=1, source_target_pairs={{0,3},{1,2},{2,1},{3,0},{4,7},{5,6},{6,5},{7,4},{8,11},{9,10},{10,... | collective-permute-start | bytes 98312 | tf_op jit(solution)/shard_map/ppermute | solution.py:31
  10.4 0.4 %collective-permute-start.3 = (bf16[16,8,128]{2,1,0:T(8,128)(2,1)S(1)}, bf16[16,8,128]{2,1,0:T(8,128)(2,1)S(1)}, u32[]{:S(2)}, u32[]{:S(2)}) collective-permute-start(bf16[16,8,128]{2,1,0:T(8,128)(2,1)S(1)} %pad_maximum_fusion), channel_id=1, source_target_pairs={{0,2},{1,3},{2,0},{3,1},{4,6},{5,7},{6,4},{7,5},{8,10},{9,11},{10,... | collective-permute-start | bytes 98312 | tf_op jit(solution)/shard_map/ppermute | solution.py:31
  10.9 1.6 %collective-permute-start.10 = (bf16[7,8,8,128]{3,2,1,0:T(8,128)(2,1)}, bf16[7,8,8,128]{3,2,1,0:T(8,128)(2,1)S(1)}, u32[]{:S(2)}, u32[]{:S(2)}) collective-permute-start(bf16[7,8,8,128]{3,2,1,0:T(8,128)(2,1)} %get-tuple-element.36), channel_id=1, source_target_pairs={{0,24},{8,16},{16,8},{24,0},{1,25},{9,17},{17,9},{25,1},{2,26},{10... | collective-permute-start | bytes 344072 | tf_op jit(solution)/shard_map/ppermute | solution.py:43
  12.5 1.2 %collective-permute-done.2 = bf16[16,8,128]{2,1,0:T(8,128)(2,1)S(1)} collective-permute-done((bf16[16,8,128]{2,1,0:T(8,128)(2,1)S(1)}, bf16[16,8,128]{2,1,0:T(8,128)(2,1)S(1)}, u32[]{:S(2)}, u32[]{:S(2)}) %collective-permute-start.2) | collective-permute-done | bytes 32800 | tf_op jit(solution)/shard_map/ppermute | solution.py:31
  13.7 0.6 %collective-permute-done.3 = bf16[16,8,128]{2,1,0:T(8,128)(2,1)S(1)} collective-permute-done((bf16[16,8,128]{2,1,0:T(8,128)(2,1)S(1)}, bf16[16,8,128]{2,1,0:T(8,128)(2,1)S(1)}, u32[]{:S(2)}, u32[]{:S(2)}) %collective-permute-start.3) | collective-permute-done | bytes 32800 | tf_op jit(solution)/shard_map/ppermute | solution.py:31
  14.5 1.6 %collective-permute-start.5 = (bf16[11,8,128]{2,1,0:T(8,128)(2,1)S(1)}, bf16[11,8,128]{2,1,0:T(8,128)(2,1)S(1)}, u32[]{:S(2)}, u32[]{:S(2)}) collective-permute-start(bf16[11,8,128]{2,1,0:T(8,128)(2,1)S(1)} %get-tuple-element.54), channel_id=1, source_target_pairs={{0,24},{8,16},{16,8},{24,0},{1,25},{9,17},{17,9},{25,1},{2,26},{10... | collective-permute-start | bytes 67592 | tf_op jit(solution)/shard_map/ppermute | solution.py:43
  16.1 1.8 %inner_warp.1 = (f32[48,8,128]{2,1,0:T(8,128)S(1)}, f32[48,8,128]{2,1,0:T(8,128)S(1)}, f32[6,70,8,128]{3,2,1,0:T(8,128)S(1)}) custom-call(bf16[64,8,128]{2,1,0:T(8,128)(2,1)S(1)} %constant_dynamic-update-slice_fusion.pieces, s32[3,64,8,128]{3,2,1,0:T(8,128)S(1)} %bitcast.14, bf16[3,64,8,128]{3,2,1,0:T(8,128)(2,1)S(1)} %bitcast.18, ...), custom_call_target="tpu_custom_call" | custom-call | flops 1000000000 | bytes 8000000 | tf_op jit(solution)/shard_map/inner_warp/pallas_call | solution.py:646
  17.9 0.5 %end_warp.1 = (f32[16,8,128]{2,1,0:T(8,128)S(1)}, f32[16,8,128]{2,1,0:T(8,128)S(1)}, f32[16,8,128]{2,1,0:T(8,128)S(1)}, f32[5,8,128]{2,1,0:T(8,128)S(1)}, f32[6,42,8,128]{3,2,1,0:T(8,128)S(1)}) custom-call(bf16[11,8,128]{2,1,0:T(8,128)(2,1)S(1)} %get-tuple-element.56.low_t, bf16[11,8,128]{2,1,0:T(8,128)(2,1)S(1)} %get-tuple-element.55.high_t, ...), custom_call_target="tpu_custom_call" | custom-call | flops 300000000 | bytes 8000000 | tf_op jit(solution)/shard_map/end_warp/pallas_call | solution.py:647
  18.4 1.5 %collective-permute-start.6 = (f32[16,8,128]{2,1,0:T(8,128)S(1)}, f32[16,8,128]{2,1,0:T(8,128)S(1)}, u32[]{:S(2)}, u32[]{:S(2)}) collective-permute-start(f32[16,8,128]{2,1,0:T(8,128)S(1)} %get-tuple-element.32), channel_id=1, source_target_pairs={{0,3},{1,2},{2,1},{3,0},{4,7},{5,6},{6,5},{7,4},{8,11},{9,10},{10,... | collective-permute-start | bytes 196616 | tf_op jit(solution)/shard_map/ppermute | solution.py:31
  19.9 1.1 %collective-permute-start.7 = (f32[16,8,128]{2,1,0:T(8,128)S(1)}, f32[16,8,128]{2,1,0:T(8,128)S(1)}, u32[]{:S(2)}, u32[]{:S(2)}) collective-permute-start(f32[16,8,128]{2,1,0:T(8,128)S(1)} %get-tuple-element.33), channel_id=1, source_target_pairs={{0,1},{1,0},{2,3},{3,2},{4,5},{5,4},{6,7},{7,6},{8,9},{9,8},{10,11... | collective-permute-start | bytes 196616 | tf_op jit(solution)/shard_map/ppermute | solution.py:31
  20.9 1.0 %collective-permute-start.8 = (f32[16,8,128]{2,1,0:T(8,128)S(1)}, f32[16,8,128]{2,1,0:T(8,128)S(1)}, u32[]{:S(2)}, u32[]{:S(2)}) collective-permute-start(f32[16,8,128]{2,1,0:T(8,128)S(1)} %get-tuple-element.34), channel_id=1, source_target_pairs={{0,2},{1,3},{2,0},{3,1},{4,6},{5,7},{6,4},{7,5},{8,10},{9,11},{10,... | collective-permute-start | bytes 196616 | tf_op jit(solution)/shard_map/ppermute | solution.py:31
  22.0 1.2 %rest_warp.1 = (f32[80,8,128]{2,1,0:T(8,128)S(1)}, f32[16,8,128]{2,1,0:T(8,128)S(1)}) custom-call(f32[6,70,8,128]{3,2,1,0:T(8,128)S(1)} %get-tuple-element.37.moved, f32[6,42,8,128]{3,2,1,0:T(8,128)S(1)} %get-tuple-element.38.moved_ends, f32[48,8,128]{2,1,0:T(8,128)S(1)} %get-tuple-element.39.sent, f32[5,8,128]{2,1,0:T(8,128)S(1)} %get-tuple-element.40.ends, ...), custom_call_target="tpu_custom_call" | custom-call | flops 600000000 | bytes 8000000 | tf_op jit(solution)/shard_map/rest_warp/pallas_call | solution.py:652
  23.2 0.5 %image.1 = (f32[80,8,128]{2,1,0:T(8,128)S(1)}, f32[72,8,128]{2,1,0:T(8,128)S(1)}, f32[72,8,128]{2,1,0:T(8,128)S(1)}) custom-call(bf16[7,8,8,128]{3,2,1,0:T(8,128)(2,1)S(1)} %collective-permute-done.9.near_m, bf16[7,8,8,128]{3,2,1,0:T(8,128)(2,1)S(1)} %collective-permute-done.10.far_m, bf16[64,8,128]{2,1,0:T(8,128)(2,1)S(1)} %bitcast.25), custom_call_target="tpu_custom_call" | custom-call | flops 400000000 | bytes 8000000 | tf_op jit(solution)/shard_map/image/pallas_call | solution.py:656
  23.7 1.1 %force.1 = f32[3,72,8,128]{3,2,1,0:T(8,128)S(1)} custom-call(f32[80,8,128]{2,1,0:T(8,128)S(1)} %get-tuple-element.42.warped, f32[80,8,128]{2,1,0:T(8,128)S(1)} %get-tuple-element.46.image, f32[72,8,128]{2,1,0:T(8,128)S(1)} %get-tuple-element.47.mean, f32[72,8,128]{2,1,0:T(8,128)S(1)} %get-tuple-element.48.variance), custom_call_target="tpu_custom_call" | custom-call | flops 1000000000 | bytes 8000000 | tf_op jit(solution)/shard_map/force/pallas_call | solution.py:657
  24.9 0.2 collective-permute-done.7
  25.0 0.1 collective-permute-done.8
  25.2 2.4 %collective-permute-start.11 = (f32[8,8,128]{2,1,0:T(8,128)S(1)}, f32[8,8,128]{2,1,0:T(8,128)S(1)}, u32[]{:S(2)}, u32[]{:S(2)}) collective-permute-start(f32[8,8,128]{2,1,0:T(8,128)S(1)} %slice_bitcast_fusion), channel_id=1, source_target_pairs={{0,4},{1,5},{2,6},{3,7},{4,0},{5,1},{6,2},{7,3},{8,12},{9,13},{10,... | collective-permute-start | bytes 98312 | tf_op jit(solution)/shard_map/ppermute | solution.py:31
  27.6 1.8 %smooth.1 = f32[3,64,8,128]{3,2,1,0:T(8,128)} custom-call(f32[3,72,8,128]{3,2,1,0:T(8,128)S(1)} %force.1), custom_call_target="tpu_custom_call" | custom-call | flops 600000000 | bytes 8000000 | tf_op jit(solution)/shard_map/smooth/pallas_call | solution.py:664
  29.4 0.7 %collective-permute-done.11 = f32[8,8,128]{2,1,0:T(8,128)S(1)} collective-permute-done((f32[8,8,128]{2,1,0:T(8,128)S(1)}, f32[8,8,128]{2,1,0:T(8,128)S(1)}, u32[]{:S(2)}, u32[]{:S(2)}) %collective-permute-start.11) | collective-permute-done | bytes 32800 | tf_op jit(solution)/shard_map/ppermute | solution.py:31
  30.1 0.6 %fusion.1 = f32[8,8,128]{2,1,0:T(8,128)} fusion(f32[8,8,128]{2,1,0:T(8,128)S(1)} %collective-permute-done.11, f32[1,2,8,8,128]{4,3,2,1,0:T(8,128)S(1)} %bitcast.27), kind=kLoop, calls=%fused_computation.4 | loop fusion | flops 16384 | bytes 98304 | tf_op jit(solution)/shard_map/mul | solution.py:665
  (27 shorter events, 0.2 us)
Async XLA Ops:
  0.6 15.5 %copy-start = (s32[1,3,64,8,128]{4,3,2,1,0:T(8,128)S(1)}, s32[1,3,64,8,128]{4,3,2,1,0:T(8,128)}, u32[]{:S(2)}) copy-start(s32[1,3,64,8,128]{4,3,2,1,0:T(8,128)} %param.6) | copy-start | bytes 2359300
  0.6 15.4 %copy-start.1 = (bf16[1,3,64,8,128]{4,3,2,1,0:T(8,128)(2,1)S(1)}, bf16[1,3,64,8,128]{4,3,2,1,0:T(8,128)(2,1)}, u32[]{:S(2)}) copy-start(bf16[1,3,64,8,128]{4,3,2,1,0:T(8,128)(2,1)} %param.7) | copy-start | bytes 1179652
  0.7 15.4 %copy-start.2 = (bf16[1,64,8,128]{3,2,1,0:T(8,128)(2,1)S(1)}, bf16[1,64,8,128]{3,2,1,0:T(8,128)(2,1)}, u32[]{:S(2)}) copy-start(bf16[1,64,8,128]{3,2,1,0:T(8,128)(2,1)} %param.5) | copy-start | bytes 393220
  0.7 6.6 %collective-permute-start = (bf16[8,8,128]{2,1,0:T(8,128)(2,1)}, bf16[8,8,128]{2,1,0:T(8,128)(2,1)S(1)}, u32[]{:S(2)}, u32[]{:S(2)}) collective-permute-start(bf16[8,8,128]{2,1,0:T(8,128)(2,1)} %template.1), channel_id=1, source_target_pairs={{0,4},{1,5},{2,6},{3,7},{4,0},{5,1},{6,2},{7,3},{8,12},{9,13},{10,... | collective-permute-start | bytes 49160 | tf_op jit(solution)/shard_map/ppermute | solution.py:31
  4.8 0.8 %copy-start.3 = (bf16[8,8,128]{2,1,0:T(8,128)(2,1)S(1)}, bf16[8,8,128]{2,1,0:T(8,128)(2,1)}, u32[]{:S(2)}) copy-start(bf16[8,8,128]{2,1,0:T(8,128)(2,1)} %template.1) | copy-start | bytes 49156
  7.3 5.2 %collective-permute-start.1 = (bf16[16,8,128]{2,1,0:T(8,128)(2,1)S(1)}, bf16[16,8,128]{2,1,0:T(8,128)(2,1)S(1)}, u32[]{:S(2)}, u32[]{:S(2)}) collective-permute-start(bf16[16,8,128]{2,1,0:T(8,128)(2,1)S(1)} %pad_maximum_fusion), channel_id=1, source_target_pairs={{0,1},{1,0},{2,3},{3,2},{4,5},{5,4},{6,7},{7,6},{8,9},{9,8},{10,11... | collective-permute-start | bytes 98312 | tf_op jit(solution)/shard_map/ppermute | solution.py:31
  8.9 4.8 %collective-permute-start.2 = (bf16[16,8,128]{2,1,0:T(8,128)(2,1)S(1)}, bf16[16,8,128]{2,1,0:T(8,128)(2,1)S(1)}, u32[]{:S(2)}, u32[]{:S(2)}) collective-permute-start(bf16[16,8,128]{2,1,0:T(8,128)(2,1)S(1)} %pad_maximum_fusion), channel_id=1, source_target_pairs={{0,3},{1,2},{2,1},{3,0},{4,7},{5,6},{6,5},{7,4},{8,11},{9,10},{10,... | collective-permute-start | bytes 98312 | tf_op jit(solution)/shard_map/ppermute | solution.py:31
  10.4 3.9 %collective-permute-start.3 = (bf16[16,8,128]{2,1,0:T(8,128)(2,1)S(1)}, bf16[16,8,128]{2,1,0:T(8,128)(2,1)S(1)}, u32[]{:S(2)}, u32[]{:S(2)}) collective-permute-start(bf16[16,8,128]{2,1,0:T(8,128)(2,1)S(1)} %pad_maximum_fusion), channel_id=1, source_target_pairs={{0,2},{1,3},{2,0},{3,1},{4,6},{5,7},{6,4},{7,5},{8,10},{9,11},{10,... | collective-permute-start | bytes 98312 | tf_op jit(solution)/shard_map/ppermute | solution.py:31
  10.9 11.1 %collective-permute-start.9 = (bf16[7,8,8,128]{3,2,1,0:T(8,128)(2,1)}, bf16[7,8,8,128]{3,2,1,0:T(8,128)(2,1)S(1)}, u32[]{:S(2)}, u32[]{:S(2)}) collective-permute-start(bf16[7,8,8,128]{3,2,1,0:T(8,128)(2,1)} %get-tuple-element.35), channel_id=1, source_target_pairs={{0,8},{8,0},{16,24},{24,16},{1,9},{9,1},{17,25},{25,17},{2,10},{10... | collective-permute-start | bytes 344072 | tf_op jit(solution)/shard_map/ppermute | solution.py:37
  10.9 11.1 %collective-permute-start.10 = (bf16[7,8,8,128]{3,2,1,0:T(8,128)(2,1)}, bf16[7,8,8,128]{3,2,1,0:T(8,128)(2,1)S(1)}, u32[]{:S(2)}, u32[]{:S(2)}) collective-permute-start(bf16[7,8,8,128]{3,2,1,0:T(8,128)(2,1)} %get-tuple-element.36), channel_id=1, source_target_pairs={{0,24},{8,16},{16,8},{24,0},{1,25},{9,17},{17,9},{25,1},{2,26},{10... | collective-permute-start | bytes 344072 | tf_op jit(solution)/shard_map/ppermute | solution.py:43
  14.4 3.5 %collective-permute-start.4 = (bf16[11,8,128]{2,1,0:T(8,128)(2,1)S(1)}, bf16[11,8,128]{2,1,0:T(8,128)(2,1)S(1)}, u32[]{:S(2)}, u32[]{:S(2)}) collective-permute-start(bf16[11,8,128]{2,1,0:T(8,128)(2,1)S(1)} %broadcast_select_fusion.1), channel_id=1, source_target_pairs={{0,8},{8,0},{16,24},{24,16},{1,9},{9,1},{17,25},{25,17},{2,10},{10... | collective-permute-start | bytes 67592 | tf_op jit(solution)/shard_map/ppermute | solution.py:37
  14.5 3.5 %collective-permute-start.5 = (bf16[11,8,128]{2,1,0:T(8,128)(2,1)S(1)}, bf16[11,8,128]{2,1,0:T(8,128)(2,1)S(1)}, u32[]{:S(2)}, u32[]{:S(2)}) collective-permute-start(bf16[11,8,128]{2,1,0:T(8,128)(2,1)S(1)} %get-tuple-element.54), channel_id=1, source_target_pairs={{0,24},{8,16},{16,8},{24,0},{1,25},{9,17},{17,9},{25,1},{2,26},{10... | collective-permute-start | bytes 67592 | tf_op jit(solution)/shard_map/ppermute | solution.py:43
  18.4 6.5 %collective-permute-start.6 = (f32[16,8,128]{2,1,0:T(8,128)S(1)}, f32[16,8,128]{2,1,0:T(8,128)S(1)}, u32[]{:S(2)}, u32[]{:S(2)}) collective-permute-start(f32[16,8,128]{2,1,0:T(8,128)S(1)} %get-tuple-element.32), channel_id=1, source_target_pairs={{0,3},{1,2},{2,1},{3,0},{4,7},{5,6},{6,5},{7,4},{8,11},{9,10},{10,... | collective-permute-start | bytes 196616 | tf_op jit(solution)/shard_map/ppermute | solution.py:31
  19.9 5.2 %collective-permute-start.7 = (f32[16,8,128]{2,1,0:T(8,128)S(1)}, f32[16,8,128]{2,1,0:T(8,128)S(1)}, u32[]{:S(2)}, u32[]{:S(2)}) collective-permute-start(f32[16,8,128]{2,1,0:T(8,128)S(1)} %get-tuple-element.33), channel_id=1, source_target_pairs={{0,1},{1,0},{2,3},{3,2},{4,5},{5,4},{6,7},{7,6},{8,9},{9,8},{10,11... | collective-permute-start | bytes 196616 | tf_op jit(solution)/shard_map/ppermute | solution.py:31
  20.9 4.3 %collective-permute-start.8 = (f32[16,8,128]{2,1,0:T(8,128)S(1)}, f32[16,8,128]{2,1,0:T(8,128)S(1)}, u32[]{:S(2)}, u32[]{:S(2)}) collective-permute-start(f32[16,8,128]{2,1,0:T(8,128)S(1)} %get-tuple-element.34), channel_id=1, source_target_pairs={{0,2},{1,3},{2,0},{3,1},{4,6},{5,7},{6,4},{7,5},{8,10},{9,11},{10,... | collective-permute-start | bytes 196616 | tf_op jit(solution)/shard_map/ppermute | solution.py:31
  25.2 4.9 %collective-permute-start.11 = (f32[8,8,128]{2,1,0:T(8,128)S(1)}, f32[8,8,128]{2,1,0:T(8,128)S(1)}, u32[]{:S(2)}, u32[]{:S(2)}) collective-permute-start(f32[8,8,128]{2,1,0:T(8,128)S(1)} %slice_bitcast_fusion), channel_id=1, source_target_pairs={{0,4},{1,5},{2,6},{3,7},{4,0},{5,1},{6,2},{7,3},{8,12},{9,13},{10,... | collective-permute-start | bytes 98312 | tf_op jit(solution)/shard_map/ppermute | solution.py:31

commit v7 on v6

--- a/solution.py
+++ b/solution.py
@@ -253,7 +253,7 @@
             send[i] = subjects[z].astype(f32) - out
             return carry
 
-        lax.fori_loop(0, away, body, 0, unroll=6)
+        lax.fori_loop(0, away, body, 0, unroll=8)
 
     part = (away, rows, cols)
     return local_call(
@@ -262,61 +262,70 @@
     )
 
 
+def end_planes():
+    return 3 * SHIFT + 1, 3 * SHIFT + 2
+
+
 def build_end_warp(depth, rows, cols, members, groups):
     share = depth // members
-    quarter, kept = members // PEERS, depth // PEERS
-    away = depth - kept
-    inner = SHIFT + EDGE
-    planes = HALO + inner
-
-    def kernel(
-        low_t, high_t, near_t, far_t, shifts, fractions, subjects, send_in, *outs_and_scratch
-    ):
-        *sends, ends, shifted, slab = outs_and_scratch
+    kept = depth // PEERS
+    below, above = end_planes()
+    planes = below + above
+
+    def kernel(low_t, high_t, near_t, far_t, shifts, fractions, subjects, send_in, *outs_and_scratch):
+        *sends, ends, slab, shifted = outs_and_scratch
         odd = lax.axis_index("gz") % 2 == 1
         me = lax.axis_index("subj")
         inside = has_far(lax.axis_index("gz"), groups)
+        near, far = near_t[...].astype(f32), jnp.where(inside, far_t[...].astype(f32), 0.0)
+        front, back = below - SHIFT, above - SHIFT - 1
+        slab[0:SHIFT] = jnp.where(odd, near, far)[HALO - SHIFT :]
+        slab[SHIFT:below] = low_t[0:front].astype(f32)
+        slab[below : below + back] = high_t[HALO - back : HALO].astype(f32)
+        slab[below + back : planes] = jnp.where(odd, far, near)[: SHIFT + 1]
+        move_columns(slab, shifted, 0, planes)
+        for number, send in enumerate(sends):
+            send[...] = send_in[number * kept : (number + 1) * kept]
+        for number, z in enumerate(end_slices(depth)):
+            plane = z if z < SHIFT else below + z - (depth - SHIFT - 1)
+            out = warp_slice(shifted, plane, *slice_fields(shifts, fractions, z))
+            ends[number] = out
+            residual = subjects[z].astype(f32) - out
+            apart = me ^ (z // share)
+            index = (apart // PEERS) * share + z % share
+            for k, send in enumerate(sends, 1):
+
+                @pl.when(apart % PEERS == k)
+                def _():
+                    send[index] = residual
+
+    part = (kept, rows, cols)
+    count = len(end_slices(depth))
+    return local_call(
+        kernel, "end_warp", [part] * (PEERS - 1) + [(count, rows, cols)], 8,
+        [(planes, rows, cols), (TAPS, planes, rows, cols)], 300_000_000,
+    )
+
+
+def build_rest_warp(depth, rows, cols, members, groups):
+    share = depth // members
+    kept = depth // PEERS
+    planes = HALO + SHIFT + EDGE
+
+    def kernel(
+        moved, low_t, high_t, near_t, far_t, sent, ends, near_m, far_m, shifts, fractions, subjects,
+        warped, keep, slab, moved_ends,
+    ):
+        me = lax.axis_index("subj")
+        odd = lax.axis_index("gz") % 2 == 1
+        inside = has_far(lax.axis_index("gz"), groups)
+        inner = SHIFT + EDGE
         near, far = near_t[...].astype(f32), jnp.where(inside, far_t[...].astype(f32), 0.0)
         slab[0:HALO] = jnp.where(odd, near, far)
         slab[HALO:planes] = low_t[0:inner].astype(f32)
         slab[planes : planes + inner] = high_t[HALO - inner : HALO].astype(f32)
         slab[planes + inner : 2 * planes] = jnp.where(odd, far, near)
-        move_columns(slab, shifted, 0, 2 * planes)
-        for number, send in enumerate(sends):
-            send[...] = send_in[number * kept : (number + 1) * kept]
-        for number, z in enumerate(end_slices(depth)):
-            plane = HALO + z if z < SHIFT else 2 * planes - HALO - depth + z
-            out = warp_slice(shifted, plane - SHIFT, *slice_fields(shifts, fractions, z))
-            ends[number] = out
-            residual = subjects[z].astype(f32) - out
-            apart = me ^ (z // share)
-            index = (apart // PEERS) * share + z % share
-            for k, send in enumerate(sends, 1):
-
-                @pl.when(apart % PEERS == k)
-                def _():
-                    send[index] = residual
-
-    part = (kept, rows, cols)
-    count = len(end_slices(depth))
-    return local_call(
-        kernel, "end_warp",
-        [part] * (PEERS - 1) + [(count, rows, cols), (TAPS, 2 * planes, rows, cols)], 8,
-        [(2 * planes, rows, cols)], 300_000_000,
-    )
-
-
-def build_rest_warp(depth, rows, cols, members, groups):
-    share = depth // members
-    kept = depth // PEERS
-    planes = HALO + SHIFT + EDGE
-
-    def kernel(
-        moved, moved_ends, sent, ends, near_m, far_m, shifts, fractions, subjects, warped, keep
-    ):
-        me = lax.axis_index("subj")
-        odd = lax.axis_index("gz") % 2 == 1
-        inside = has_far(lax.axis_index("gz"), groups)
+        move_columns(slab, moved_ends, 0, 2 * planes)
 
         def body(i, carry):
             z = peer_shard(i, me, share, members, 0)
@@ -355,7 +364,8 @@
         lax.fori_loop(0, EDGE, outside, 0, unroll=2)
 
     return local_call(
-        kernel, "rest_warp", [(depth + 2 * EDGE, rows, cols), (kept, rows, cols)], 9, [],
+        kernel, "rest_warp", [(depth + 2 * EDGE, rows, cols), (kept, rows, cols)], 12,
+        [(2 * planes, rows, cols), (TAPS, 2 * planes, rows, cols)],
         600_000_000,
     )
 
@@ -644,13 +654,13 @@
     near_t, far_t = swap_near(to_near, "gz"), swap_far(to_far, "gz")
 
     sent, send, moved = build_inner_warp(depth, rows, cols, members)(pieces, shift, fraction, subject)
-    *sends, ends, moved_ends = build_end_warp(depth, rows, cols, members, groups)(
+    *sends, ends = build_end_warp(depth, rows, cols, members, groups)(
         low_t, high_t, near_t, far_t, shift, fraction, subject, send
     )
 
     parts = [swap(sends[k - 1], "subj", k) for k in (3, 1, 2)]
     warped, keep = build_rest_warp(depth, rows, cols, members, groups)(
-        moved, moved_ends, sent, ends, near_m, far_m, shift, fraction, subject
+        moved, low_t, high_t, near_t, far_t, sent, ends, near_m, far_m, shift, fraction, subject
     )
     near_m, far_m, subject, warped = lax.optimization_barrier((near_m, far_m, subject, warped))
     image, mean, variance = build_image(depth, rows, cols, groups)(near_m, far_m, subject)
@@ -660,9 +670,16 @@
     for bit in bits:
         pairs = keep.reshape((-1, 2, share) + keep.shape[1:])
         keep, send = [pairs[:, part].reshape((-1,) + keep.shape[1:]) for part in (0, 1)]
-        keep = keep + swap(send, "subj", bit)
+        arrived = swap(send, "subj", bit)
+        if bit != bits[-1]:
+            keep = keep + arrived
     (velocity,) = build_smooth(depth, rows, cols)(force)
-    template_force = keep * (1.0 / math.sqrt(subject_count * members))
+    scale = 1.0 / math.sqrt(subject_count * members)
+
+    def finish(one, two, out):
+        out[...] = (one[...] + two[...]) * scale
+
+    (template_force,) = local_call(finish, "finish", [(share, rows, cols)], 2, [], 10_000)(keep, arrived)
     return (velocity[None], template_force)
 
 

time: 31 us -> 30.8 us (level)
  Pallas kernels: 8.76 us -> 9.53 us
  other arithmetic: 0.67 us -> 0.05 us
    pallas_call x0 -> x1, Pallas kernels: none -> 0.62 us  [per_device(): local_call(finish, 'finish', [(share, rows, cols)], 2, [], 10000)]
    mul x1 -> x0, other arithmetic: 0.62 us -> none  [per_device(): template_force = keep * (1.0 / math.sqrt(subject_count * members))]
  transfers between devices with their start and end apart: 12 -> 12, of which waited for: 5 -> 3; matrix products, arithmetic and copies ran while one was open for 0% -> 0% of each run, Pallas kernels for 29% -> 29%
where the time goes in v7:
time: 30.8 us; the launch traced here: 30.6 us
  starting transfers between devices  16.9 us (55%)
  Pallas kernels  9.53 us (31%)
  waiting for transfers between devices  2.55 us (8%)
  local copies, waits for them, and re-layouts  0.81 us (3%)
  between operations  0.8 us (3%)
    ppermute x8, starting transfers between devices, swap(): return lax.ppermute(block, axis, [(i, i ^ bit) for i in range(count)])  13.6 us
    ppermute x2, starting transfers between devices, swap_far(): lax.ppermute(block, axis, [(i, (i + 1 if i % 2 else i - 1) % count) for i...  3.21 us
    ppermute x8, waiting for transfers between devices, swap(): return lax.ppermute(block, axis, [(i, i ^ bit) for i in range(count)])  2.54 us
    pallas_call x1, Pallas kernels, per_device(): velocity, = build_smooth(depth, rows, cols)(force)  1.84 us
    pallas_call x1, Pallas kernels, per_device(): to_near, to_far = build_pack(depth, rows, cols)(shift, fraction, subject)  1.76 us
    pallas_call x1, Pallas kernels, per_device(): build_inner_warp(depth, rows, cols, members)  1.76 us
    pallas_call x1, Pallas kernels, per_device(): build_rest_warp(depth, rows, cols, members, groups)  1.53 us
    pallas_call x1, Pallas kernels, per_device(): build_force(depth, rows, cols, groups)(warped, image, mean, variance)  1.1 us
  transfers between devices with their start and end apart: 12, of which 3 were waited for; matrix products, arithmetic and copies ran while one was open for 0% of the time, Pallas kernels for 29%

profile of v7, /device:TPU:0, one launch (start us, length us, event | category | flops | bytes accessed | tf_op | source)
XLA Modules:
  0.0 30.6 jit_solution(17435513037358560897)
XLA Ops:
  0.7 4.1 %collective-permute-start = (bf16[8,8,128]{2,1,0:T(8,128)(2,1)}, bf16[8,8,128]{2,1,0:T(8,128)(2,1)S(1)}, u32[]{:S(2)}, u32[]{:S(2)}) collective-permute-start(bf16[8,8,128]{2,1,0:T(8,128)(2,1)} %template.1), channel_id=1, source_target_pairs={{0,4},{1,5},{2,6},{3,7},{4,0},{5,1},{6,2},{7,3},{8,12},{9,13},{10,... | collective-permute-start | bytes 49160 | tf_op jit(solution)/shard_map/ppermute | solution.py:31
  4.8 0.7 %copy-done.3 = bf16[8,8,128]{2,1,0:T(8,128)(2,1)S(1)} copy-done((bf16[8,8,128]{2,1,0:T(8,128)(2,1)S(1)}, bf16[8,8,128]{2,1,0:T(8,128)(2,1)}, u32[]{:S(2)}) %copy-start.3) | copy-done | bytes 16408
  5.5 1.8 %pack.1 = (bf16[7,8,8,128]{3,2,1,0:T(8,128)(2,1)}, bf16[7,8,8,128]{3,2,1,0:T(8,128)(2,1)}) custom-call(s32[3,64,8,128]{3,2,1,0:T(8,128)} %bitcast.9, bf16[3,64,8,128]{3,2,1,0:T(8,128)(2,1)} %bitcast.13, bf16[64,8,128]{2,1,0:T(8,128)(2,1)} %bitcast.17), custom_call_target="tpu_custom_call" | custom-call | flops 1000000 | bytes 2000000 | tf_op jit(solution)/shard_map/pack/pallas_call | solution.py:635
  7.3 1.6 %collective-permute-start.1 = (bf16[16,8,128]{2,1,0:T(8,128)(2,1)S(1)}, bf16[16,8,128]{2,1,0:T(8,128)(2,1)S(1)}, u32[]{:S(2)}, u32[]{:S(2)}) collective-permute-start(bf16[16,8,128]{2,1,0:T(8,128)(2,1)S(1)} %pad_maximum_fusion), channel_id=1, source_target_pairs={{0,1},{1,0},{2,3},{3,2},{4,5},{5,4},{6,7},{7,6},{8,9},{9,8},{10,11... | collective-permute-start | bytes 98312 | tf_op jit(solution)/shard_map/ppermute | solution.py:31
  8.9 1.5 %collective-permute-start.2 = (bf16[16,8,128]{2,1,0:T(8,128)(2,1)S(1)}, bf16[16,8,128]{2,1,0:T(8,128)(2,1)S(1)}, u32[]{:S(2)}, u32[]{:S(2)}) collective-permute-start(bf16[16,8,128]{2,1,0:T(8,128)(2,1)S(1)} %pad_maximum_fusion), channel_id=1, source_target_pairs={{0,3},{1,2},{2,1},{3,0},{4,7},{5,6},{6,5},{7,4},{8,11},{9,10},{10,... | collective-permute-start | bytes 98312 | tf_op jit(solution)/shard_map/ppermute | solution.py:31
  10.4 0.4 %collective-permute-start.3 = (bf16[16,8,128]{2,1,0:T(8,128)(2,1)S(1)}, bf16[16,8,128]{2,1,0:T(8,128)(2,1)S(1)}, u32[]{:S(2)}, u32[]{:S(2)}) collective-permute-start(bf16[16,8,128]{2,1,0:T(8,128)(2,1)S(1)} %pad_maximum_fusion), channel_id=1, source_target_pairs={{0,2},{1,3},{2,0},{3,1},{4,6},{5,7},{6,4},{7,5},{8,10},{9,11},{10,... | collective-permute-start | bytes 98312 | tf_op jit(solution)/shard_map/ppermute | solution.py:31
  10.9 1.6 %collective-permute-start.10 = (bf16[7,8,8,128]{3,2,1,0:T(8,128)(2,1)}, bf16[7,8,8,128]{3,2,1,0:T(8,128)(2,1)S(1)}, u32[]{:S(2)}, u32[]{:S(2)}) collective-permute-start(bf16[7,8,8,128]{3,2,1,0:T(8,128)(2,1)} %get-tuple-element.35), channel_id=1, source_target_pairs={{0,24},{8,16},{16,8},{24,0},{1,25},{9,17},{17,9},{25,1},{2,26},{10... | collective-permute-start | bytes 344072 | tf_op jit(solution)/shard_map/ppermute | solution.py:43
  12.5 1.2 %collective-permute-done.2 = bf16[16,8,128]{2,1,0:T(8,128)(2,1)S(1)} collective-permute-done((bf16[16,8,128]{2,1,0:T(8,128)(2,1)S(1)}, bf16[16,8,128]{2,1,0:T(8,128)(2,1)S(1)}, u32[]{:S(2)}, u32[]{:S(2)}) %collective-permute-start.2) | collective-permute-done | bytes 32800 | tf_op jit(solution)/shard_map/ppermute | solution.py:31
  13.7 0.6 %collective-permute-done.3 = bf16[16,8,128]{2,1,0:T(8,128)(2,1)S(1)} collective-permute-done((bf16[16,8,128]{2,1,0:T(8,128)(2,1)S(1)}, bf16[16,8,128]{2,1,0:T(8,128)(2,1)S(1)}, u32[]{:S(2)}, u32[]{:S(2)}) %collective-permute-start.3) | collective-permute-done | bytes 32800 | tf_op jit(solution)/shard_map/ppermute | solution.py:31
  14.4 0.1 collective-permute-start.4
  14.5 1.6 %collective-permute-start.5 = (bf16[11,8,128]{2,1,0:T(8,128)(2,1)S(1)}, bf16[11,8,128]{2,1,0:T(8,128)(2,1)S(1)}, u32[]{:S(2)}, u32[]{:S(2)}) collective-permute-start(bf16[11,8,128]{2,1,0:T(8,128)(2,1)S(1)} %get-tuple-element.52), channel_id=1, source_target_pairs={{0,24},{8,16},{16,8},{24,0},{1,25},{9,17},{17,9},{25,1},{2,26},{10... | collective-permute-start | bytes 67592 | tf_op jit(solution)/shard_map/ppermute | solution.py:43
  16.1 1.8 %inner_warp.1 = (f32[48,8,128]{2,1,0:T(8,128)S(1)}, f32[48,8,128]{2,1,0:T(8,128)S(1)}, f32[6,70,8,128]{3,2,1,0:T(8,128)S(1)}) custom-call(bf16[64,8,128]{2,1,0:T(8,128)(2,1)S(1)} %constant_dynamic-update-slice_fusion.pieces, s32[3,64,8,128]{3,2,1,0:T(8,128)S(1)} %bitcast.10, bf16[3,64,8,128]{3,2,1,0:T(8,128)(2,1)S(1)} %bitcast.14, ...), custom_call_target="tpu_custom_call" | custom-call | flops 1000000000 | bytes 8000000 | tf_op jit(solution)/shard_map/inner_warp/pallas_call | solution.py:656
  17.9 0.4 %end_warp.1 = (f32[16,8,128]{2,1,0:T(8,128)S(1)}, f32[16,8,128]{2,1,0:T(8,128)S(1)}, f32[16,8,128]{2,1,0:T(8,128)S(1)}, f32[5,8,128]{2,1,0:T(8,128)S(1)}) custom-call(bf16[11,8,128]{2,1,0:T(8,128)(2,1)S(1)} %get-tuple-element.54.low_t, bf16[11,8,128]{2,1,0:T(8,128)(2,1)S(1)} %get-tuple-element.53.high_t, ...), custom_call_target="tpu_custom_call" | custom-call | flops 300000000 | bytes 8000000 | tf_op jit(solution)/shard_map/end_warp/pallas_call | solution.py:657
  18.3 1.5 %collective-permute-start.6 = (f32[16,8,128]{2,1,0:T(8,128)S(1)}, f32[16,8,128]{2,1,0:T(8,128)S(1)}, u32[]{:S(2)}, u32[]{:S(2)}) collective-permute-start(f32[16,8,128]{2,1,0:T(8,128)S(1)} %get-tuple-element.31), channel_id=1, source_target_pairs={{0,3},{1,2},{2,1},{3,0},{4,7},{5,6},{6,5},{7,4},{8,11},{9,10},{10,... | collective-permute-start | bytes 196616 | tf_op jit(solution)/shard_map/ppermute | solution.py:31
  19.8 1.0 %collective-permute-start.7 = (f32[16,8,128]{2,1,0:T(8,128)S(1)}, f32[16,8,128]{2,1,0:T(8,128)S(1)}, u32[]{:S(2)}, u32[]{:S(2)}) collective-permute-start(f32[16,8,128]{2,1,0:T(8,128)S(1)} %get-tuple-element.32), channel_id=1, source_target_pairs={{0,1},{1,0},{2,3},{3,2},{4,5},{5,4},{6,7},{7,6},{8,9},{9,8},{10,11... | collective-permute-start | bytes 196616 | tf_op jit(solution)/shard_map/ppermute | solution.py:31
  20.8 1.0 %collective-permute-start.8 = (f32[16,8,128]{2,1,0:T(8,128)S(1)}, f32[16,8,128]{2,1,0:T(8,128)S(1)}, u32[]{:S(2)}, u32[]{:S(2)}) collective-permute-start(f32[16,8,128]{2,1,0:T(8,128)S(1)} %get-tuple-element.33), channel_id=1, source_target_pairs={{0,2},{1,3},{2,0},{3,1},{4,6},{5,7},{6,4},{7,5},{8,10},{9,11},{10,... | collective-permute-start | bytes 196616 | tf_op jit(solution)/shard_map/ppermute | solution.py:31
  21.8 1.5 %rest_warp.1 = (f32[80,8,128]{2,1,0:T(8,128)S(1)}, f32[16,8,128]{2,1,0:T(8,128)S(1)}) custom-call(f32[6,70,8,128]{3,2,1,0:T(8,128)S(1)} %get-tuple-element.36.moved, bf16[11,8,128]{2,1,0:T(8,128)(2,1)S(1)} %get-tuple-element.54.low_t, bf16[11,8,128]{2,1,0:T(8,128)(2,1)S(1)} %get-tuple-element.53.high_t, ...), custom_call_target="tpu_custom_call" | custom-call | flops 600000000 | bytes 8000000 | tf_op jit(solution)/shard_map/rest_warp/pallas_call | solution.py:662
  23.4 0.5 %image.1 = (f32[80,8,128]{2,1,0:T(8,128)S(1)}, f32[72,8,128]{2,1,0:T(8,128)S(1)}, f32[72,8,128]{2,1,0:T(8,128)S(1)}) custom-call(bf16[7,8,8,128]{3,2,1,0:T(8,128)(2,1)S(1)} %collective-permute-done.9.near_m, bf16[7,8,8,128]{3,2,1,0:T(8,128)(2,1)S(1)} %collective-permute-done.10.far_m, bf16[64,8,128]{2,1,0:T(8,128)(2,1)S(1)} %bitcast.21), custom_call_target="tpu_custom_call" | custom-call | flops 400000000 | bytes 8000000 | tf_op jit(solution)/shard_map/image/pallas_call | solution.py:666
  23.9 1.1 %force.1 = f32[3,72,8,128]{3,2,1,0:T(8,128)S(1)} custom-call(f32[80,8,128]{2,1,0:T(8,128)S(1)} %get-tuple-element.40.warped, f32[80,8,128]{2,1,0:T(8,128)S(1)} %get-tuple-element.44.image, f32[72,8,128]{2,1,0:T(8,128)S(1)} %get-tuple-element.45.mean, f32[72,8,128]{2,1,0:T(8,128)S(1)} %get-tuple-element.46.variance), custom_call_target="tpu_custom_call" | custom-call | flops 1000000000 | bytes 8000000 | tf_op jit(solution)/shard_map/force/pallas_call | solution.py:667
  25.0 0.0 collective-permute-done.8
  25.1 2.4 %collective-permute-start.11 = (f32[8,8,128]{2,1,0:T(8,128)S(1)}, f32[8,8,128]{2,1,0:T(8,128)S(1)}, u32[]{:S(2)}, u32[]{:S(2)}) collective-permute-start(f32[8,8,128]{2,1,0:T(8,128)S(1)} %get-tuple-element.59), channel_id=1, source_target_pairs={{0,4},{1,5},{2,6},{3,7},{4,0},{5,1},{6,2},{7,3},{8,12},{9,13},{10,... | collective-permute-start | bytes 98312 | tf_op jit(solution)/shard_map/ppermute | solution.py:31
  27.5 1.8 %smooth.1 = f32[3,64,8,128]{3,2,1,0:T(8,128)} custom-call(f32[3,72,8,128]{3,2,1,0:T(8,128)S(1)} %force.1), custom_call_target="tpu_custom_call" | custom-call | flops 600000000 | bytes 8000000 | tf_op jit(solution)/shard_map/smooth/pallas_call | solution.py:676
  29.3 0.7 %collective-permute-done.11.two = f32[8,8,128]{2,1,0:T(8,128)S(1)} collective-permute-done((f32[8,8,128]{2,1,0:T(8,128)S(1)}, f32[8,8,128]{2,1,0:T(8,128)S(1)}, u32[]{:S(2)}, u32[]{:S(2)}) %collective-permute-start.11) | collective-permute-done | bytes 32800 | tf_op jit(solution)/shard_map/ppermute | solution.py:31
  30.0 0.6 %finish.1 = f32[8,8,128]{2,1,0:T(8,128)} custom-call(f32[8,8,128]{2,1,0:T(8,128)S(1)} %get-tuple-element.60.one, f32[8,8,128]{2,1,0:T(8,128)S(1)} %collective-permute-done.11.two), custom_call_target="tpu_custom_call" | custom-call | flops 10000 | bytes 8000000 | tf_op jit(solution)/shard_map/finish/pallas_call | solution.py:682
  (27 shorter events, 0.1 us)
Async XLA Ops:
  0.6 15.5 %copy-start = (s32[1,3,64,8,128]{4,3,2,1,0:T(8,128)S(1)}, s32[1,3,64,8,128]{4,3,2,1,0:T(8,128)}, u32[]{:S(2)}) copy-start(s32[1,3,64,8,128]{4,3,2,1,0:T(8,128)} %param.6) | copy-start | bytes 2359300
  0.6 15.4 %copy-start.1 = (bf16[1,3,64,8,128]{4,3,2,1,0:T(8,128)(2,1)S(1)}, bf16[1,3,64,8,128]{4,3,2,1,0:T(8,128)(2,1)}, u32[]{:S(2)}) copy-start(bf16[1,3,64,8,128]{4,3,2,1,0:T(8,128)(2,1)} %param.7) | copy-start | bytes 1179652
  0.7 15.4 %copy-start.2 = (bf16[1,64,8,128]{3,2,1,0:T(8,128)(2,1)S(1)}, bf16[1,64,8,128]{3,2,1,0:T(8,128)(2,1)}, u32[]{:S(2)}) copy-start(bf16[1,64,8,128]{3,2,1,0:T(8,128)(2,1)} %param.5) | copy-start | bytes 393220
  0.7 6.6 %collective-permute-start = (bf16[8,8,128]{2,1,0:T(8,128)(2,1)}, bf16[8,8,128]{2,1,0:T(8,128)(2,1)S(1)}, u32[]{:S(2)}, u32[]{:S(2)}) collective-permute-start(bf16[8,8,128]{2,1,0:T(8,128)(2,1)} %template.1), channel_id=1, source_target_pairs={{0,4},{1,5},{2,6},{3,7},{4,0},{5,1},{6,2},{7,3},{8,12},{9,13},{10,... | collective-permute-start | bytes 49160 | tf_op jit(solution)/shard_map/ppermute | solution.py:31
  4.8 0.8 %copy-start.3 = (bf16[8,8,128]{2,1,0:T(8,128)(2,1)S(1)}, bf16[8,8,128]{2,1,0:T(8,128)(2,1)}, u32[]{:S(2)}) copy-start(bf16[8,8,128]{2,1,0:T(8,128)(2,1)} %template.1) | copy-start | bytes 49156
  7.3 5.2 %collective-permute-start.1 = (bf16[16,8,128]{2,1,0:T(8,128)(2,1)S(1)}, bf16[16,8,128]{2,1,0:T(8,128)(2,1)S(1)}, u32[]{:S(2)}, u32[]{:S(2)}) collective-permute-start(bf16[16,8,128]{2,1,0:T(8,128)(2,1)S(1)} %pad_maximum_fusion), channel_id=1, source_target_pairs={{0,1},{1,0},{2,3},{3,2},{4,5},{5,4},{6,7},{7,6},{8,9},{9,8},{10,11... | collective-permute-start | bytes 98312 | tf_op jit(solution)/shard_map/ppermute | solution.py:31
  8.9 4.8 %collective-permute-start.2 = (bf16[16,8,128]{2,1,0:T(8,128)(2,1)S(1)}, bf16[16,8,128]{2,1,0:T(8,128)(2,1)S(1)}, u32[]{:S(2)}, u32[]{:S(2)}) collective-permute-start(bf16[16,8,128]{2,1,0:T(8,128)(2,1)S(1)} %pad_maximum_fusion), channel_id=1, source_target_pairs={{0,3},{1,2},{2,1},{3,0},{4,7},{5,6},{6,5},{7,4},{8,11},{9,10},{10,... | collective-permute-start | bytes 98312 | tf_op jit(solution)/shard_map/ppermute | solution.py:31
  10.4 3.9 %collective-permute-start.3 = (bf16[16,8,128]{2,1,0:T(8,128)(2,1)S(1)}, bf16[16,8,128]{2,1,0:T(8,128)(2,1)S(1)}, u32[]{:S(2)}, u32[]{:S(2)}) collective-permute-start(bf16[16,8,128]{2,1,0:T(8,128)(2,1)S(1)} %pad_maximum_fusion), channel_id=1, source_target_pairs={{0,2},{1,3},{2,0},{3,1},{4,6},{5,7},{6,4},{7,5},{8,10},{9,11},{10,... | collective-permute-start | bytes 98312 | tf_op jit(solution)/shard_map/ppermute | solution.py:31
  10.9 10.9 %collective-permute-start.9 = (bf16[7,8,8,128]{3,2,1,0:T(8,128)(2,1)}, bf16[7,8,8,128]{3,2,1,0:T(8,128)(2,1)S(1)}, u32[]{:S(2)}, u32[]{:S(2)}) collective-permute-start(bf16[7,8,8,128]{3,2,1,0:T(8,128)(2,1)} %get-tuple-element.34), channel_id=1, source_target_pairs={{0,8},{8,0},{16,24},{24,16},{1,9},{9,1},{17,25},{25,17},{2,10},{10... | collective-permute-start | bytes 344072 | tf_op jit(solution)/shard_map/ppermute | solution.py:37
  10.9 10.9 %collective-permute-start.10 = (bf16[7,8,8,128]{3,2,1,0:T(8,128)(2,1)}, bf16[7,8,8,128]{3,2,1,0:T(8,128)(2,1)S(1)}, u32[]{:S(2)}, u32[]{:S(2)}) collective-permute-start(bf16[7,8,8,128]{3,2,1,0:T(8,128)(2,1)} %get-tuple-element.35), channel_id=1, source_target_pairs={{0,24},{8,16},{16,8},{24,0},{1,25},{9,17},{17,9},{25,1},{2,26},{10... | collective-permute-start | bytes 344072 | tf_op jit(solution)/shard_map/ppermute | solution.py:43
  14.4 3.5 %collective-permute-start.4 = (bf16[11,8,128]{2,1,0:T(8,128)(2,1)S(1)}, bf16[11,8,128]{2,1,0:T(8,128)(2,1)S(1)}, u32[]{:S(2)}, u32[]{:S(2)}) collective-permute-start(bf16[11,8,128]{2,1,0:T(8,128)(2,1)S(1)} %broadcast_select_fusion.1), channel_id=1, source_target_pairs={{0,8},{8,0},{16,24},{24,16},{1,9},{9,1},{17,25},{25,17},{2,10},{10... | collective-permute-start | bytes 67592 | tf_op jit(solution)/shard_map/ppermute | solution.py:37
  14.5 3.4 %collective-permute-start.5 = (bf16[11,8,128]{2,1,0:T(8,128)(2,1)S(1)}, bf16[11,8,128]{2,1,0:T(8,128)(2,1)S(1)}, u32[]{:S(2)}, u32[]{:S(2)}) collective-permute-start(bf16[11,8,128]{2,1,0:T(8,128)(2,1)S(1)} %get-tuple-element.52), channel_id=1, source_target_pairs={{0,24},{8,16},{16,8},{24,0},{1,25},{9,17},{17,9},{25,1},{2,26},{10... | collective-permute-start | bytes 67592 | tf_op jit(solution)/shard_map/ppermute | solution.py:43
  18.3 6.7 %collective-permute-start.6 = (f32[16,8,128]{2,1,0:T(8,128)S(1)}, f32[16,8,128]{2,1,0:T(8,128)S(1)}, u32[]{:S(2)}, u32[]{:S(2)}) collective-permute-start(f32[16,8,128]{2,1,0:T(8,128)S(1)} %get-tuple-element.31), channel_id=1, source_target_pairs={{0,3},{1,2},{2,1},{3,0},{4,7},{5,6},{6,5},{7,4},{8,11},{9,10},{10,... | collective-permute-start | bytes 196616 | tf_op jit(solution)/shard_map/ppermute | solution.py:31
  19.8 5.3 %collective-permute-start.7 = (f32[16,8,128]{2,1,0:T(8,128)S(1)}, f32[16,8,128]{2,1,0:T(8,128)S(1)}, u32[]{:S(2)}, u32[]{:S(2)}) collective-permute-start(f32[16,8,128]{2,1,0:T(8,128)S(1)} %get-tuple-element.32), channel_id=1, source_target_pairs={{0,1},{1,0},{2,3},{3,2},{4,5},{5,4},{6,7},{7,6},{8,9},{9,8},{10,11... | collective-permute-start | bytes 196616 | tf_op jit(solution)/shard_map/ppermute | solution.py:31
  20.8 4.3 %collective-permute-start.8 = (f32[16,8,128]{2,1,0:T(8,128)S(1)}, f32[16,8,128]{2,1,0:T(8,128)S(1)}, u32[]{:S(2)}, u32[]{:S(2)}) collective-permute-start(f32[16,8,128]{2,1,0:T(8,128)S(1)} %get-tuple-element.33), channel_id=1, source_target_pairs={{0,2},{1,3},{2,0},{3,1},{4,6},{5,7},{6,4},{7,5},{8,10},{9,11},{10,... | collective-permute-start | bytes 196616 | tf_op jit(solution)/shard_map/ppermute | solution.py:31
  25.1 4.9 %collective-permute-start.11 = (f32[8,8,128]{2,1,0:T(8,128)S(1)}, f32[8,8,128]{2,1,0:T(8,128)S(1)}, u32[]{:S(2)}, u32[]{:S(2)}) collective-permute-start(f32[8,8,128]{2,1,0:T(8,128)S(1)} %get-tuple-element.59), channel_id=1, source_target_pairs={{0,4},{1,5},{2,6},{3,7},{4,0},{5,1},{6,2},{7,3},{8,12},{9,13},{10,... | collective-permute-start | bytes 98312 | tf_op jit(solution)/shard_map/ppermute | solution.py:31

commit v8 on v6

--- a/solution.py
+++ b/solution.py
@@ -18,7 +18,7 @@
 f32 = jnp.float32
 bf16 = jnp.bfloat16
 PEERS = 4
-ORDER = (0, 1, 3, 2)
+ORDER = (0, 3, 1, 2)
 VMEM_LIMIT = 48 * 1024 * 1024
 
 raw = [math.exp(-k * k / (2 * sigma * sigma)) for k in range(SMOOTH + 1)]
@@ -214,7 +214,7 @@
             pltpu.VMEM((2, 4, EDGE, rows, cols), bf16),
             pltpu.SemaphoreType.DMA((6,)),
         ],
-        compiler_params=pltpu.CompilerParams(vmem_limit_bytes=62 * 1024 * 1024),
+        compiler_params=pltpu.CompilerParams(vmem_limit_bytes=60 * 1024 * 1024),
         cost_estimate=pl.CostEstimate(flops=1_000_000, bytes_accessed=2_000_000, transcendentals=0),
         name="pack",
     )

time: 31 us -> 30.9 us (level)
  no operation moved by 1% of the time
where the time goes in v8:
time: 30.9 us; the launch traced here: 30.6 us
  starting transfers between devices  16.9 us (55%)
  Pallas kernels  8.76 us (28%)
  waiting for transfers between devices  2.74 us (9%)
  local copies, waits for them, and re-layouts  0.81 us (3%)
  between operations  0.79 us (3%)
  other arithmetic  0.67 us (2%)
    ppermute x8, starting transfers between devices, swap(): return lax.ppermute(block, axis, [(i, i ^ bit) for i in range(count)])  13.6 us
    ppermute x2, starting transfers between devices, swap_far(): lax.ppermute(block, axis, [(i, (i + 1 if i % 2 else i - 1) % count) for i...  3.21 us
    ppermute x8, waiting for transfers between devices, swap(): return lax.ppermute(block, axis, [(i, i ^ bit) for i in range(count)])  2.73 us
    pallas_call x1, Pallas kernels, per_device(): velocity, = build_smooth(depth, rows, cols)(force)  1.84 us
    pallas_call x1, Pallas kernels, per_device(): build_inner_warp(depth, rows, cols, members)  1.81 us
    pallas_call x1, Pallas kernels, per_device(): to_near, to_far = build_pack(depth, rows, cols)(shift, fraction, subject)  1.76 us
    pallas_call x1, Pallas kernels, per_device(): build_rest_warp(depth, rows, cols, members, groups)  1.23 us
    pallas_call x1, Pallas kernels, per_device(): build_force(depth, rows, cols, groups)(warped, image, mean, variance)  1.11 us
  transfers between devices with their start and end apart: 12, of which 5 were waited for; matrix products, arithmetic and copies ran while one was open for 0% of the time, Pallas kernels for 29%

profile of v8, /device:TPU:0, one launch (start us, length us, event | category | flops | bytes accessed | tf_op | source)
XLA Modules:
  0.0 30.6 jit_solution(5903012138327037578)
XLA Ops:
  0.7 4.1 %collective-permute-start = (bf16[8,8,128]{2,1,0:T(8,128)(2,1)}, bf16[8,8,128]{2,1,0:T(8,128)(2,1)S(1)}, u32[]{:S(2)}, u32[]{:S(2)}) collective-permute-start(bf16[8,8,128]{2,1,0:T(8,128)(2,1)} %template.1), channel_id=1, source_target_pairs={{0,4},{1,5},{2,6},{3,7},{4,0},{5,1},{6,2},{7,3},{8,12},{9,13},{10,... | collective-permute-start | bytes 49160 | tf_op jit(solution)/shard_map/ppermute | solution.py:31
  4.8 0.7 %copy-done.3 = bf16[8,8,128]{2,1,0:T(8,128)(2,1)S(1)} copy-done((bf16[8,8,128]{2,1,0:T(8,128)(2,1)S(1)}, bf16[8,8,128]{2,1,0:T(8,128)(2,1)}, u32[]{:S(2)}) %copy-start.3) | copy-done | bytes 16408
  5.5 1.8 %pack.1 = (bf16[7,8,8,128]{3,2,1,0:T(8,128)(2,1)}, bf16[7,8,8,128]{3,2,1,0:T(8,128)(2,1)}) custom-call(s32[3,64,8,128]{3,2,1,0:T(8,128)} %bitcast.13, bf16[3,64,8,128]{3,2,1,0:T(8,128)(2,1)} %bitcast.17, bf16[64,8,128]{2,1,0:T(8,128)(2,1)} %bitcast.21), custom_call_target="tpu_custom_call" | custom-call | flops 1000000 | bytes 2000000 | tf_op jit(solution)/shard_map/pack/pallas_call | solution.py:625
  7.3 2.6 %collective-permute-start.1 = (bf16[16,8,128]{2,1,0:T(8,128)(2,1)S(1)}, bf16[16,8,128]{2,1,0:T(8,128)(2,1)S(1)}, u32[]{:S(2)}, u32[]{:S(2)}) collective-permute-start(bf16[16,8,128]{2,1,0:T(8,128)(2,1)S(1)} %pad_maximum_fusion), channel_id=1, source_target_pairs={{0,3},{1,2},{2,1},{3,0},{4,7},{5,6},{6,5},{7,4},{8,11},{9,10},{10,... | collective-permute-start | bytes 98312 | tf_op jit(solution)/shard_map/ppermute | solution.py:31
  9.9 0.5 %collective-permute-start.2 = (bf16[16,8,128]{2,1,0:T(8,128)(2,1)S(1)}, bf16[16,8,128]{2,1,0:T(8,128)(2,1)S(1)}, u32[]{:S(2)}, u32[]{:S(2)}) collective-permute-start(bf16[16,8,128]{2,1,0:T(8,128)(2,1)S(1)} %pad_maximum_fusion), channel_id=1, source_target_pairs={{0,1},{1,0},{2,3},{3,2},{4,5},{5,4},{6,7},{7,6},{8,9},{9,8},{10,11... | collective-permute-start | bytes 98312 | tf_op jit(solution)/shard_map/ppermute | solution.py:31
  10.4 0.4 %collective-permute-start.3 = (bf16[16,8,128]{2,1,0:T(8,128)(2,1)S(1)}, bf16[16,8,128]{2,1,0:T(8,128)(2,1)S(1)}, u32[]{:S(2)}, u32[]{:S(2)}) collective-permute-start(bf16[16,8,128]{2,1,0:T(8,128)(2,1)S(1)} %pad_maximum_fusion), channel_id=1, source_target_pairs={{0,2},{1,3},{2,0},{3,1},{4,6},{5,7},{6,4},{7,5},{8,10},{9,11},{10,... | collective-permute-start | bytes 98312 | tf_op jit(solution)/shard_map/ppermute | solution.py:31
  10.9 1.6 %collective-permute-start.10 = (bf16[7,8,8,128]{3,2,1,0:T(8,128)(2,1)}, bf16[7,8,8,128]{3,2,1,0:T(8,128)(2,1)S(1)}, u32[]{:S(2)}, u32[]{:S(2)}) collective-permute-start(bf16[7,8,8,128]{3,2,1,0:T(8,128)(2,1)} %get-tuple-element.36), channel_id=1, source_target_pairs={{0,24},{8,16},{16,8},{24,0},{1,25},{9,17},{17,9},{25,1},{2,26},{10... | collective-permute-start | bytes 344072 | tf_op jit(solution)/shard_map/ppermute | solution.py:43
  12.5 1.3 %collective-permute-done.2 = bf16[16,8,128]{2,1,0:T(8,128)(2,1)S(1)} collective-permute-done((bf16[16,8,128]{2,1,0:T(8,128)(2,1)S(1)}, bf16[16,8,128]{2,1,0:T(8,128)(2,1)S(1)}, u32[]{:S(2)}, u32[]{:S(2)}) %collective-permute-start.2) | collective-permute-done | bytes 32800 | tf_op jit(solution)/shard_map/ppermute | solution.py:31
  13.8 0.5 %collective-permute-done.3 = bf16[16,8,128]{2,1,0:T(8,128)(2,1)S(1)} collective-permute-done((bf16[16,8,128]{2,1,0:T(8,128)(2,1)S(1)}, bf16[16,8,128]{2,1,0:T(8,128)(2,1)S(1)}, u32[]{:S(2)}, u32[]{:S(2)}) %collective-permute-start.3) | collective-permute-done | bytes 32800 | tf_op jit(solution)/shard_map/ppermute | solution.py:31
  14.4 0.1 collective-permute-start.4
  14.5 1.6 %collective-permute-start.5 = (bf16[11,8,128]{2,1,0:T(8,128)(2,1)S(1)}, bf16[11,8,128]{2,1,0:T(8,128)(2,1)S(1)}, u32[]{:S(2)}, u32[]{:S(2)}) collective-permute-start(bf16[11,8,128]{2,1,0:T(8,128)(2,1)S(1)} %get-tuple-element.54), channel_id=1, source_target_pairs={{0,24},{8,16},{16,8},{24,0},{1,25},{9,17},{17,9},{25,1},{2,26},{10... | collective-permute-start | bytes 67592 | tf_op jit(solution)/shard_map/ppermute | solution.py:43
  16.1 1.8 %inner_warp.1 = (f32[48,8,128]{2,1,0:T(8,128)S(1)}, f32[48,8,128]{2,1,0:T(8,128)S(1)}, f32[6,70,8,128]{3,2,1,0:T(8,128)S(1)}) custom-call(bf16[64,8,128]{2,1,0:T(8,128)(2,1)S(1)} %constant_dynamic-update-slice_fusion.pieces, s32[3,64,8,128]{3,2,1,0:T(8,128)S(1)} %bitcast.14, bf16[3,64,8,128]{3,2,1,0:T(8,128)(2,1)S(1)} %bitcast.18, ...), custom_call_target="tpu_custom_call" | custom-call | flops 1000000000 | bytes 8000000 | tf_op jit(solution)/shard_map/inner_warp/pallas_call | solution.py:646
  17.9 0.5 %end_warp.1 = (f32[16,8,128]{2,1,0:T(8,128)S(1)}, f32[16,8,128]{2,1,0:T(8,128)S(1)}, f32[16,8,128]{2,1,0:T(8,128)S(1)}, f32[5,8,128]{2,1,0:T(8,128)S(1)}, f32[6,42,8,128]{3,2,1,0:T(8,128)S(1)}) custom-call(bf16[11,8,128]{2,1,0:T(8,128)(2,1)S(1)} %get-tuple-element.56.low_t, bf16[11,8,128]{2,1,0:T(8,128)(2,1)S(1)} %get-tuple-element.55.high_t, ...), custom_call_target="tpu_custom_call" | custom-call | flops 300000000 | bytes 8000000 | tf_op jit(solution)/shard_map/end_warp/pallas_call | solution.py:647
  18.4 1.5 %collective-permute-start.6 = (f32[16,8,128]{2,1,0:T(8,128)S(1)}, f32[16,8,128]{2,1,0:T(8,128)S(1)}, u32[]{:S(2)}, u32[]{:S(2)}) collective-permute-start(f32[16,8,128]{2,1,0:T(8,128)S(1)} %get-tuple-element.32), channel_id=1, source_target_pairs={{0,3},{1,2},{2,1},{3,0},{4,7},{5,6},{6,5},{7,4},{8,11},{9,10},{10,... | collective-permute-start | bytes 196616 | tf_op jit(solution)/shard_map/ppermute | solution.py:31
  19.9 0.5 %collective-permute-start.7 = (f32[16,8,128]{2,1,0:T(8,128)S(1)}, f32[16,8,128]{2,1,0:T(8,128)S(1)}, u32[]{:S(2)}, u32[]{:S(2)}) collective-permute-start(f32[16,8,128]{2,1,0:T(8,128)S(1)} %get-tuple-element.33), channel_id=1, source_target_pairs={{0,1},{1,0},{2,3},{3,2},{4,5},{5,4},{6,7},{7,6},{8,9},{9,8},{10,11... | collective-permute-start | bytes 196616 | tf_op jit(solution)/shard_map/ppermute | solution.py:31
  20.4 1.6 %collective-permute-start.8 = (f32[16,8,128]{2,1,0:T(8,128)S(1)}, f32[16,8,128]{2,1,0:T(8,128)S(1)}, u32[]{:S(2)}, u32[]{:S(2)}) collective-permute-start(f32[16,8,128]{2,1,0:T(8,128)S(1)} %get-tuple-element.34), channel_id=1, source_target_pairs={{0,2},{1,3},{2,0},{3,1},{4,6},{5,7},{6,4},{7,5},{8,10},{9,11},{10,... | collective-permute-start | bytes 196616 | tf_op jit(solution)/shard_map/ppermute | solution.py:31
  22.0 1.2 %rest_warp.1 = (f32[80,8,128]{2,1,0:T(8,128)S(1)}, f32[16,8,128]{2,1,0:T(8,128)S(1)}) custom-call(f32[6,70,8,128]{3,2,1,0:T(8,128)S(1)} %get-tuple-element.37.moved, f32[6,42,8,128]{3,2,1,0:T(8,128)S(1)} %get-tuple-element.38.moved_ends, f32[48,8,128]{2,1,0:T(8,128)S(1)} %get-tuple-element.39.sent, f32[5,8,128]{2,1,0:T(8,128)S(1)} %get-tuple-element.40.ends, ...), custom_call_target="tpu_custom_call" | custom-call | flops 600000000 | bytes 8000000 | tf_op jit(solution)/shard_map/rest_warp/pallas_call | solution.py:652
  23.2 0.5 %image.1 = (f32[80,8,128]{2,1,0:T(8,128)S(1)}, f32[72,8,128]{2,1,0:T(8,128)S(1)}, f32[72,8,128]{2,1,0:T(8,128)S(1)}) custom-call(bf16[7,8,8,128]{3,2,1,0:T(8,128)(2,1)S(1)} %collective-permute-done.9.near_m, bf16[7,8,8,128]{3,2,1,0:T(8,128)(2,1)S(1)} %collective-permute-done.10.far_m, bf16[64,8,128]{2,1,0:T(8,128)(2,1)S(1)} %bitcast.25), custom_call_target="tpu_custom_call" | custom-call | flops 400000000 | bytes 8000000 | tf_op jit(solution)/shard_map/image/pallas_call | solution.py:656
  23.7 1.1 %force.1 = f32[3,72,8,128]{3,2,1,0:T(8,128)S(1)} custom-call(f32[80,8,128]{2,1,0:T(8,128)S(1)} %get-tuple-element.42.warped, f32[80,8,128]{2,1,0:T(8,128)S(1)} %get-tuple-element.46.image, f32[72,8,128]{2,1,0:T(8,128)S(1)} %get-tuple-element.47.mean, f32[72,8,128]{2,1,0:T(8,128)S(1)} %get-tuple-element.48.variance), custom_call_target="tpu_custom_call" | custom-call | flops 1000000000 | bytes 8000000 | tf_op jit(solution)/shard_map/force/pallas_call | solution.py:657
  24.9 0.2 collective-permute-done.7
  25.1 2.4 %collective-permute-start.11 = (f32[8,8,128]{2,1,0:T(8,128)S(1)}, f32[8,8,128]{2,1,0:T(8,128)S(1)}, u32[]{:S(2)}, u32[]{:S(2)}) collective-permute-start(f32[8,8,128]{2,1,0:T(8,128)S(1)} %slice_bitcast_fusion), channel_id=1, source_target_pairs={{0,4},{1,5},{2,6},{3,7},{4,0},{5,1},{6,2},{7,3},{8,12},{9,13},{10,... | collective-permute-start | bytes 98312 | tf_op jit(solution)/shard_map/ppermute | solution.py:31
  27.5 1.8 %smooth.1 = f32[3,64,8,128]{3,2,1,0:T(8,128)} custom-call(f32[3,72,8,128]{3,2,1,0:T(8,128)S(1)} %force.1), custom_call_target="tpu_custom_call" | custom-call | flops 600000000 | bytes 8000000 | tf_op jit(solution)/shard_map/smooth/pallas_call | solution.py:664
  29.4 0.7 %collective-permute-done.11 = f32[8,8,128]{2,1,0:T(8,128)S(1)} collective-permute-done((f32[8,8,128]{2,1,0:T(8,128)S(1)}, f32[8,8,128]{2,1,0:T(8,128)S(1)}, u32[]{:S(2)}, u32[]{:S(2)}) %collective-permute-start.11) | collective-permute-done | bytes 32800 | tf_op jit(solution)/shard_map/ppermute | solution.py:31
  30.0 0.6 %fusion.1 = f32[8,8,128]{2,1,0:T(8,128)} fusion(f32[8,8,128]{2,1,0:T(8,128)S(1)} %collective-permute-done.11, f32[1,2,8,8,128]{4,3,2,1,0:T(8,128)S(1)} %bitcast.27), kind=kLoop, calls=%fused_computation.4 | loop fusion | flops 16384 | bytes 98304 | tf_op jit(solution)/shard_map/mul | solution.py:665
  (27 shorter events, 0.2 us)
Async XLA Ops:
  0.6 15.5 %copy-start = (s32[1,3,64,8,128]{4,3,2,1,0:T(8,128)S(1)}, s32[1,3,64,8,128]{4,3,2,1,0:T(8,128)}, u32[]{:S(2)}) copy-start(s32[1,3,64,8,128]{4,3,2,1,0:T(8,128)} %param.6) | copy-start | bytes 2359300
  0.6 15.4 %copy-start.1 = (bf16[1,3,64,8,128]{4,3,2,1,0:T(8,128)(2,1)S(1)}, bf16[1,3,64,8,128]{4,3,2,1,0:T(8,128)(2,1)}, u32[]{:S(2)}) copy-start(bf16[1,3,64,8,128]{4,3,2,1,0:T(8,128)(2,1)} %param.7) | copy-start | bytes 1179652
  0.7 15.4 %copy-start.2 = (bf16[1,64,8,128]{3,2,1,0:T(8,128)(2,1)S(1)}, bf16[1,64,8,128]{3,2,1,0:T(8,128)(2,1)}, u32[]{:S(2)}) copy-start(bf16[1,64,8,128]{3,2,1,0:T(8,128)(2,1)} %param.5) | copy-start | bytes 393220
  0.7 6.6 %collective-permute-start = (bf16[8,8,128]{2,1,0:T(8,128)(2,1)}, bf16[8,8,128]{2,1,0:T(8,128)(2,1)S(1)}, u32[]{:S(2)}, u32[]{:S(2)}) collective-permute-start(bf16[8,8,128]{2,1,0:T(8,128)(2,1)} %template.1), channel_id=1, source_target_pairs={{0,4},{1,5},{2,6},{3,7},{4,0},{5,1},{6,2},{7,3},{8,12},{9,13},{10,... | collective-permute-start | bytes 49160 | tf_op jit(solution)/shard_map/ppermute | solution.py:31
  4.8 0.8 %copy-start.3 = (bf16[8,8,128]{2,1,0:T(8,128)(2,1)S(1)}, bf16[8,8,128]{2,1,0:T(8,128)(2,1)}, u32[]{:S(2)}) copy-start(bf16[8,8,128]{2,1,0:T(8,128)(2,1)} %template.1) | copy-start | bytes 49156
  7.3 5.2 %collective-permute-start.1 = (bf16[16,8,128]{2,1,0:T(8,128)(2,1)S(1)}, bf16[16,8,128]{2,1,0:T(8,128)(2,1)S(1)}, u32[]{:S(2)}, u32[]{:S(2)}) collective-permute-start(bf16[16,8,128]{2,1,0:T(8,128)(2,1)S(1)} %pad_maximum_fusion), channel_id=1, source_target_pairs={{0,3},{1,2},{2,1},{3,0},{4,7},{5,6},{6,5},{7,4},{8,11},{9,10},{10,... | collective-permute-start | bytes 98312 | tf_op jit(solution)/shard_map/ppermute | solution.py:31
  9.9 3.9 %collective-permute-start.2 = (bf16[16,8,128]{2,1,0:T(8,128)(2,1)S(1)}, bf16[16,8,128]{2,1,0:T(8,128)(2,1)S(1)}, u32[]{:S(2)}, u32[]{:S(2)}) collective-permute-start(bf16[16,8,128]{2,1,0:T(8,128)(2,1)S(1)} %pad_maximum_fusion), channel_id=1, source_target_pairs={{0,1},{1,0},{2,3},{3,2},{4,5},{5,4},{6,7},{7,6},{8,9},{9,8},{10,11... | collective-permute-start | bytes 98312 | tf_op jit(solution)/shard_map/ppermute | solution.py:31
  10.4 3.9 %collective-permute-start.3 = (bf16[16,8,128]{2,1,0:T(8,128)(2,1)S(1)}, bf16[16,8,128]{2,1,0:T(8,128)(2,1)S(1)}, u32[]{:S(2)}, u32[]{:S(2)}) collective-permute-start(bf16[16,8,128]{2,1,0:T(8,128)(2,1)S(1)} %pad_maximum_fusion), channel_id=1, source_target_pairs={{0,2},{1,3},{2,0},{3,1},{4,6},{5,7},{6,4},{7,5},{8,10},{9,11},{10,... | collective-permute-start | bytes 98312 | tf_op jit(solution)/shard_map/ppermute | solution.py:31
  10.9 11.1 %collective-permute-start.9 = (bf16[7,8,8,128]{3,2,1,0:T(8,128)(2,1)}, bf16[7,8,8,128]{3,2,1,0:T(8,128)(2,1)S(1)}, u32[]{:S(2)}, u32[]{:S(2)}) collective-permute-start(bf16[7,8,8,128]{3,2,1,0:T(8,128)(2,1)} %get-tuple-element.35), channel_id=1, source_target_pairs={{0,8},{8,0},{16,24},{24,16},{1,9},{9,1},{17,25},{25,17},{2,10},{10... | collective-permute-start | bytes 344072 | tf_op jit(solution)/shard_map/ppermute | solution.py:37
  10.9 11.1 %collective-permute-start.10 = (bf16[7,8,8,128]{3,2,1,0:T(8,128)(2,1)}, bf16[7,8,8,128]{3,2,1,0:T(8,128)(2,1)S(1)}, u32[]{:S(2)}, u32[]{:S(2)}) collective-permute-start(bf16[7,8,8,128]{3,2,1,0:T(8,128)(2,1)} %get-tuple-element.36), channel_id=1, source_target_pairs={{0,24},{8,16},{16,8},{24,0},{1,25},{9,17},{17,9},{25,1},{2,26},{10... | collective-permute-start | bytes 344072 | tf_op jit(solution)/shard_map/ppermute | solution.py:43
  14.4 3.5 %collective-permute-start.4 = (bf16[11,8,128]{2,1,0:T(8,128)(2,1)S(1)}, bf16[11,8,128]{2,1,0:T(8,128)(2,1)S(1)}, u32[]{:S(2)}, u32[]{:S(2)}) collective-permute-start(bf16[11,8,128]{2,1,0:T(8,128)(2,1)S(1)} %broadcast_select_fusion.1), channel_id=1, source_target_pairs={{0,8},{8,0},{16,24},{24,16},{1,9},{9,1},{17,25},{25,17},{2,10},{10... | collective-permute-start | bytes 67592 | tf_op jit(solution)/shard_map/ppermute | solution.py:37
  14.5 3.4 %collective-permute-start.5 = (bf16[11,8,128]{2,1,0:T(8,128)(2,1)S(1)}, bf16[11,8,128]{2,1,0:T(8,128)(2,1)S(1)}, u32[]{:S(2)}, u32[]{:S(2)}) collective-permute-start(bf16[11,8,128]{2,1,0:T(8,128)(2,1)S(1)} %get-tuple-element.54), channel_id=1, source_target_pairs={{0,24},{8,16},{16,8},{24,0},{1,25},{9,17},{17,9},{25,1},{2,26},{10... | collective-permute-start | bytes 67592 | tf_op jit(solution)/shard_map/ppermute | solution.py:43
  18.4 6.5 %collective-permute-start.6 = (f32[16,8,128]{2,1,0:T(8,128)S(1)}, f32[16,8,128]{2,1,0:T(8,128)S(1)}, u32[]{:S(2)}, u32[]{:S(2)}) collective-permute-start(f32[16,8,128]{2,1,0:T(8,128)S(1)} %get-tuple-element.32), channel_id=1, source_target_pairs={{0,3},{1,2},{2,1},{3,0},{4,7},{5,6},{6,5},{7,4},{8,11},{9,10},{10,... | collective-permute-start | bytes 196616 | tf_op jit(solution)/shard_map/ppermute | solution.py:31
  19.9 5.2 %collective-permute-start.7 = (f32[16,8,128]{2,1,0:T(8,128)S(1)}, f32[16,8,128]{2,1,0:T(8,128)S(1)}, u32[]{:S(2)}, u32[]{:S(2)}) collective-permute-start(f32[16,8,128]{2,1,0:T(8,128)S(1)} %get-tuple-element.33), channel_id=1, source_target_pairs={{0,1},{1,0},{2,3},{3,2},{4,5},{5,4},{6,7},{7,6},{8,9},{9,8},{10,11... | collective-permute-start | bytes 196616 | tf_op jit(solution)/shard_map/ppermute | solution.py:31
  20.4 4.7 %collective-permute-start.8 = (f32[16,8,128]{2,1,0:T(8,128)S(1)}, f32[16,8,128]{2,1,0:T(8,128)S(1)}, u32[]{:S(2)}, u32[]{:S(2)}) collective-permute-start(f32[16,8,128]{2,1,0:T(8,128)S(1)} %get-tuple-element.34), channel_id=1, source_target_pairs={{0,2},{1,3},{2,0},{3,1},{4,6},{5,7},{6,4},{7,5},{8,10},{9,11},{10,... | collective-permute-start | bytes 196616 | tf_op jit(solution)/shard_map/ppermute | solution.py:31
  25.1 4.9 %collective-permute-start.11 = (f32[8,8,128]{2,1,0:T(8,128)S(1)}, f32[8,8,128]{2,1,0:T(8,128)S(1)}, u32[]{:S(2)}, u32[]{:S(2)}) collective-permute-start(f32[8,8,128]{2,1,0:T(8,128)S(1)} %slice_bitcast_fusion), channel_id=1, source_target_pairs={{0,4},{1,5},{2,6},{3,7},{4,0},{5,1},{6,2},{7,3},{8,12},{9,13},{10,... | collective-permute-start | bytes 98312 | tf_op jit(solution)/shard_map/ppermute | solution.py:31
